TPU v7x, 32 devices: a whole 2x2x4 slice. The times are simulated.
32 devices in a mesh: tm: 4 (over z), tensor: 8 (over y, x, core).
Axes of the slice: x: 2, y: 2, z: 4, core: 2. Of those that a mesh axis runs over, the one named last changes fastest.
Arguments:
- integrals: bfloat16 [1024, 2, 4096], P('tensor'), may hold values from -0.75 to 0.75
- pair_lists: int32 [16, 2], replicated, may hold values from 0 to 7, as said below
- occ_density: bfloat16 [4, 8, 64, 64], P('tm', 'tensor'), may hold values from -0.75 to 0.75
- virt_density: bfloat16 [4, 8, 64, 64], P('tm', 'tensor'), may hold values from -0.75 to 0.75
- cosine_weights: float32 [4, 4], replicated, may hold values from -3 to 3
- coulomb_blocks: float32 [16, 64, 64], replicated, may hold values from -0.75 to 0.75
Outputs:
- screened: float32 [4, 1024, 1024], P('tm', 'tensor')
Inputs may be any that keep to these rules, and one draw needn't show every extreme that they name: `pair_lists`: row p names the 2 pair blocks listed with aux block p, all different, in ascending order. Every pair block is named in 1 to 6 rows, and some pair block in exactly 6 rows.
All inputs are finite; a program needn't handle non-finite values.
Results may differ from a plain program's by a relative error of at most 0.01.
Values may be sent and summed in bfloat16 or wider, within the bound.
No kernel may reach another device: no remote copies, remote signals or barrier semaphores. Data moves between devices by JAX's collectives and lax.ppermute only.
A program may use at most 64 MiB of HBM per device.

v0:
```python
import jax
import jax.numpy as jnp
from jax import lax
from jax.sharding import PartitionSpec as P

MOST = 6


def listed_blocks(pair_lists, pair_index):
    block_count = pair_lists.shape[0]
    member = jnp.any(pair_lists == pair_index, axis=1)
    positions = jnp.cumsum(member.astype(jnp.int32)) - 1
    slot_ids = jnp.arange(MOST, dtype=jnp.int32)
    matches = member[None, :] & (positions[None, :] == slot_ids[:, None])
    labels = jnp.arange(block_count, dtype=jnp.int32)
    located = jnp.sum(jnp.where(matches, labels[None, :], 0), axis=1)
    return jnp.where(jnp.any(matches, axis=1), located, block_count)


def density_product(row_data, occupied, virtual):
    row_count = row_data.shape[0]
    orbital_width = occupied.shape[0]
    half_done = jnp.dot(
        row_data.reshape(row_count * orbital_width, orbital_width),
        virtual,
        preferred_element_type=jnp.float32,
    )
    half_done = half_done.astype(jnp.bfloat16).reshape(row_count, orbital_width, orbital_width)
    contracted = jnp.einsum("rms,ml->rls", half_done, occupied, preferred_element_type=jnp.float32)
    return contracted.astype(jnp.bfloat16).reshape(row_count, orbital_width * orbital_width)


def pack_rows(local_rows, first_row, pair_lists, pair_count, block_rows):
    row_count = local_rows.shape[0]
    row_ids = first_row + jnp.arange(row_count, dtype=jnp.int32)
    targets = pair_lists[row_ids // block_rows]
    places = jnp.broadcast_to(jnp.arange(row_count, dtype=jnp.int32)[:, None], targets.shape)
    zero_buffer = jnp.zeros((pair_count, row_count, local_rows.shape[2]), local_rows.dtype)
    filled = zero_buffer.at[targets, places].set(local_rows)
    return filled.reshape(pair_count * row_count, local_rows.shape[2])


def per_device(integrals, pair_lists, occ_density, virt_density, cosine_weights, coulomb_blocks):
    tensor_size = lax.axis_size("tensor")
    owner_pair = lax.axis_index("tensor")
    local_count = integrals.shape[0]
    slab_rows = local_count * tensor_size
    block_count = coulomb_blocks.shape[0]
    block_rows = coulomb_blocks.shape[1]
    occupied = occ_density[0, 0]
    virtual = virt_density[0, 0]
    chosen = listed_blocks(pair_lists, owner_pair)
    wanted = (
        chosen[:, None] * block_rows + jnp.arange(block_rows, dtype=jnp.int32)[None, :]
    ).reshape(-1)
    outgoing = pack_rows(integrals, owner_pair * local_count, pair_lists, tensor_size, block_rows)
    arrived = lax.all_to_all(outgoing, "tensor", split_axis=0, concat_axis=0, tiled=True)
    tile_rows = jnp.take(arrived, wanted, axis=0, mode="fill", fill_value=0)
    weighted = density_product(tile_rows, occupied, virtual)
    gram_block = lax.dot_general(
        weighted, tile_rows, (((1,), (1,)), ((), ())), preferred_element_type=jnp.float32
    )
    most_count = chosen.shape[0]
    block_ids = jnp.arange(block_count, dtype=jnp.int32)
    slot_ids = jnp.arange(most_count, dtype=jnp.int32)
    block_match = chosen[None, :] == block_ids[:, None]
    slot_of = jnp.sum(jnp.where(block_match, slot_ids[None, :], 0), axis=1)
    present = jnp.any(block_match, axis=1)
    slab_ids = jnp.arange(slab_rows, dtype=jnp.int32)
    row_block = slab_ids // block_rows
    source_row = jnp.where(
        present[row_block],
        slot_of[row_block] * block_rows + slab_ids % block_rows,
        most_count * block_rows,
    )
    rounded_terms = gram_block.astype(jnp.bfloat16)
    outgoing_terms = jnp.take(rounded_terms, source_row, axis=0, mode="fill", fill_value=0)
    arrived_terms = lax.all_to_all(
        outgoing_terms, "tensor", split_axis=0, concat_axis=0, tiled=True
    )
    received = arrived_terms.reshape(tensor_size, local_count, most_count, block_rows)
    every_chosen = jax.vmap(lambda pair_index: listed_blocks(pair_lists, pair_index))(
        jnp.arange(tensor_size, dtype=jnp.int32)
    )
    placement = (every_chosen[:, :, None] == block_ids[None, None, :]).astype(jnp.bfloat16)
    placed = jnp.einsum("srja,sjp->rpa", received, placement, preferred_element_type=jnp.float32)
    chi_rows = placed.reshape(local_count, slab_rows)
    spread = jnp.einsum(
        "ft,trc->frc",
        cosine_weights,
        lax.all_to_all(
            chi_rows[None].astype(jnp.bfloat16), "tm", split_axis=2, concat_axis=0, tiled=True
        ).astype(jnp.float32),
        precision=lax.Precision.HIGHEST,
    )
    freq_rows = lax.all_to_all(
        spread.astype(jnp.bfloat16), "tm", split_axis=0, concat_axis=2, tiled=True
    ).astype(spread.dtype)
    shaped = freq_rows.reshape(1, local_count, block_count, block_rows)
    screened = jnp.einsum("frpa,pab->frpb", shaped, coulomb_blocks, precision=lax.Precision.HIGHEST)
    return screened.reshape(1, local_count, slab_rows)


def solution(mesh):
    in_specs = (
        P("tensor", None, None),
        P(),
        P("tm", "tensor", None, None),
        P("tm", "tensor", None, None),
        P(),
        P(),
    )
    out_specs = P("tm", "tensor", None)
    return jax.shard_map(
        per_device, mesh=mesh, in_specs=in_specs, out_specs=out_specs, check_vma=False
    )
```

profile of v0, /device:TPU:0, one launch (start us, length us, event | category | flops | bytes accessed | tf_op | source)
XLA Modules:
  0.0 278.4 jit_solution(11747451895038781436)
XLA Ops:
  0.0 0.8 copy.44
  0.8 0.6 gather_fusion
  1.7 2.7 reshape.432
  4.4 4.3 %broadcast_in_dim.112 = bf16[8,128,4096]{2,1,0:T(8,128)(2,1)} broadcast(bf16[]{:T(256)} %constant.105.clone.1), dimensions={} | broadcast | bytes 8388610 | tf_op jit(solution)/shard_map/broadcast_in_dim | solution.py:38
  8.7 65.4 %scatter_fusion = bf16[8,128,4096]{2,1,0:T(8,128)(2,1)} fusion(bf16[8,128,4096]{2,1,0:T(8,128)(2,1)} %broadcast_in_dim.112, s32[256]{0:T(256)S(1)} %reshape.430, bf16[256,4096]{1,0:T(8,128)(2,1)S(1)} %reshape.432), kind=kCustom, calls=%fused_computation.3 | custom fusion | bytes 6293504 | tf_op jit(solution)/shard_map/scatter | solution.py:39
  74.1 8.8 %all-to-all-start = ((bf16[8,128,4096]{2,1,0:T(8,128)(2,1)}), bf16[8,128,4096]{2,1,0:T(8,128)(2,1)}, u32[]{:S(2)}, u32[]{:S(2)}) async-start(bf16[8,128,4096]{2,1,0:T(8,128)(2,1)} %scatter_fusion), calls=%async_computation | async-start | bytes 16777216 | tf_op jit(solution)/shard_map/all_to_all | solution.py:57
  84.1 0.7 fusion.30
  84.8 4.4 %select_reduce_fusion.1 = pred[1024]{0:T(1024)(128)(4,1)S(1)} fusion(pred[]{:T(512)} %bitcast.11, pred[]{:T(512)} %bitcast.12, pred[]{:T(512)} %bitcast.13, pred[]{:T(512)} %bitcast.14, pred[]{:T(512)} %bitcast.15, pred[]{:T(512)} %bitcast.17, pred[]{:T(512)} %bitcast.16), kind=kLoop, calls=%fused_computation.35 | loop fusion | flops 23552 | bytes 1031 | tf_op jit(solution)/shard_map/gather | solution.py:72
  89.3 0.7 fusion.29
  90.0 4.3 %compare_select_fusion.5 = s32[1024,1]{0,1:T(1,128)S(1)} fusion(s32[]{:T(128)} %bitcast.28, s32[]{:T(128)} %bitcast.29, s32[]{:T(128)} %bitcast.30, s32[]{:T(128)} %bitcast.31, s32[]{:T(128)} %bitcast.32, s32[]{:T(128)} %bitcast.34, s32[]{:T(128)} %bitcast.33), kind=kLoop, calls=%fused_computation.51 | loop fusion | flops 23552 | bytes 4124 | tf_op jit(solution)/shard_map/gather | solution.py:73
  94.4 11.2 %compare_and_fusion = (pred[8,128]{1,0:T(8,128)(4,1)S(1)}, pred[1024]{0:T(1024)(128)(4,1)S(1)}, s32[1024]{0:T(1024)S(1)}) fusion(pred[1024]{0:T(1024)(128)(4,1)S(1)} %compare_reduce_fusion, pred[1024]{0:T(1024)(128)(4,1)S(1)} %compare_reduce_fusion.1, pred[1024]{0:T(1024)(128)(4,1)S(1)} %compare_reduce_fusion.2, ...), kind=kLoop, calls=%fused_computation.84 | loop fusion | flops 35840 | bytes 20525 | tf_op jit(solution)/shard_map/jit(_take)/and | solution.py:77
  105.6 71.5 %all-to-all-done = bf16[8,128,4096]{2,1,0:T(8,128)(2,1)} async-done(((bf16[8,128,4096]{2,1,0:T(8,128)(2,1)}), bf16[8,128,4096]{2,1,0:T(8,128)(2,1)}, u32[]{:S(2)}, u32[]{:S(2)}) %all-to-all-start) | async-done | bytes 8388640 | tf_op jit(solution)/shard_map/all_to_all | solution.py:57
  177.1 12.7 %gather_fusion.1 = bf16[384,4096]{1,0:T(8,128)(2,1)} fusion(bf16[1024,4096]{1,0:T(8,128)(2,1)} %bitcast.39, s32[1024]{0:T(1024)S(1)} %pad_clamp_fusion), kind=kCustom, calls=%fused_computation.1 | custom fusion | bytes 6292992 | tf_op jit(solution)/shard_map/jit(_take)/gather | solution.py:58
  189.8 3.8 %broadcast_select_fusion = bf16[384,4096]{1,0:T(8,128)(2,1)} fusion(bf16[384,4096]{1,0:T(8,128)(2,1)} %gather_fusion.1, pred[384]{0:T(512)(128)(4,1)S(1)} %compare_and_fusion.1), kind=kLoop, calls=%fused_computation.6 | loop fusion | flops 1572864 | bytes 6291840 | tf_op jit(solution)/shard_map/jit(_take)/select_n | solution.py:58
  193.6 9.7 %select_n.195 = bf16[24576,64]{1,0:T(8,128)(2,1)} reshape(bf16[384,4096]{1,0:T(8,128)(2,1)} %broadcast_select_fusion) | data formatting | bytes 6291456 | tf_op jit(solution)/shard_map/jit(_take)/select_n | solution.py:58
  203.3 6.8 %convolution_convert_fusion = bf16[24576,64]{0,1:T(8,128)(2,1)} fusion(bf16[24576,64]{1,0:T(8,128)(2,1)} %select_n.195, bf16[1,1,64,64]{3,2,1,0:T(8,128)(2,1)S(1)} %copy-done.2), kind=kOutput, calls=%fused_computation.4 | convolution fusion | flops 202899456 | bytes 6299648 | tf_op jit(solution)/shard_map/dot_general | solution.py:23
  210.1 9.7 %reshape.354 = bf16[384,64,64]{1,0,2:T(8,128)(2,1)} reshape(bf16[24576,64]{0,1:T(8,128)(2,1)} %convolution_convert_fusion) | data formatting | bytes 6291456 | tf_op jit(solution)/shard_map/reshape | solution.py:28
  219.8 5.1 %convert_bitcast_fusion = bf16[384,64,64]{0,1,2:T(8,128)(2,1)S(1)} fusion(bf16[384,64,64]{1,0,2:T(8,128)(2,1)} %reshape.354, bf16[1,1,64,64]{3,2,1,0:T(8,128)(2,1)S(1)} %copy-done.3), kind=kOutput, calls=%fused_computation.5 | convolution fusion | flops 202899456 | bytes 6299648 | tf_op jit(solution)/shard_map/rms,ml->rls/dot_general | solution.py:29
  225.0 1.9 copy.47
  226.9 1.8 convolution_convert_fusion.1
  228.7 3.9 %gather_fusion.2 = bf16[1024,384]{1,0:T(8,128)(2,1)S(1)} fusion(bf16[384,384]{1,0:T(8,128)(2,1)S(1)} %convolution_convert_fusion.1, s32[1024]{0:T(1024)S(1)} %broadcast_clamp_fusion), kind=kCustom, calls=%fused_computation.2 | custom fusion | bytes 1576960 | tf_op jit(solution)/shard_map/jit(_take)/gather | solution.py:77
  233.0 0.9 broadcast_select_fusion.1
  233.9 3.5 %all-to-all-start.1 = ((bf16[8,128,384]{1,2,0:T(8,128)(2,1)}), bf16[8,128,384]{1,2,0:T(8,128)(2,1)S(1)}, u32[]{:S(2)}, u32[]{:S(2)}) async-start(bf16[8,128,384]{1,2,0:T(8,128)(2,1)} %broadcast_select_fusion.1), calls=%async_computation.1 | async-start | bytes 1572864 | tf_op jit(solution)/shard_map/all_to_all | solution.py:78
  238.1 12.0 %all-to-all-done.1 = bf16[8,128,384]{1,2,0:T(8,128)(2,1)S(1)} async-done(((bf16[8,128,384]{1,2,0:T(8,128)(2,1)}), bf16[8,128,384]{1,2,0:T(8,128)(2,1)S(1)}, u32[]{:S(2)}, u32[]{:S(2)}) %all-to-all-start.1) | async-done | bytes 786464 | tf_op jit(solution)/shard_map/all_to_all | solution.py:78
  250.0 0.6 fusion.2
  251.1 0.5 broadcast.669
  251.6 2.2 reduce.24
  253.9 11.8 %all_to_all.48 = bf16[4,2,16384]{2,1,0:T(2,128)(2,1)S(1)} all-to-all(bf16[4,2,16384]{2,1,0:T(2,128)(2,1)S(1)} %reshape.511), channel_id=1, replica_groups=mesh['tm'=4,'tensor'=8] {'tm'}, dimensions={0} | all-to-all | bytes 524288 | tf_op jit(solution)/shard_map/all_to_all | solution.py:91
  266.2 0.6 fusion.1
  266.8 9.8 %all_to_all.49 = bf16[4,128,256]{2,1,0:T(8,128)(2,1)S(1)} all-to-all(bf16[4,128,256]{2,1,0:T(8,128)(2,1)S(1)} %copy.53), channel_id=1, replica_groups=mesh['tm'=4,'tensor'=8] {'tm'}, dimensions={0} | all-to-all | bytes 524288 | tf_op jit(solution)/shard_map/all_to_all | solution.py:96
  276.8 0.6 fusion.31
  277.4 1.0 copy.56
  (59 shorter events, 3.7 us)
Async XLA Ops:
  0.0 276.8 %copy-start = (f32[16,64,64]{2,1,0:T(8,128)S(1)}, f32[16,64,64]{2,1,0:T(8,128)}, u32[]{:S(2)}) copy-start(f32[16,64,64]{2,1,0:T(8,128)} %param.11) | copy-start | bytes 786436
  74.1 8.8 %copy-start.4 = (s32[16,2]{0,1:T(2,128)S(1)}, s32[16,2]{0,1:T(2,128)}, u32[]{:S(2)}) copy-start(s32[16,2]{0,1:T(2,128)} %param.7) | copy-start | bytes 388
  74.1 103.0 %all-to-all-start = ((bf16[8,128,4096]{2,1,0:T(8,128)(2,1)}), bf16[8,128,4096]{2,1,0:T(8,128)(2,1)}, u32[]{:S(2)}, u32[]{:S(2)}) async-start(bf16[8,128,4096]{2,1,0:T(8,128)(2,1)} %scatter_fusion), calls=%async_computation | async-start | bytes 16777216 | tf_op jit(solution)/shard_map/all_to_all | solution.py:57
  193.6 9.7 %copy-start.2 = (bf16[1,1,64,64]{3,2,1,0:T(8,128)(2,1)S(1)}, bf16[1,1,64,64]{3,2,1,0:T(8,128)(2,1)}, u32[]{:S(2)}) copy-start(bf16[1,1,64,64]{3,2,1,0:T(8,128)(2,1)} %param.9) | copy-start | bytes 24580
  210.1 9.7 %copy-start.3 = (bf16[1,1,64,64]{3,2,1,0:T(8,128)(2,1)S(1)}, bf16[1,1,64,64]{3,2,1,0:T(8,128)(2,1)}, u32[]{:S(2)}) copy-start(bf16[1,1,64,64]{3,2,1,0:T(8,128)(2,1)} %param.8) | copy-start | bytes 24580
  225.0 1.9 copy-start.1
  233.9 16.1 %all-to-all-start.1 = ((bf16[8,128,384]{1,2,0:T(8,128)(2,1)}), bf16[8,128,384]{1,2,0:T(8,128)(2,1)S(1)}, u32[]{:S(2)}, u32[]{:S(2)}) async-start(bf16[8,128,384]{1,2,0:T(8,128)(2,1)} %broadcast_select_fusion.1), calls=%async_computation.1 | async-start | bytes 1572864 | tf_op jit(solution)/shard_map/all_to_all | solution.py:78
  250.0 16.2 %copy-start.5 = (f32[4,4]{1,0:T(4,128)S(1)}, f32[4,4]{1,0:T(4,128)}, u32[]{:S(2)}) copy-start(f32[4,4]{1,0:T(4,128)} %param.10) | copy-start | bytes 196
where the time goes:
time: 282 us; the launch traced here: 278 us
  local copies, waits for them, and re-layouts  117 us (41%)
  waiting for transfers between devices  83.4 us (30%)
  other arithmetic  28.5 us (10%)
  blocking collectives  21.6 us (8%)
  matrix products  15.5 us (5%)
  starting transfers between devices  12.4 us (4%)
    all_to_all x1, waiting for transfers between devices, per_device(): lax.all_to_all(outgoing, 'tensor', split_axis=0, concat_axis=0, tiled=True)  71.5 us
    scatter x1, local copies, waits for them, and re-layouts, pack_rows(): filled = zero_buffer.at[targets, places].set(local_rows)  65.4 us
    gather x1, local copies, waits for them, and re-layouts, per_device(): tile_rows = jnp.take(arrived, wanted, axis=0, mode='fill', fill_value=0)  12.7 us
    all_to_all x1, waiting for transfers between devices, per_device(): lax.all_to_all(outgoing_terms, 'tensor', split_axis=0, concat_axis=0, til...  12 us
    all_to_all x1, blocking collectives, per_device(): lax.all_to_all(chi_rows[None].astype(jnp.bfloat16), 'tm', split_axis=2, c...  11.8 us
    and x1, other arithmetic, per_device(): jnp.take(rounded_terms, source_row, axis=0, mode='fill', fill_value=0)  11.2 us
    all_to_all x1, blocking collectives, per_device(): lax.all_to_all(spread.astype(jnp.bfloat16), 'tm', split_axis=0, concat_ax...  9.8 us
    select_n x1, local copies, waits for them, and re-layouts, per_device(): tile_rows = jnp.take(arrived, wanted, axis=0, mode='fill', fill_value=0)  9.71 us
  transfers between devices with their start and end apart: 2, of which 2 were waited for; matrix products, arithmetic and copies ran while one was open for 8% of the time, Pallas kernels for 0%

commit v1 on v0

--- a/solution.py
+++ b/solution.py
@@ -1,9 +1,15 @@
+import functools
+
 import jax
 import jax.numpy as jnp
 from jax import lax
+from jax.experimental import pallas as pl
+from jax.experimental.pallas import tpu as pltpu
 from jax.sharding import PartitionSpec as P
 
 MOST = 6
+HALF = 64
+LANES = 128
 
 
 def listed_blocks(pair_lists, pair_index):
@@ -40,7 +46,7 @@
     return filled.reshape(pair_count * row_count, local_rows.shape[2])
 
 
-def per_device(integrals, pair_lists, occ_density, virt_density, cosine_weights, coulomb_blocks):
+def any_slice(integrals, pair_lists, occ_density, virt_density, cosine_weights, coulomb_blocks):
     tensor_size = lax.axis_size("tensor")
     owner_pair = lax.axis_index("tensor")
     local_count = integrals.shape[0]
@@ -101,6 +107,248 @@
     return screened.reshape(1, local_count, slab_rows)
 
 
+def swap_groups(rows_ref, out_ref):
+    count = rows_ref.shape[0] // HALF
+    left = lax.broadcasted_iota(jnp.int32, (count, LANES), 1) < HALF
+    for pair in range(HALF // 2):
+        even = rows_ref[pl.ds(2 * pair, count, stride=HALF), :]
+        odd = rows_ref[pl.ds(2 * pair + 1, count, stride=HALF), :]
+        first = jnp.where(left, even, pltpu.roll(odd, HALF, 1))
+        second = jnp.where(left, pltpu.roll(even, HALF, 1), odd)
+        out_ref[0, 0, :count, pair * LANES : (pair + 1) * LANES] = first.astype(out_ref.dtype)
+        out_ref[0, 0, count:, pair * LANES : (pair + 1) * LANES] = second.astype(out_ref.dtype)
+
+
+def turn_kernel(tile_ref, out_ref, rows_ref):
+    count = rows_ref.shape[0] // HALF
+    for piece in range(count):
+        chunk = tile_ref[0, 0, :, piece * LANES : (piece + 1) * LANES]
+        rows_ref[piece * HALF : (piece + 1) * HALF, :] = chunk.astype(jnp.float32)
+    left = lax.broadcasted_iota(jnp.int32, (count, LANES), 1) < HALF
+    for low in range(HALF // 2):
+        near = rows_ref[pl.ds(low, count, stride=HALF), :]
+        far = rows_ref[pl.ds(low + HALF // 2, count, stride=HALF), :]
+        first = jnp.where(left, near, pltpu.roll(far, HALF, 1))
+        second = jnp.where(left, pltpu.roll(near, HALF, 1), far)
+        out_ref[0, 0, :count, low * LANES : (low + 1) * LANES] = first.astype(out_ref.dtype)
+        out_ref[0, 0, count:, low * LANES : (low + 1) * LANES] = second.astype(out_ref.dtype)
+
+
+def mix_kernel(turned_ref, density_ref, out_ref, rows_ref):
+    occupied = density_ref[0, 0, :, :HALF]
+    virtual = density_ref[0, 0, :, HALF:].astype(jnp.float32)
+    wide = 4 * HALF
+    row_ids = lax.broadcasted_iota(jnp.int32, (wide, wide), 0) // HALF
+    col_ids = lax.broadcasted_iota(jnp.int32, (wide, wide), 1) // HALF
+    twice = jnp.concatenate([virtual, virtual], axis=1)
+    strip = jnp.concatenate([twice, twice], axis=1)
+    tiled = jnp.concatenate([strip, strip, strip, strip], axis=0)
+    diagonal = jnp.where(row_ids == col_ids, tiled, 0.0).astype(jnp.bfloat16)
+    groups = turned_ref.shape[3] // wide
+    halves = []
+    for group in range(groups):
+        half_done = jnp.dot(
+            occupied,
+            turned_ref[0, 0, :, group * wide : (group + 1) * wide],
+            preferred_element_type=jnp.float32,
+        )
+        halves.append(half_done.astype(jnp.bfloat16))
+    mixed = jnp.dot(
+        jnp.concatenate(halves, axis=0), diagonal, preferred_element_type=jnp.float32
+    )
+    for group in range(groups):
+        block = mixed[group * HALF : (group + 1) * HALF]
+        rows_ref[2 * group * HALF : (2 * group + 1) * HALF, :] = block[:, :LANES]
+        rows_ref[(2 * group + 1) * HALF : (2 * group + 2) * HALF, :] = block[:, LANES:]
+    swap_groups(rows_ref, out_ref)
+
+
+def gram_kernel(weights_ref, match_ref, *refs):
+    mixed_refs, piece_refs = refs[:4], refs[4:12]
+    out_ref, sum_ref = refs[12], refs[13]
+    step = pl.program_id(0)
+    caps = sum_ref.shape[0]
+
+    @pl.when(step == 0)
+    def _():
+        sum_ref[...] = jnp.zeros_like(sum_ref)
+
+    depth = mixed_refs[0].shape[-1]
+    for column in range(caps):
+        right = jnp.concatenate([piece[column] for piece in piece_refs], axis=0)
+        for time in range(4):
+            left = mixed_refs[time][...].reshape(-1, depth)
+            sum_ref[column, time] += lax.dot_general(
+                left, right, (((1,), (1,)), ((), ())), preferred_element_type=jnp.float32
+            )
+
+    @pl.when(step == pl.num_programs(0) - 1)
+    def _():
+        rows = out_ref.shape[1]
+        for part in range(rows // HALF):
+            chi = []
+            for time in range(4):
+                total = None
+                for mine in range(caps):
+                    place = mine * rows + part * HALF
+                    for column in range(caps):
+                        row = (mine * 2 + part) * caps + column
+                        term = sum_ref[column, time, place : place + HALF, :] * match_ref[row : row + 1, :]
+                        total = term if total is None else total + term
+                chi.append(total)
+            for freq in range(4):
+                value = weights_ref[freq, 0] * chi[0]
+                for time in range(1, 4):
+                    value = value + weights_ref[freq, time] * chi[time]
+                out_ref[freq, part * HALF : (part + 1) * HALF, :] = value.astype(out_ref.dtype)
+
+
+def screen_kernel(place_ref, r0, r1, r2, r3, high_ref, low_ref, out_ref):
+    plane, device = place_ref[0], place_ref[1]
+    share = r0.shape[1] // 8
+    for move in range(8):
+        owner = device ^ move
+        total = None
+        for slot, ref in enumerate((r0, r1, r2, r3)):
+            first = pl.multiple_of((plane ^ slot) * share, share)
+            left = ref[:, move * share : (move + 1) * share]
+            for factor in (high_ref, low_ref):
+                term = jnp.dot(
+                    left, factor[owner, pl.ds(first, share), :], preferred_element_type=jnp.float32
+                )
+                total = term if total is None else total + term
+        out_ref[0, :, pl.ds(pl.multiple_of(owner * LANES, LANES), LANES)] = total
+
+
+def small_slice(integrals, pair_lists, occ_density, virt_density, cosine_weights, coulomb_blocks):
+    plane = lax.axis_index("tm")
+    device = lax.axis_index("tensor")
+    local_count, caps, pair_width = integrals.shape
+    share = local_count // 4
+    vmem = pl.BlockSpec(memory_space=pltpu.VMEM)
+    smem = pl.BlockSpec(memory_space=pltpu.SMEM)
+    params = pltpu.CompilerParams(vmem_limit_bytes=48 * 1024 * 1024)
+
+    def across(array, move):
+        return lax.ppermute(array, "tensor", [(i, i ^ move) for i in range(8)])
+
+    def planes(array, move):
+        return lax.ppermute(array, "tm", [(i, i ^ move) for i in range(4)])
+
+    occupied = occ_density[0, 0].T.reshape(HALF, HALF // 2, 2).swapaxes(1, 2).reshape(HALF, HALF)
+    density = jnp.concatenate([occupied, virt_density[0, 0]], axis=1)
+    own = lax.dynamic_slice_in_dim(integrals, plane * share, share, 0).transpose(1, 0, 2)
+
+    densities = [density] + [across(density, move) for move in range(1, 8)]
+
+    x_zero = across(own[0], 2)
+    y_one = across(own[1], 4)
+    x_one = across(own[1], 2)
+    y_zero = across(own[0], 4)
+    d_zero = across(x_zero, 4)
+    d_one = across(y_one, 2)
+    pieces = {
+        0: own,
+        2: jnp.stack([x_zero, x_one]),
+        4: jnp.stack([y_zero, y_one]),
+        6: jnp.stack([d_zero, d_one]),
+    }
+    for move in (0, 2, 4, 6):
+        pieces[move + 1] = across(pieces[move], 1)
+    pieces = [pieces[move] for move in range(8)]
+
+    lists = pair_lists.reshape(8, 2, caps)
+    mine = lax.dynamic_index_in_dim(lists, device, 0, keepdims=False).T.reshape(-1)
+    moves = mine ^ device
+    stacked = jnp.stack(densities)
+    picked = jnp.zeros((mine.shape[0],) + density.shape, density.dtype)
+    for move in range(8):
+        picked = jnp.where((moves == move)[:, None, None], stacked[move][None], picked)
+    picked = picked.reshape(caps, 2, HALF, LANES)
+    per_time = [picked] + [planes(picked, move) for move in range(1, 4)]
+
+    tiles = integrals.transpose(1, 0, 2).reshape(caps, 2, HALF, pair_width)
+    tile_spec = pl.BlockSpec((1, 1, HALF, pair_width), lambda a, b: (a, b, 0, 0))
+    rows_scratch = pltpu.VMEM((HALF * HALF // 2, LANES), jnp.float32)
+    turned = pl.pallas_call(
+        turn_kernel,
+        grid=(caps, 2),
+        out_shape=jax.ShapeDtypeStruct(tiles.shape, tiles.dtype),
+        in_specs=[tile_spec],
+        out_specs=tile_spec,
+        scratch_shapes=[rows_scratch],
+        compiler_params=params,
+    )(tiles)
+    mixed = [
+        pl.pallas_call(
+            mix_kernel,
+            grid=(caps, 2),
+            out_shape=jax.ShapeDtypeStruct(tiles.shape, tiles.dtype),
+            in_specs=[tile_spec, pl.BlockSpec((1, 1, HALF, LANES), lambda a, b: (a, b, 0, 0))],
+            out_specs=tile_spec,
+            scratch_shapes=[rows_scratch],
+            compiler_params=params,
+        )(turned, chosen)
+        for chosen in per_time
+    ]
+
+    theirs = jnp.stack(
+        [
+            lax.dynamic_index_in_dim(lists, device ^ move, 0, keepdims=False) for move in range(8)
+        ]
+    )
+    theirs = lax.dynamic_index_in_dim(theirs, plane // 2, 1, keepdims=False)
+    match = (mine[:, None, None] == theirs.T[None]).astype(jnp.float32)
+    match = jnp.repeat(match.reshape(-1, 8), share, axis=1)
+    order = plane ^ jnp.arange(4, dtype=jnp.int32)
+    weights = cosine_weights[order][:, order]
+    depth = 1024
+    columns = 8 * share
+    chi = pl.pallas_call(
+        gram_kernel,
+        grid=(pair_width // depth,),
+        out_shape=jax.ShapeDtypeStruct((4, local_count, columns), jnp.bfloat16),
+        in_specs=[smem, pl.BlockSpec(match.shape, lambda k: (0, 0))]
+        + [pl.BlockSpec((caps, 2, HALF, depth), lambda k: (0, 0, 0, k))] * 4
+        + [pl.BlockSpec((caps, share, depth), lambda k: (0, 0, k))] * 8,
+        out_specs=pl.BlockSpec((4, local_count, columns), lambda k: (0, 0, 0)),
+        scratch_shapes=[pltpu.VMEM((caps, 4, caps * local_count, columns), jnp.float32)],
+        compiler_params=params,
+    )(weights, match, *mixed, *pieces)
+
+    received = [chi[0]] + [planes(chi[move], move) for move in range(1, 4)]
+    grouped = coulomb_blocks.reshape(8, 2, HALF, HALF)
+    empty = jnp.zeros((8, HALF, HALF), grouped.dtype)
+    factors = jnp.concatenate(
+        [
+            jnp.concatenate([grouped[:, 0], empty], axis=2),
+            jnp.concatenate([empty, grouped[:, 1]], axis=2),
+        ],
+        axis=1,
+    )
+    high = factors.astype(jnp.bfloat16)
+    low = (factors - high.astype(jnp.float32)).astype(jnp.bfloat16)
+    place = jnp.stack([plane, device]).astype(jnp.int32)
+    return pl.pallas_call(
+        screen_kernel,
+        out_shape=jax.ShapeDtypeStruct((1, local_count, 8 * LANES), jnp.float32),
+        in_specs=[smem] + [vmem] * 6,
+        out_specs=vmem,
+        compiler_params=params,
+    )(place, *received, high, low)
+
+
+def per_device(integrals, pair_lists, occ_density, virt_density, cosine_weights, coulomb_blocks):
+    planned = (
+        lax.axis_size("tm") == 4
+        and lax.axis_size("tensor") == 8
+        and integrals.shape == (2 * HALF, 2, HALF * HALF)
+        and coulomb_blocks.shape == (16, HALF, HALF)
+    )
+    step = small_slice if planned else any_slice
+    return step(integrals, pair_lists, occ_density, virt_density, cosine_weights, coulomb_blocks)
+
+
 def solution(mesh):
     in_specs = (
         P("tensor", None, None),

time: 282 us -> 105 us (0.37); the launches traced: 278 us -> 105 us
  local copies, waits for them, and re-layouts: 117 us -> 23.3 us
  waiting for transfers between devices: 83.4 us -> 18.3 us
  Pallas kernels: 0 us -> 32.1 us
  other arithmetic: 28.5 us -> 2.8 us
  blocking collectives: 21.6 us -> 0 us
  matrix products: 15.5 us -> 0 us
  starting transfers between devices: 12.4 us -> 27.6 us
    all_to_all x2 -> x0, waiting for transfers between devices: 83.4 us -> none  [the longest x1 71.5 us: per_device(): lax.all_to_all(outgoing, 'tensor', split_axis=0, concat_axis=0, tiled=True)]
    scatter x1 -> x0, local copies, waits for them, and re-layouts: 65.4 us -> none  [pack_rows(): filled = zero_buffer.at[targets, places].set(local_rows)]
    pallas_call x0 -> x7, Pallas kernels: none -> 32.1 us  [the longest x4 17.9 us: small_slice(): pl.pallas_call(mix_kernel, grid=(caps, 2), out_shape=jax.ShapeDtypeStruct...]
    ppermute x0 -> x23, starting transfers between devices: none -> 27.6 us  [the longest x17 16 us: across(): return lax.ppermute(array, 'tensor', [(i, i ^ move) for i in range(8)])]
    all_to_all x2 -> x0, blocking collectives: 21.6 us -> none  [the longest x1 11.8 us: per_device(): lax.all_to_all(chi_rows[None].astype(jnp.bfloat16), 'tm', split_axis=2, c...]
    ppermute x0 -> x23, waiting for transfers between devices: none -> 18.3 us  [the longest x17 11.3 us: across(): return lax.ppermute(array, 'tensor', [(i, i ^ move) for i in range(8)])]
    gather x6 -> x4, local copies, waits for them, and re-layouts: 19.1 us -> 1.31 us  [small_slice(): weights = cosine_weights[order][:, order]]
    dot_general x6 -> x0, matrix products: 15.5 us -> none  [the longest x1 6.84 us: density_product(): jnp.dot(row_data.reshape(row_count * orbital_width, orbital_width), virtu...]
  transfers between devices with their start and end apart: 2 -> 23, of which waited for: 2 -> 7; matrix products, arithmetic and copies ran while one was open for 8% -> 19% of each run, Pallas kernels for 0% -> 21%
where the time goes in v1:
time: 105 us
  Pallas kernels  32.1 us (31%)
  starting transfers between devices  27.6 us (26%)
  local copies, waits for them, and re-layouts  23.3 us (22%)
  waiting for transfers between devices  18.3 us (17%)
  other arithmetic  2.8 us (3%)
    pallas_call x4, Pallas kernels, small_slice(): pl.pallas_call(mix_kernel, grid=(caps, 2), out_shape=jax.ShapeDtypeStruct...  17.9 us
    ppermute x17, starting transfers between devices, across(): return lax.ppermute(array, 'tensor', [(i, i ^ move) for i in range(8)])  16 us
    ppermute x6, starting transfers between devices, planes(): return lax.ppermute(array, 'tm', [(i, i ^ move) for i in range(4)])  11.6 us
    ppermute x17, waiting for transfers between devices, across(): return lax.ppermute(array, 'tensor', [(i, i ^ move) for i in range(8)])  11.3 us
    pallas_call x1, Pallas kernels, small_slice(): pl.pallas_call(gram_kernel, grid=(pair_width // depth,), out_shape=jax.Sh...  7.67 us
    ppermute x6, waiting for transfers between devices, planes(): return lax.ppermute(array, 'tm', [(i, i ^ move) for i in range(4)])  6.96 us
    unnamed x40, local copies, waits for them, and re-layouts  5.31 us
    pallas_call x1, Pallas kernels, small_slice(): pl.pallas_call(turn_kernel, grid=(caps, 2), out_shape=jax.ShapeDtypeStruc...  4.41 us
  transfers between devices with their start and end apart: 23, of which 7 were waited for; matrix products, arithmetic and copies ran while one was open for 19% of the time, Pallas kernels for 21%

profile of v1, /device:TPU:0, one launch (start us, length us, event | category | flops | bytes accessed | tf_op | source)
XLA Modules:
  0.0 104.6 jit_solution(12169776210845087576)
XLA Ops:
  0.0 0.9 copy.88
  2.1 2.6 %collective-permute-start.5 = (bf16[64,128]{0,1:T(8,128)(2,1)S(1)}, bf16[64,128]{0,1:T(8,128)(2,1)S(1)}, u32[]{:S(2)}, u32[]{:S(2)}) collective-permute-start(bf16[64,128]{0,1:T(8,128)(2,1)S(1)} %pad_maximum_fusion.3), channel_id=1, source_target_pairs={{0,2},{1,3},{2,0},{3,1},{4,6},{5,7},{6,4},{7,5},{8,10},{9,11},{10,... | collective-permute-start | bytes 49160 | tf_op jit(solution)/shard_map/ppermute | solution.py:233
  4.8 1.8 %collective-permute-start.3 = (bf16[64,128]{0,1:T(8,128)(2,1)S(1)}, bf16[64,128]{0,1:T(8,128)(2,1)S(1)}, u32[]{:S(2)}, u32[]{:S(2)}) collective-permute-start(bf16[64,128]{0,1:T(8,128)(2,1)S(1)} %pad_maximum_fusion.3), channel_id=1, source_target_pairs={{0,4},{1,5},{2,6},{3,7},{4,0},{5,1},{6,2},{7,3},{8,12},{9,13},{10,... | collective-permute-start | bytes 49160 | tf_op jit(solution)/shard_map/ppermute | solution.py:233
  6.5 1.5 %constant_dynamic-slice_fusion = bf16[32,2,4096]{2,1,0:T(2,128)(2,1)S(1)} fusion(bf16[128,2,4096]{2,1,0:T(2,128)(2,1)} %param.6, s32[]{:T(128)S(6)} %select_n.101), kind=kLoop, calls=%fused_computation.24 | loop fusion | bytes 1048580 | tf_op jit(solution)/shard_map/dynamic_slice | solution.py:240
  8.3 1.6 %collective-permute-start.12 = (bf16[32,4096]{1,0:T(8,128)(2,1)S(1)}, bf16[32,4096]{1,0:T(8,128)(2,1)S(1)}, u32[]{:S(2)}, u32[]{:S(2)}) collective-permute-start(bf16[32,4096]{1,0:T(8,128)(2,1)S(1)} %get-tuple-element.10), channel_id=1, source_target_pairs={{0,2},{1,3},{2,0},{3,1},{4,6},{5,7},{6,4},{7,5},{8,10},{9,11},{10,... | collective-permute-start | bytes 786440 | tf_op jit(solution)/shard_map/ppermute | solution.py:233
  13.4 2.0 %collective-permute-start.1 = (bf16[64,128]{0,1:T(8,128)(2,1)S(1)}, bf16[64,128]{0,1:T(8,128)(2,1)S(1)}, u32[]{:S(2)}, u32[]{:S(2)}) collective-permute-start(bf16[64,128]{0,1:T(8,128)(2,1)S(1)} %pad_maximum_fusion.3), channel_id=1, source_target_pairs={{0,6},{1,7},{2,4},{3,5},{4,2},{5,3},{6,0},{7,1},{8,14},{9,15},{10,... | collective-permute-start | bytes 49160 | tf_op jit(solution)/shard_map/ppermute | solution.py:233
  23.1 1.7 %collective-permute-start.15 = (bf16[32,4096]{1,0:T(8,128)(2,1)S(1)}, bf16[32,4096]{1,0:T(8,128)(2,1)S(1)}, u32[]{:S(2)}, u32[]{:S(2)}) collective-permute-start(bf16[32,4096]{1,0:T(8,128)(2,1)S(1)} %get-tuple-element.10), channel_id=1, source_target_pairs={{0,4},{1,5},{2,6},{3,7},{4,0},{5,1},{6,2},{7,3},{8,12},{9,13},{10,... | collective-permute-start | bytes 786440 | tf_op jit(solution)/shard_map/ppermute | solution.py:233
  26.7 1.8 %collective-permute-start.17 = (bf16[32,4096]{1,0:T(8,128)(2,1)S(1)}, bf16[32,4096]{1,0:T(8,128)(2,1)S(1)}, u32[]{:S(2)}, u32[]{:S(2)}) collective-permute-start(bf16[32,4096]{1,0:T(8,128)(2,1)S(1)} %collective-permute-done.11), channel_id=1, source_target_pairs={{0,4},{1,5},{2,6},{3,7},{4,0},{5,1},{6,2},{7,3},{8,12},{9,13},{10,... | collective-permute-start | bytes 786440 | tf_op jit(solution)/shard_map/ppermute | solution.py:233
  28.5 3.7 %collective-permute-done.15 = bf16[32,4096]{1,0:T(8,128)(2,1)S(1)} collective-permute-done((bf16[32,4096]{1,0:T(8,128)(2,1)S(1)}, bf16[32,4096]{1,0:T(8,128)(2,1)S(1)}, u32[]{:S(2)}, u32[]{:S(2)}) %collective-permute-start.15) | collective-permute-done | bytes 262176 | tf_op jit(solution)/shard_map/ppermute | solution.py:233
  32.3 1.7 %collective-permute-start.18 = (bf16[32,4096]{1,0:T(8,128)(2,1)S(1)}, bf16[32,4096]{1,0:T(8,128)(2,1)S(1)}, u32[]{:S(2)}, u32[]{:S(2)}) collective-permute-start(bf16[32,4096]{1,0:T(8,128)(2,1)S(1)} %collective-permute-done.15), channel_id=1, source_target_pairs={{0,2},{1,3},{2,0},{3,1},{4,6},{5,7},{6,4},{7,5},{8,10},{9,11},{10,... | collective-permute-start | bytes 786440 | tf_op jit(solution)/shard_map/ppermute | solution.py:233
  34.0 4.0 %collective-permute-done.14 = bf16[32,4096]{1,0:T(8,128)(2,1)} collective-permute-done((bf16[32,4096]{1,0:T(8,128)(2,1)S(1)}, bf16[32,4096]{1,0:T(8,128)(2,1)}, u32[]{:S(2)}, u32[]{:S(2)}) %collective-permute-start.14) | collective-permute-done | bytes 262176 | tf_op jit(solution)/shard_map/ppermute | solution.py:233
  38.0 1.0 pad_maximum_fusion.1.refs_8_
  39.1 3.5 %collective-permute-done.17 = bf16[32,4096]{1,0:T(8,128)(2,1)S(1)} collective-permute-done((bf16[32,4096]{1,0:T(8,128)(2,1)S(1)}, bf16[32,4096]{1,0:T(8,128)(2,1)S(1)}, u32[]{:S(2)}, u32[]{:S(2)}) %collective-permute-start.17) | collective-permute-done | bytes 262176 | tf_op jit(solution)/shard_map/ppermute | solution.py:233
  42.9 1.8 %collective-permute-start.7 = (bf16[2,2,64,128]{3,2,1,0:T(8,128)(2,1)S(1)}, bf16[2,2,64,128]{3,2,1,0:T(8,128)(2,1)S(1)}, u32[]{:S(2)}, u32[]{:S(2)}) collective-permute-start(bf16[2,2,64,128]{3,2,1,0:T(8,128)(2,1)S(1)} %select_select_fusion.density_ref), channel_id=1, source_target_pairs={{0,8},{8,0},{16,24},{24,16},{1,9},{9,1},{17,25},{25,17},{2,10},{10... | collective-permute-start | bytes 196616 | tf_op jit(solution)/shard_map/ppermute | solution.py:236
  46.0 1.3 %broadcast_in_dim.104 = f32[8,8,32]{2,1,0:T(8,128)} broadcast(f32[8,8]{1,0:T(8,128)} %compare_convert_fusion), dimensions={0,1} | broadcast | bytes 8448 | tf_op jit(solution)/shard_map/broadcast_in_dim | solution.py:302
  48.2 2.9 %copy.85 = bf16[2,128,4096]{2,1,0:T(8,128)(2,1)S(1)} copy(bf16[2,128,4096]{2,0,1:T(2,128)(2,1)} %bitcast.66) | data formatting | bytes 4194304 | tf_op jit(solution)/shard_map/transpose | solution.py:270
  51.1 4.4 %shard_map.64.turned_ref = bf16[2,2,64,4096]{3,2,1,0:T(8,128)(2,1)S(1)} custom-call(bf16[2,2,64,4096]{3,2,1,0:T(8,128)(2,1)S(1)} %bitcast.61), custom_call_target="tpu_custom_call" | custom-call | tf_op jit(solution)/shard_map/pallas_call | solution.py:273
  55.5 2.7 %collective-permute-start.8 = (bf16[2,2,64,128]{3,2,1,0:T(8,128)(2,1)S(1)}, bf16[2,2,64,128]{3,2,1,0:T(8,128)(2,1)S(1)}, u32[]{:S(2)}, u32[]{:S(2)}) collective-permute-start(bf16[2,2,64,128]{3,2,1,0:T(8,128)(2,1)S(1)} %select_select_fusion.density_ref), channel_id=1, source_target_pairs={{0,16},{8,24},{16,0},{24,8},{1,17},{9,25},{17,1},{25,9},{2,18},{10... | collective-permute-start | bytes 196616 | tf_op jit(solution)/shard_map/ppermute | solution.py:236
  58.3 3.6 %collective-permute-done.8.density_ref = bf16[2,2,64,128]{3,2,1,0:T(8,128)(2,1)S(1)} collective-permute-done((bf16[2,2,64,128]{3,2,1,0:T(8,128)(2,1)S(1)}, bf16[2,2,64,128]{3,2,1,0:T(8,128)(2,1)S(1)}, u32[]{:S(2)}, u32[]{:S(2)}) %collective-permute-start.8) | collective-permute-done | bytes 65568 | tf_op jit(solution)/shard_map/ppermute | solution.py:236
  61.9 2.7 %collective-permute-start.9 = (bf16[2,2,64,128]{3,2,1,0:T(8,128)(2,1)S(1)}, bf16[2,2,64,128]{3,2,1,0:T(8,128)(2,1)S(1)}, u32[]{:S(2)}, u32[]{:S(2)}) collective-permute-start(bf16[2,2,64,128]{3,2,1,0:T(8,128)(2,1)S(1)} %select_select_fusion.density_ref), channel_id=1, source_target_pairs={{0,24},{8,16},{16,8},{24,0},{1,25},{9,17},{17,9},{25,1},{2,26},{10... | collective-permute-start | bytes 196616 | tf_op jit(solution)/shard_map/ppermute | solution.py:236
  64.8 4.5 %shard_map.65.refs_0_ = bf16[2,2,64,4096]{3,2,1,0:T(8,128)(2,1)S(1)} custom-call(bf16[2,2,64,4096]{3,2,1,0:T(8,128)(2,1)S(1)} %shard_map.64.turned_ref, bf16[2,2,64,128]{3,2,1,0:T(8,128)(2,1)S(1)} %select_select_fusion.density_ref), custom_call_target="tpu_custom_call" | custom-call | tf_op jit(solution)/shard_map/pallas_call | solution.py:283
  69.3 4.5 %shard_map.66.refs_1_ = bf16[2,2,64,4096]{3,2,1,0:T(8,128)(2,1)S(1)} custom-call(bf16[2,2,64,4096]{3,2,1,0:T(8,128)(2,1)S(1)} %shard_map.64.turned_ref, bf16[2,2,64,128]{3,2,1,0:T(8,128)(2,1)S(1)} %collective-permute-done.7.density_ref), custom_call_target="tpu_custom_call" | custom-call | tf_op jit(solution)/shard_map/pallas_call | solution.py:283
  73.8 1.3 %copy-done.2 = bf16[2,2,64,4096]{3,2,1,0:T(8,128)(2,1)} copy-done((bf16[2,2,64,4096]{3,2,1,0:T(8,128)(2,1)}, bf16[2,2,64,4096]{3,2,1,0:T(8,128)(2,1)S(1)}, u32[]{:S(2)}) %copy-start.2) | copy-done | bytes 2097176
  75.2 4.5 %shard_map.67.refs_2_ = bf16[2,2,64,4096]{3,2,1,0:T(8,128)(2,1)S(1)} custom-call(bf16[2,2,64,4096]{3,2,1,0:T(8,128)(2,1)S(1)} %shard_map.64.turned_ref, bf16[2,2,64,128]{3,2,1,0:T(8,128)(2,1)S(1)} %collective-permute-done.8.density_ref), custom_call_target="tpu_custom_call" | custom-call | tf_op jit(solution)/shard_map/pallas_call | solution.py:283
  79.6 1.4 %copy-done.3 = bf16[2,2,64,4096]{3,2,1,0:T(8,128)(2,1)} copy-done((bf16[2,2,64,4096]{3,2,1,0:T(8,128)(2,1)}, bf16[2,2,64,4096]{3,2,1,0:T(8,128)(2,1)S(1)}, u32[]{:S(2)}) %copy-start.3) | copy-done | bytes 2097176
  81.0 4.5 %shard_map.68.refs_3_ = bf16[2,2,64,4096]{3,2,1,0:T(8,128)(2,1)S(1)} custom-call(bf16[2,2,64,4096]{3,2,1,0:T(8,128)(2,1)S(1)} %shard_map.64.turned_ref, bf16[2,2,64,128]{3,2,1,0:T(8,128)(2,1)S(1)} %collective-permute-done.9.density_ref), custom_call_target="tpu_custom_call" | custom-call | tf_op jit(solution)/shard_map/pallas_call | solution.py:283
  85.5 1.4 %copy-done.4 = bf16[2,2,64,4096]{3,2,1,0:T(8,128)(2,1)} copy-done((bf16[2,2,64,4096]{3,2,1,0:T(8,128)(2,1)}, bf16[2,2,64,4096]{3,2,1,0:T(8,128)(2,1)S(1)}, u32[]{:S(2)}) %copy-start.4) | copy-done | bytes 2097176
  86.9 7.7 %shard_map.69 = bf16[4,128,256]{2,1,0:T(8,128)(2,1)S(1)} custom-call(f32[4,4]{1,0:T(4,128)S(1)} %bitcast.65, f32[8,256]{1,0:T(8,128)S(1)} %reshape.92.match_ref, bf16[2,2,64,4096]{3,2,1,0:T(8,128)(2,1)} %copy-done.1, bf16[2,2,64,4096]{3,2,1,0:T(8,128)(2,1)} %copy-done.2, bf16[2,2,64,4096]{3,2,1,0:T(8,128)(2,1)} %copy-done.3, ...), custom_call_target="tpu_custom_call" | custom-call | tf_op jit(solution)/shard_map/pallas_call | solution.py:307
  94.7 1.7 %collective-permute-start.21 = (bf16[128,256]{1,0:T(8,128)(2,1)S(1)}, bf16[128,256]{1,0:T(8,128)(2,1)S(1)}, u32[]{:S(2)}, u32[]{:S(2)}) collective-permute-start(bf16[128,256]{1,0:T(8,128)(2,1)S(1)} %get-tuple-element.12), channel_id=1, source_target_pairs={{0,16},{8,24},{16,0},{24,8},{1,17},{9,25},{17,1},{25,9},{2,18},{10... | collective-permute-start | bytes 196616 | tf_op jit(solution)/shard_map/ppermute | solution.py:236
  96.4 2.7 %collective-permute-start.22 = (bf16[128,256]{1,0:T(8,128)(2,1)S(1)}, bf16[128,256]{1,0:T(8,128)(2,1)S(1)}, u32[]{:S(2)}, u32[]{:S(2)}) collective-permute-start(bf16[128,256]{1,0:T(8,128)(2,1)S(1)} %get-tuple-element.11), channel_id=1, source_target_pairs={{0,24},{8,16},{16,8},{24,0},{1,25},{9,17},{17,9},{25,1},{2,26},{10... | collective-permute-start | bytes 196616 | tf_op jit(solution)/shard_map/ppermute | solution.py:236
  99.9 2.6 %collective-permute-done.22.r3 = bf16[128,256]{1,0:T(8,128)(2,1)S(1)} collective-permute-done((bf16[128,256]{1,0:T(8,128)(2,1)S(1)}, bf16[128,256]{1,0:T(8,128)(2,1)S(1)}, u32[]{:S(2)}, u32[]{:S(2)}) %collective-permute-start.22) | collective-permute-done | bytes 65568 | tf_op jit(solution)/shard_map/ppermute | solution.py:236
  102.5 2.1 %shard_map.70 = f32[1,128,1024]{2,1,0:T(8,128)} custom-call(s32[2]{0:T(128)S(1)} %pad_add_fusion.place_ref, bf16[128,256]{1,0:T(8,128)(2,1)S(1)} %get-tuple-element.14.r0, bf16[128,256]{1,0:T(8,128)(2,1)S(1)} %collective-permute-done.20.r1, bf16[128,256]{1,0:T(8,128)(2,1)S(1)} %collective-permute-done.21.r2, ...), custom_call_target="tpu_custom_call" | custom-call | tf_op jit(solution)/shard_map/pallas_call | solution.py:332
  (119 shorter events, 18.2 us)
Async XLA Ops:
  0.0 44.7 %copy-start = (f32[4,4]{1,0:T(4,128)S(1)}, f32[4,4]{1,0:T(4,128)}, u32[]{:S(2)}) copy-start(f32[4,4]{1,0:T(4,128)} %param.10) | copy-start | bytes 196
  1.6 11.1 %collective-permute-start.6 = (bf16[64,128]{0,1:T(8,128)(2,1)S(1)}, bf16[64,128]{0,1:T(8,128)(2,1)S(1)}, u32[]{:S(2)}, u32[]{:S(2)}) collective-permute-start(bf16[64,128]{0,1:T(8,128)(2,1)S(1)} %pad_maximum_fusion.3), channel_id=1, source_target_pairs={{0,1},{1,0},{2,3},{3,2},{4,5},{5,4},{6,7},{7,6},{8,9},{9,8},{10,11... | collective-permute-start | bytes 49160 | tf_op jit(solution)/shard_map/ppermute | solution.py:233
  2.1 11.1 %collective-permute-start.5 = (bf16[64,128]{0,1:T(8,128)(2,1)S(1)}, bf16[64,128]{0,1:T(8,128)(2,1)S(1)}, u32[]{:S(2)}, u32[]{:S(2)}) collective-permute-start(bf16[64,128]{0,1:T(8,128)(2,1)S(1)} %pad_maximum_fusion.3), channel_id=1, source_target_pairs={{0,2},{1,3},{2,0},{3,1},{4,6},{5,7},{6,4},{7,5},{8,10},{9,11},{10,... | collective-permute-start | bytes 49160 | tf_op jit(solution)/shard_map/ppermute | solution.py:233
  4.7 8.7 %collective-permute-start.4 = (bf16[64,128]{0,1:T(8,128)(2,1)S(1)}, bf16[64,128]{0,1:T(8,128)(2,1)S(1)}, u32[]{:S(2)}, u32[]{:S(2)}) collective-permute-start(bf16[64,128]{0,1:T(8,128)(2,1)S(1)} %pad_maximum_fusion.3), channel_id=1, source_target_pairs={{0,3},{1,2},{2,1},{3,0},{4,7},{5,6},{6,5},{7,4},{8,11},{9,10},{10,... | collective-permute-start | bytes 49160 | tf_op jit(solution)/shard_map/ppermute | solution.py:233
  4.8 10.7 %collective-permute-start.3 = (bf16[64,128]{0,1:T(8,128)(2,1)S(1)}, bf16[64,128]{0,1:T(8,128)(2,1)S(1)}, u32[]{:S(2)}, u32[]{:S(2)}) collective-permute-start(bf16[64,128]{0,1:T(8,128)(2,1)S(1)} %pad_maximum_fusion.3), channel_id=1, source_target_pairs={{0,4},{1,5},{2,6},{3,7},{4,0},{5,1},{6,2},{7,3},{8,12},{9,13},{10,... | collective-permute-start | bytes 49160 | tf_op jit(solution)/shard_map/ppermute | solution.py:233
  8.3 18.2 %collective-permute-start.12 = (bf16[32,4096]{1,0:T(8,128)(2,1)S(1)}, bf16[32,4096]{1,0:T(8,128)(2,1)S(1)}, u32[]{:S(2)}, u32[]{:S(2)}) collective-permute-start(bf16[32,4096]{1,0:T(8,128)(2,1)S(1)} %get-tuple-element.10), channel_id=1, source_target_pairs={{0,2},{1,3},{2,0},{3,1},{4,6},{5,7},{6,4},{7,5},{8,10},{9,11},{10,... | collective-permute-start | bytes 786440 | tf_op jit(solution)/shard_map/ppermute | solution.py:233
  12.7 13.9 %collective-permute-start.11 = (bf16[32,4096]{1,0:T(8,128)(2,1)S(1)}, bf16[32,4096]{1,0:T(8,128)(2,1)S(1)}, u32[]{:S(2)}, u32[]{:S(2)}) collective-permute-start(bf16[32,4096]{1,0:T(8,128)(2,1)S(1)} %get-tuple-element.9), channel_id=1, source_target_pairs={{0,2},{1,3},{2,0},{3,1},{4,6},{5,7},{6,4},{7,5},{8,10},{9,11},{10,... | collective-permute-start | bytes 786440 | tf_op jit(solution)/shard_map/ppermute | solution.py:233
  13.3 8.6 %collective-permute-start.2 = (bf16[64,128]{0,1:T(8,128)(2,1)S(1)}, bf16[64,128]{0,1:T(8,128)(2,1)S(1)}, u32[]{:S(2)}, u32[]{:S(2)}) collective-permute-start(bf16[64,128]{0,1:T(8,128)(2,1)S(1)} %pad_maximum_fusion.3), channel_id=1, source_target_pairs={{0,5},{1,4},{2,7},{3,6},{4,1},{5,0},{6,3},{7,2},{8,13},{9,12},{10,... | collective-permute-start | bytes 49160 | tf_op jit(solution)/shard_map/ppermute | solution.py:233
  13.4 9.7 %collective-permute-start.1 = (bf16[64,128]{0,1:T(8,128)(2,1)S(1)}, bf16[64,128]{0,1:T(8,128)(2,1)S(1)}, u32[]{:S(2)}, u32[]{:S(2)}) collective-permute-start(bf16[64,128]{0,1:T(8,128)(2,1)S(1)} %pad_maximum_fusion.3), channel_id=1, source_target_pairs={{0,6},{1,7},{2,4},{3,5},{4,2},{5,3},{6,0},{7,1},{8,14},{9,15},{10,... | collective-permute-start | bytes 49160 | tf_op jit(solution)/shard_map/ppermute | solution.py:233
  15.4 10.1 %collective-permute-start = (bf16[64,128]{0,1:T(8,128)(2,1)S(1)}, bf16[64,128]{0,1:T(8,128)(2,1)S(1)}, u32[]{:S(2)}, u32[]{:S(2)}) collective-permute-start(bf16[64,128]{0,1:T(8,128)(2,1)S(1)} %pad_maximum_fusion.3), channel_id=1, source_target_pairs={{0,7},{1,6},{2,5},{3,4},{4,3},{5,2},{6,1},{7,0},{8,15},{9,14},{10,... | collective-permute-start | bytes 49160 | tf_op jit(solution)/shard_map/ppermute | solution.py:233
  21.9 65.0 %collective-permute-start.10 = (bf16[2,32,4096]{2,1,0:T(8,128)(2,1)S(1)}, bf16[2,32,4096]{2,1,0:T(8,128)(2,1)S(1)}, u32[]{:S(2)}, u32[]{:S(2)}) collective-permute-start(bf16[2,32,4096]{2,1,0:T(8,128)(2,1)S(1)} %bitcast.63), channel_id=1, source_target_pairs={{0,1},{1,0},{2,3},{3,2},{4,5},{5,4},{6,7},{7,6},{8,9},{9,8},{10,11... | collective-permute-start | bytes 1572872 | tf_op jit(solution)/shard_map/ppermute | solution.py:233
  23.1 9.2 %collective-permute-start.15 = (bf16[32,4096]{1,0:T(8,128)(2,1)S(1)}, bf16[32,4096]{1,0:T(8,128)(2,1)S(1)}, u32[]{:S(2)}, u32[]{:S(2)}) collective-permute-start(bf16[32,4096]{1,0:T(8,128)(2,1)S(1)} %get-tuple-element.10), channel_id=1, source_target_pairs={{0,4},{1,5},{2,6},{3,7},{4,0},{5,1},{6,2},{7,3},{8,12},{9,13},{10,... | collective-permute-start | bytes 786440 | tf_op jit(solution)/shard_map/ppermute | solution.py:233
  25.5 17.1 %copy-start.12 = (pred[2,2]{1,0:T(4,128)(4,1)S(1)}, pred[2,2]{1,0:T(4,128)(4,1)}, u32[]{:S(2)}) copy-start(pred[2,2]{1,0:T(4,128)(4,1)} %copy.98) | copy-start | bytes 16
  25.5 12.5 %collective-permute-start.14 = (bf16[32,4096]{1,0:T(8,128)(2,1)S(1)}, bf16[32,4096]{1,0:T(8,128)(2,1)}, u32[]{:S(2)}, u32[]{:S(2)}) collective-permute-start(bf16[32,4096]{1,0:T(8,128)(2,1)S(1)} %get-tuple-element.9), channel_id=1, source_target_pairs={{0,4},{1,5},{2,6},{3,7},{4,0},{5,1},{6,2},{7,3},{8,12},{9,13},{10,... | collective-permute-start | bytes 786440 | tf_op jit(solution)/shard_map/ppermute | solution.py:233
  26.5 16.2 %copy-start.10 = (bf16[64,128]{1,0:T(8,128)(2,1)S(1)}, bf16[64,128]{1,0:T(8,128)(2,1)}, u32[]{:S(2)}) copy-start(bf16[64,128]{1,0:T(8,128)(2,1)} %copy.89) | copy-start | bytes 49156
  26.5 16.2 %copy-start.13 = (pred[2,2]{1,0:T(4,128)(4,1)S(1)}, pred[2,2]{1,0:T(4,128)(4,1)}, u32[]{:S(2)}) copy-start(pred[2,2]{1,0:T(4,128)(4,1)} %copy.96) | copy-start | bytes 16
  26.5 16.2 %copy-start.14 = (pred[2,2]{1,0:T(4,128)(4,1)S(1)}, pred[2,2]{1,0:T(4,128)(4,1)}, u32[]{:S(2)}) copy-start(pred[2,2]{1,0:T(4,128)(4,1)} %copy.94) | copy-start | bytes 16
  26.5 16.2 %copy-start.15 = (pred[2,2]{1,0:T(4,128)(4,1)S(1)}, pred[2,2]{1,0:T(4,128)(4,1)}, u32[]{:S(2)}) copy-start(pred[2,2]{1,0:T(4,128)(4,1)} %copy.92) | copy-start | bytes 16
  26.5 16.2 %copy-start.16 = (pred[2,2]{1,0:T(4,128)(4,1)S(1)}, pred[2,2]{1,0:T(4,128)(4,1)}, u32[]{:S(2)}) copy-start(pred[2,2]{1,0:T(4,128)(4,1)} %copy.90) | copy-start | bytes 16
  26.5 16.2 %copy-start.17 = (pred[2,2]{1,0:T(4,128)(4,1)S(1)}, pred[2,2]{1,0:T(4,128)(4,1)}, u32[]{:S(2)}) copy-start(pred[2,2]{1,0:T(4,128)(4,1)} %copy.86) | copy-start | bytes 16
  26.6 18.1 %copy-start.18 = (s32[4]{0:T(128)S(1)}, s32[4]{0:T(128)}, u32[]{:S(2)}) copy-start(s32[4]{0:T(128)} %fusion.2) | copy-start | bytes 52
  26.6 60.3 %collective-permute-start.13 = (bf16[2,32,4096]{2,1,0:T(8,128)(2,1)S(1)}, bf16[2,32,4096]{2,1,0:T(8,128)(2,1)S(1)}, u32[]{:S(2)}, u32[]{:S(2)}) collective-permute-start(bf16[2,32,4096]{2,1,0:T(8,128)(2,1)S(1)} %pad_maximum_fusion.refs_6_), channel_id=1, source_target_pairs={{0,1},{1,0},{2,3},{3,2},{4,5},{5,4},{6,7},{7,6},{8,9},{9,8},{10,11... | collective-permute-start | bytes 1572872 | tf_op jit(solution)/shard_map/ppermute | solution.py:233
  26.7 15.8 %collective-permute-start.17 = (bf16[32,4096]{1,0:T(8,128)(2,1)S(1)}, bf16[32,4096]{1,0:T(8,128)(2,1)S(1)}, u32[]{:S(2)}, u32[]{:S(2)}) collective-permute-start(bf16[32,4096]{1,0:T(8,128)(2,1)S(1)} %collective-permute-done.11), channel_id=1, source_target_pairs={{0,4},{1,5},{2,6},{3,7},{4,0},{5,1},{6,2},{7,3},{8,12},{9,13},{10,... | collective-permute-start | bytes 786440 | tf_op jit(solution)/shard_map/ppermute | solution.py:233
  32.3 6.8 %collective-permute-start.18 = (bf16[32,4096]{1,0:T(8,128)(2,1)S(1)}, bf16[32,4096]{1,0:T(8,128)(2,1)S(1)}, u32[]{:S(2)}, u32[]{:S(2)}) collective-permute-start(bf16[32,4096]{1,0:T(8,128)(2,1)S(1)} %collective-permute-done.15), channel_id=1, source_target_pairs={{0,2},{1,3},{2,0},{3,1},{4,6},{5,7},{6,4},{7,5},{8,10},{9,11},{10,... | collective-permute-start | bytes 786440 | tf_op jit(solution)/shard_map/ppermute | solution.py:233
  39.0 47.9 %collective-permute-start.16 = (bf16[2,32,4096]{2,1,0:T(8,128)(2,1)S(1)}, bf16[2,32,4096]{2,1,0:T(8,128)(2,1)}, u32[]{:S(2)}, u32[]{:S(2)}) collective-permute-start(bf16[2,32,4096]{2,1,0:T(8,128)(2,1)S(1)} %pad_maximum_fusion.1.refs_8_), channel_id=1, source_target_pairs={{0,1},{1,0},{2,3},{3,2},{4,5},{5,4},{6,7},{7,6},{8,9},{9,8},{10,11... | collective-permute-start | bytes 1572872 | tf_op jit(solution)/shard_map/ppermute | solution.py:233
  42.6 44.3 %collective-permute-start.19 = (bf16[2,32,4096]{2,1,0:T(8,128)(2,1)S(1)}, bf16[2,32,4096]{2,1,0:T(8,128)(2,1)}, u32[]{:S(2)}, u32[]{:S(2)}) collective-permute-start(bf16[2,32,4096]{2,1,0:T(8,128)(2,1)S(1)} %pad_maximum_fusion.2.refs_10_), channel_id=1, source_target_pairs={{0,1},{1,0},{2,3},{3,2},{4,5},{5,4},{6,7},{7,6},{8,9},{9,8},{10,11... | collective-permute-start | bytes 1572872 | tf_op jit(solution)/shard_map/ppermute | solution.py:233
  42.9 12.6 %collective-permute-start.7 = (bf16[2,2,64,128]{3,2,1,0:T(8,128)(2,1)S(1)}, bf16[2,2,64,128]{3,2,1,0:T(8,128)(2,1)S(1)}, u32[]{:S(2)}, u32[]{:S(2)}) collective-permute-start(bf16[2,2,64,128]{3,2,1,0:T(8,128)(2,1)S(1)} %select_select_fusion.density_ref), channel_id=1, source_target_pairs={{0,8},{8,0},{16,24},{24,16},{1,9},{9,1},{17,25},{25,17},{2,10},{10... | collective-permute-start | bytes 196616 | tf_op jit(solution)/shard_map/ppermute | solution.py:236
  55.5 6.4 %collective-permute-start.8 = (bf16[2,2,64,128]{3,2,1,0:T(8,128)(2,1)S(1)}, bf16[2,2,64,128]{3,2,1,0:T(8,128)(2,1)S(1)}, u32[]{:S(2)}, u32[]{:S(2)}) collective-permute-start(bf16[2,2,64,128]{3,2,1,0:T(8,128)(2,1)S(1)} %select_select_fusion.density_ref), channel_id=1, source_target_pairs={{0,16},{8,24},{16,0},{24,8},{1,17},{9,25},{17,1},{25,9},{2,18},{10... | collective-permute-start | bytes 196616 | tf_op jit(solution)/shard_map/ppermute | solution.py:236
  61.9 19.1 %collective-permute-start.9 = (bf16[2,2,64,128]{3,2,1,0:T(8,128)(2,1)S(1)}, bf16[2,2,64,128]{3,2,1,0:T(8,128)(2,1)S(1)}, u32[]{:S(2)}, u32[]{:S(2)}) collective-permute-start(bf16[2,2,64,128]{3,2,1,0:T(8,128)(2,1)S(1)} %select_select_fusion.density_ref), channel_id=1, source_target_pairs={{0,24},{8,16},{16,8},{24,0},{1,25},{9,17},{17,9},{25,1},{2,26},{10... | collective-permute-start | bytes 196616 | tf_op jit(solution)/shard_map/ppermute | solution.py:236
  94.6 4.5 %collective-permute-start.20 = (bf16[128,256]{1,0:T(8,128)(2,1)S(1)}, bf16[128,256]{1,0:T(8,128)(2,1)S(1)}, u32[]{:S(2)}, u32[]{:S(2)}) collective-permute-start(bf16[128,256]{1,0:T(8,128)(2,1)S(1)} %get-tuple-element.13), channel_id=1, source_target_pairs={{0,8},{8,0},{16,24},{24,16},{1,9},{9,1},{17,25},{25,17},{2,10},{10... | collective-permute-start | bytes 196616 | tf_op jit(solution)/shard_map/ppermute | solution.py:236
  94.7 5.2 %collective-permute-start.21 = (bf16[128,256]{1,0:T(8,128)(2,1)S(1)}, bf16[128,256]{1,0:T(8,128)(2,1)S(1)}, u32[]{:S(2)}, u32[]{:S(2)}) collective-permute-start(bf16[128,256]{1,0:T(8,128)(2,1)S(1)} %get-tuple-element.12), channel_id=1, source_target_pairs={{0,16},{8,24},{16,0},{24,8},{1,17},{9,25},{17,1},{25,9},{2,18},{10... | collective-permute-start | bytes 196616 | tf_op jit(solution)/shard_map/ppermute | solution.py:236
  96.4 6.1 %collective-permute-start.22 = (bf16[128,256]{1,0:T(8,128)(2,1)S(1)}, bf16[128,256]{1,0:T(8,128)(2,1)S(1)}, u32[]{:S(2)}, u32[]{:S(2)}) collective-permute-start(bf16[128,256]{1,0:T(8,128)(2,1)S(1)} %get-tuple-element.11), channel_id=1, source_target_pairs={{0,24},{8,16},{16,8},{24,0},{1,25},{9,17},{17,9},{25,1},{2,26},{10... | collective-permute-start | bytes 196616 | tf_op jit(solution)/shard_map/ppermute | solution.py:236
  (10 other events, 85.3 us)

commit v2 on v0

--- a/solution.py
+++ b/solution.py
@@ -1,9 +1,15 @@
+import functools
+
 import jax
 import jax.numpy as jnp
 from jax import lax
+from jax.experimental import pallas as pl
+from jax.experimental.pallas import tpu as pltpu
 from jax.sharding import PartitionSpec as P
 
 MOST = 6
+HALF = 64
+LANES = 128
 
 
 def listed_blocks(pair_lists, pair_index):
@@ -40,7 +46,7 @@
     return filled.reshape(pair_count * row_count, local_rows.shape[2])
 
 
-def per_device(integrals, pair_lists, occ_density, virt_density, cosine_weights, coulomb_blocks):
+def any_slice(integrals, pair_lists, occ_density, virt_density, cosine_weights, coulomb_blocks):
     tensor_size = lax.axis_size("tensor")
     owner_pair = lax.axis_index("tensor")
     local_count = integrals.shape[0]
@@ -101,6 +107,321 @@
     return screened.reshape(1, local_count, slab_rows)
 
 
+def exchange_halves(even, odd):
+    left = lax.broadcasted_iota(jnp.int32, even.shape, 1) < HALF
+    first = jnp.where(left, even, pltpu.roll(odd, HALF, 1))
+    second = jnp.where(left, pltpu.roll(even, HALF, 1), odd)
+    return first, second
+
+
+def own_kernel(
+    rows_ref, occupied_ref, virtual_ref, low_ref, high_ref, density_ref, share_ref, two_ref, done
+):
+    share = share_ref.shape[0]
+    caps, pair_width = share_ref.shape[1:]
+    first = pl.multiple_of(lax.axis_index("tm") * share, share)
+    copies = [
+        pltpu.make_async_copy(rows_ref.at[pl.ds(first, share)], share_ref, done.at[0]),
+        pltpu.make_async_copy(occupied_ref.at[0, 0], two_ref.at[0], done.at[1]),
+        pltpu.make_async_copy(virtual_ref.at[0, 0], two_ref.at[1], done.at[2]),
+    ]
+    for copy in copies:
+        copy.start()
+    for copy in copies[1:]:
+        copy.wait()
+    both = jnp.concatenate([two_ref[0], two_ref[1]], axis=1)
+    density_ref[...] = both
+    half = share // 2
+    for piece in range(HALF // half):
+        place = caps * pair_width + piece * LANES
+        block = both[piece * half : (piece + 1) * half]
+        low_ref[:, place : place + LANES] = block
+        high_ref[:, place : place + LANES] = block
+    copies[0].wait()
+    width = 1024
+    for place in range(0, pair_width, width):
+        apart = jnp.swapaxes(share_ref[:, :, place : place + width], 0, 1)
+        for column in range(caps):
+            lanes = slice(column * pair_width + place, column * pair_width + place + width)
+            low_ref[:, lanes] = apart[column, :half]
+            high_ref[:, lanes] = apart[column, half:]
+
+
+def pair_kernel(low_ref, high_ref, x_ref, y_ref, *refs):
+    to_x_ref, to_y_ref = refs[-2:]
+    caps, pair_width = to_x_ref.shape[1], to_x_ref.shape[3]
+    for column in range(caps):
+        lanes = slice(column * pair_width, (column + 1) * pair_width)
+        to_x_ref[0, column] = high_ref[:, lanes]
+        to_x_ref[1, column] = y_ref[:, lanes]
+        to_y_ref[0, column] = low_ref[:, lanes]
+        to_y_ref[1, column] = x_ref[:, lanes]
+
+
+def gather_kernel(density_ref, x_ref, y_ref, d_ref, out_ref):
+    half = x_ref.shape[0]
+    start = x_ref.shape[1] - HALF // half * LANES
+    out_ref[0] = density_ref[...]
+    out_ref[3] = d_ref[...]
+    for piece in range(HALF // half):
+        lanes = slice(start + piece * LANES, start + (piece + 1) * LANES)
+        out_ref[1, piece * half : (piece + 1) * half] = x_ref[:, lanes]
+        out_ref[2, piece * half : (piece + 1) * half] = y_ref[:, lanes]
+
+
+def order_kernel(x_ref, y_ref, *refs):
+    refs[-2][...] = x_ref[...]
+    refs[-1][...] = y_ref[...]
+
+
+def turn_kernel(rows_ref, out_ref, apart_ref):
+    caps, parts, count, pair_width = out_ref.shape
+    width = 1024
+    for place in range(0, pair_width, width):
+        block = rows_ref[:, :, place : place + width]
+        apart_ref[:, :, place : place + width] = jnp.swapaxes(block, 0, 1)
+    for column in range(caps):
+        for part in range(parts):
+            lanes = [
+                apart_ref[column, part * count : (part + 1) * count, place : place + LANES]
+                for place in range(0, pair_width, LANES)
+            ]
+            by_row = jnp.swapaxes(jnp.stack(lanes), 0, 1)
+            for low in range(count // 2):
+                first, second = exchange_halves(by_row[low], by_row[low + count // 2])
+                place = slice(low * LANES, (low + 1) * LANES)
+                out_ref[column, part, : count // 2, place] = first
+                out_ref[column, part, count // 2 :, place] = second
+
+
+def pick_kernel(lists_ref, near_ref, core_ref, after_ref, out_ref, all_ref):
+    device = lax.axis_index("tensor")
+    for move in range(4):
+        all_ref[2 * move] = near_ref[move]
+        all_ref[2 * move + 1] = core_ref[move]
+    row = lax.broadcasted_iota(jnp.int32, (HALF, HALF), 0)
+    col = lax.broadcasted_iota(jnp.int32, (HALF, HALF), 1)
+    source = 2 * (col % (HALF // 2)) + col // (HALF // 2)
+    order = (row == source).astype(jnp.float32).astype(jnp.bfloat16)
+    for column in range(out_ref.shape[0]):
+        for part in range(out_ref.shape[1]):
+            pair = lists_ref[column, 2 * device + part]
+            chosen = all_ref[pair ^ device]
+            turned = chosen[:, :HALF].astype(jnp.float32).T.astype(jnp.bfloat16)
+            moved = jnp.dot(turned, order, preferred_element_type=jnp.float32)
+            both = jnp.concatenate([moved, chosen[:, HALF:].astype(jnp.float32)], axis=1)
+            out_ref[column, part] = both.astype(jnp.bfloat16)
+
+
+def mix_kernel(turned_ref, density_ref, out_ref, mark_ref):
+    caps, parts, count, pair_width = out_ref.shape
+    wide = 4 * HALF
+    row_ids = lax.broadcasted_iota(jnp.int32, (wide, wide), 0) // HALF
+    col_ids = lax.broadcasted_iota(jnp.int32, (wide, wide), 1) // HALF
+    groups = pair_width // wide
+    mark_ref[...] = jnp.zeros_like(mark_ref)
+    for column in range(caps):
+        for part in range(parts):
+            occupied = density_ref[column, part, :, :HALF]
+            virtual = density_ref[column, part, :, HALF:].astype(jnp.float32)
+            twice = jnp.concatenate([virtual, virtual], axis=1)
+            strip = jnp.concatenate([twice, twice], axis=1)
+            tiled = jnp.concatenate([strip, strip, strip, strip], axis=0)
+            diagonal = jnp.where(row_ids == col_ids, tiled, 0.0).astype(jnp.bfloat16)
+            halves = []
+            for group in range(groups):
+                half_done = jnp.dot(
+                    occupied,
+                    turned_ref[column, part, :, group * wide : (group + 1) * wide],
+                    preferred_element_type=jnp.float32,
+                )
+                halves.append(half_done.astype(jnp.bfloat16))
+            mixed = jnp.dot(
+                jnp.concatenate(halves, axis=0), diagonal, preferred_element_type=jnp.float32
+            ).astype(jnp.bfloat16)
+            near = mixed[:, :LANES].reshape(groups, HALF, LANES)
+            far = mixed[:, LANES:].reshape(groups, HALF, LANES)
+            by_row = jnp.stack([near, far], axis=1).reshape(2 * groups, HALF, LANES)
+            by_row = jnp.swapaxes(by_row, 0, 1)
+            for pair in range(HALF // 2):
+                first, second = exchange_halves(by_row[2 * pair], by_row[2 * pair + 1])
+                place = slice(pair * LANES, (pair + 1) * LANES)
+                out_ref[column, part, : count // 2, place] = first
+                out_ref[column, part, count // 2 :, place] = second
+
+
+def gram_kernel(weights_ref, lists_ref, *refs):
+    mixed_refs, near_refs, core_refs, out_ref = refs[:4], refs[4:8], refs[8:12], refs[12]
+    plane = lax.axis_index("tm")
+    device = lax.axis_index("tensor")
+    caps = mixed_refs[0].shape[0]
+    rows, columns = out_ref.shape[1:]
+    owner = lax.broadcasted_iota(jnp.int32, (1, columns), 1) // (columns // 8)
+    for part in range(rows // HALF):
+        chi = [None] * 4
+        for mine in range(caps):
+            pair = lists_ref[mine, 2 * device + part]
+            listed = jnp.zeros((1, columns), jnp.int32)
+            right = []
+            for move in range(8):
+                block = 2 * (device ^ move) + plane // 2
+                second = (lists_ref[1, block] == pair).astype(jnp.int32)
+                either = second + (lists_ref[0, block] == pair).astype(jnp.int32)
+                listed = jnp.where(owner == move, either, listed)
+                to_x, to_y, from_x, from_y = core_refs if move % 2 else near_refs
+                halves = (
+                    (to_y.at[0], to_x.at[0]),
+                    (to_y.at[1], from_x.at[0]),
+                    (from_y.at[0], to_x.at[1]),
+                    (from_y.at[1], from_x.at[1]),
+                )[move // 2]
+                right += [half[second] for half in halves]
+            left = [mixed[mine, part] for mixed in mixed_refs]
+            found = lax.dot_general(
+                jnp.concatenate(left, axis=0),
+                jnp.concatenate(right, axis=0),
+                (((1,), (1,)), ((), ())),
+                preferred_element_type=jnp.float32,
+            )
+            found = jnp.where(listed > 0, found, 0.0)
+            for time in range(4):
+                term = found[time * HALF : (time + 1) * HALF]
+                chi[time] = term if chi[time] is None else chi[time] + term
+        for freq in range(4):
+            value = weights_ref[plane ^ freq, plane] * chi[0]
+            for time in range(1, 4):
+                value = value + weights_ref[plane ^ freq, plane ^ time] * chi[time]
+            out_ref[freq, part * HALF : (part + 1) * HALF, :] = value.astype(out_ref.dtype)
+
+
+def screen_kernel(chi_ref, r1, r2, r3, factor_ref, out_ref):
+    plane = lax.axis_index("tm")
+    device = lax.axis_index("tensor")
+    share = r1.shape[1] // 8
+    for move in range(8):
+        owner = device ^ move
+        sums = []
+        for pair in ((0, 1), (2, 3)):
+            total = None
+            for slot in pair:
+                other = plane ^ slot
+                source = chi_ref.at[0] if slot == 0 else (r1, r2, r3)[slot - 1]
+                left = source[:, move * share : (move + 1) * share]
+                first = pl.multiple_of((other % 2) * share, share)
+                factor = factor_ref[2 * owner + other // 2, pl.ds(first, share), :]
+                term = jnp.dot(
+                    left, factor.astype(jnp.bfloat16), preferred_element_type=jnp.float32
+                )
+                total = term if total is None else total + term
+            sums.append(total)
+        low = jnp.where(plane < 2, sums[0], sums[1])
+        high = jnp.where(plane < 2, sums[1], sums[0])
+        place = pl.ds(pl.multiple_of(owner * LANES, LANES), LANES)
+        out_ref[0, :, place] = jnp.concatenate([low, high], axis=1)
+
+
+def small_slice(integrals, pair_lists, occ_density, virt_density, cosine_weights, coulomb_blocks):
+    local_count, caps, pair_width = integrals.shape
+    share = local_count // 4
+    columns = 8 * share
+    vmem = pl.BlockSpec(memory_space=pltpu.VMEM)
+    smem = pl.BlockSpec(memory_space=pltpu.SMEM)
+    tiles = jax.ShapeDtypeStruct((caps, 2, HALF, pair_width), jnp.bfloat16)
+
+    def kernel(body, out_shape, in_specs, microseconds, scratch=(), room=16):
+        return pl.pallas_call(
+            body,
+            out_shape=out_shape,
+            in_specs=in_specs,
+            out_specs=jax.tree.map(lambda _: vmem, out_shape),
+            scratch_shapes=list(scratch),
+            compiler_params=pltpu.CompilerParams(vmem_limit_bytes=room * 1024 * 1024),
+            cost_estimate=pl.CostEstimate(
+                flops=int(microseconds * 1e9), bytes_accessed=0, transcendentals=0
+            ),
+        )
+
+    def across(array, move):
+        return lax.ppermute(array, "tensor", [(i, i ^ move) for i in range(8)])
+
+    def planes(array, move):
+        return lax.ppermute(array, "tm", [(i, i ^ move) for i in range(4)])
+
+    lists = pair_lists.T
+    half = share // 2
+    message = jax.ShapeDtypeStruct(
+        (half, caps * pair_width + HALF // half * LANES), jnp.bfloat16
+    )
+    block = jax.ShapeDtypeStruct((HALF, LANES), jnp.bfloat16)
+    both = jax.ShapeDtypeStruct((2, caps, half, pair_width), jnp.bfloat16)
+    low, high, density = kernel(
+        own_kernel,
+        [message, message, block],
+        [pl.BlockSpec(memory_space=pltpu.HBM)] * 3,
+        2,
+        [
+            pltpu.VMEM((share, caps, pair_width), jnp.bfloat16),
+            pltpu.VMEM((2, HALF, HALF), jnp.bfloat16),
+            pltpu.SemaphoreType.DMA((3,)),
+        ],
+        room=62,
+    )(integrals, occ_density, virt_density)
+    x_low = across(low, 2)
+    y_high = across(high, 4)
+    turned = kernel(
+        turn_kernel, tiles, [vmem], 1.2, [pltpu.VMEM((caps, local_count, pair_width), jnp.bfloat16)]
+    )(integrals)
+    near = kernel(
+        gather_kernel, jax.ShapeDtypeStruct((4, HALF, LANES), jnp.bfloat16), [vmem] * 4, 0.2
+    )(density, x_low, y_high, across(density, 6))
+    to_x, to_y = kernel(pair_kernel, [both] * 2, [vmem] * 6, 0.3)(
+        low, high, x_low, y_high, turned, near
+    )
+    picked = kernel(
+        pick_kernel,
+        jax.ShapeDtypeStruct((caps, 2, HALF, LANES), jnp.bfloat16),
+        [smem] + [vmem] * 3,
+        1,
+        [pltpu.VMEM((8, HALF, LANES), jnp.bfloat16)],
+    )(lists, near, across(near, 1), to_x)
+    per_time = [picked] + [planes(picked, move) for move in range(1, 4)]
+
+    mark = jax.ShapeDtypeStruct((8, LANES), jnp.float32)
+    mixed, marks = zip(
+        *[kernel(mix_kernel, [tiles, mark], [vmem] * 2, 0.1)(turned, each) for each in per_time]
+    )
+
+    from_x, from_y = kernel(order_kernel, [both] * 2, [vmem] * 6, 0.3)(
+        across(to_x, 2), across(to_y, 4), *marks[:3], per_time[3]
+    )
+    pieces = [to_x, to_y, from_x, from_y]
+    chi = kernel(
+        gram_kernel,
+        jax.ShapeDtypeStruct((4, local_count, columns), jnp.bfloat16),
+        [smem, smem] + [vmem] * 12,
+        3,
+    )(cosine_weights, lists, *mixed, *pieces, *[across(piece, 1) for piece in pieces])
+
+    received = [planes(chi[move], move) for move in range(1, 4)]
+    return kernel(
+        screen_kernel,
+        jax.ShapeDtypeStruct((1, local_count, 8 * LANES), jnp.float32),
+        [vmem] * 5,
+        1,
+    )(chi, *received, coulomb_blocks)
+
+
+def per_device(integrals, pair_lists, occ_density, virt_density, cosine_weights, coulomb_blocks):
+    planned = (
+        lax.axis_size("tm") == 4
+        and lax.axis_size("tensor") == 8
+        and integrals.shape == (2 * HALF, 2, HALF * HALF)
+        and coulomb_blocks.shape == (16, HALF, HALF)
+    )
+    step = small_slice if planned else any_slice
+    return step(integrals, pair_lists, occ_density, virt_density, cosine_weights, coulomb_blocks)
+
+
 def solution(mesh):
     in_specs = (
         P("tensor", None, None),

time: 282 us -> 46.5 us (0.16); the launches traced: 278 us -> 46.2 us
  local copies, waits for them, and re-layouts: 117 us -> 1.69 us
  waiting for transfers between devices: 83.4 us -> 12.4 us
  other arithmetic: 28.5 us -> 0 us
  blocking collectives: 21.6 us -> 0 us
  Pallas kernels: 0 us -> 15.7 us
  matrix products: 15.5 us -> 0 us
  starting transfers between devices: 12.4 us -> 16.3 us
    all_to_all x2 -> x0, waiting for transfers between devices: 83.4 us -> none  [the longest x1 71.5 us: per_device(): lax.all_to_all(outgoing, 'tensor', split_axis=0, concat_axis=0, tiled=True)]
    scatter x1 -> x0, local copies, waits for them, and re-layouts: 65.4 us -> none  [pack_rows(): filled = zero_buffer.at[targets, places].set(local_rows)]
    all_to_all x2 -> x0, blocking collectives: 21.6 us -> none  [the longest x1 11.8 us: per_device(): lax.all_to_all(chi_rows[None].astype(jnp.bfloat16), 'tm', split_axis=2, c...]
    gather x6 -> x0, local copies, waits for them, and re-layouts: 19.1 us -> none  [the longest x1 12.7 us: per_device(): tile_rows = jnp.take(arrived, wanted, axis=0, mode='fill', fill_value=0)]
    ppermute x0 -> x16, starting transfers between devices: none -> 16.3 us  [the longest x6 8.92 us: planes(): return lax.ppermute(array, 'tm', [(i, i ^ move) for i in range(4)])]
    pallas_call x0 -> x12, Pallas kernels: none -> 15.7 us  [the longest x4 6.94 us: small_slice(): kernel(mix_kernel, [tiles, mark], [vmem] * 2, 0.1)(turned, each)]
    dot_general x6 -> x0, matrix products: 15.5 us -> none  [the longest x1 6.84 us: density_product(): jnp.dot(row_data.reshape(row_count * orbital_width, orbital_width), virtu...]
    all_to_all x2 -> x0, starting transfers between devices: 12.4 us -> none  [the longest x1 8.84 us: per_device(): lax.all_to_all(outgoing, 'tensor', split_axis=0, concat_axis=0, tiled=True)]
  transfers between devices with their start and end apart: 2 -> 16, of which waited for: 2 -> 7; matrix products, arithmetic and copies ran while one was open for 8% -> 0% of each run, Pallas kernels for 0% -> 20%
where the time goes in v2:
time: 46.5 us; the launch traced here: 46.2 us
  starting transfers between devices  16.3 us (35%)
  Pallas kernels  15.7 us (34%)
  waiting for transfers between devices  12.4 us (27%)
  local copies, waits for them, and re-layouts  1.69 us (4%)
    ppermute x6, starting transfers between devices, planes(): return lax.ppermute(array, 'tm', [(i, i ^ move) for i in range(4)])  8.92 us
    ppermute x10, starting transfers between devices, across(): return lax.ppermute(array, 'tensor', [(i, i ^ move) for i in range(8)])  7.4 us
    pallas_call x4, Pallas kernels, small_slice(): kernel(mix_kernel, [tiles, mark], [vmem] * 2, 0.1)(turned, each)  6.94 us
    ppermute x6, waiting for transfers between devices, planes(): return lax.ppermute(array, 'tm', [(i, i ^ move) for i in range(4)])  6.67 us
    ppermute x10, waiting for transfers between devices, across(): return lax.ppermute(array, 'tensor', [(i, i ^ move) for i in range(8)])  5.69 us
    pallas_call x1, Pallas kernels, small_slice(): kernel(gram_kernel, jax.ShapeDtypeStruct((4, local_count, columns), jnp.b...  3.07 us
    pallas_call x1, Pallas kernels, small_slice(): kernel(own_kernel, [message, message, block], [pl.BlockSpec(memory_space=...  1.93 us
    unnamed x14, local copies, waits for them, and re-layouts  1.67 us
  transfers between devices with their start and end apart: 16, of which 7 were waited for; matrix products, arithmetic and copies ran while one was open for 0% of the time, Pallas kernels for 20%

profile of v2, /device:TPU:0, one launch (start us, length us, event | category | flops | bytes accessed | tf_op | source)
XLA Modules:
  0.0 46.2 jit_solution(8097519543835018304)
XLA Ops:
  0.0 1.9 %shard_map.65 = (bf16[16,8704]{1,0:T(8,128)(2,1)}, bf16[16,8704]{1,0:T(8,128)(2,1)}, bf16[64,128]{1,0:T(8,128)(2,1)}) custom-call(bf16[128,2,4096]{2,1,0:T(2,128)(2,1)} %rows_ref.3, bf16[1,1,64,64]{3,2,1,0:T(8,128)(2,1)} %occupied_ref.1, bf16[1,1,64,64]{3,2,1,0:T(8,128)(2,1)} %virtual_ref.1), custom_call_target="tpu_custom_call" | custom-call | flops 2000000000 | tf_op jit(solution)/shard_map/pallas_call | solution.py:357
  1.9 3.0 %collective-permute-start = (bf16[16,8704]{1,0:T(8,128)(2,1)}, bf16[16,8704]{1,0:T(8,128)(2,1)S(1)}, u32[]{:S(2)}, u32[]{:S(2)}) collective-permute-start(bf16[16,8704]{1,0:T(8,128)(2,1)} %get-tuple-element.20.low_ref), channel_id=1, source_target_pairs={{0,2},{1,3},{2,0},{3,1},{4,6},{5,7},{6,4},{7,5},{8,10},{9,11},{10,... | collective-permute-start | bytes 835592 | tf_op jit(solution)/shard_map/ppermute | solution.py:345
  4.9 1.5 %collective-permute-start.1 = (bf16[16,8704]{1,0:T(8,128)(2,1)}, bf16[16,8704]{1,0:T(8,128)(2,1)S(1)}, u32[]{:S(2)}, u32[]{:S(2)}) collective-permute-start(bf16[16,8704]{1,0:T(8,128)(2,1)} %get-tuple-element.21.high_ref), channel_id=1, source_target_pairs={{0,4},{1,5},{2,6},{3,7},{4,0},{5,1},{6,2},{7,3},{8,12},{9,13},{10,... | collective-permute-start | bytes 835592 | tf_op jit(solution)/shard_map/ppermute | solution.py:345
  6.5 1.6 %copy-done.4 = bf16[128,2,4096]{2,1,0:T(2,128)(2,1)S(1)} copy-done((bf16[128,2,4096]{2,1,0:T(2,128)(2,1)S(1)}, bf16[128,2,4096]{2,1,0:T(2,128)(2,1)}, u32[]{:S(2)}) %copy-start.4) | copy-done | bytes 2097176
  8.1 1.5 %shard_map.64.refs_0_.turned_ref = bf16[2,2,64,4096]{3,2,1,0:T(8,128)(2,1)S(1)} custom-call(bf16[128,2,4096]{2,1,0:T(2,128)(2,1)S(1)} %copy-done.4), custom_call_target="tpu_custom_call" | custom-call | flops 1200000000 | tf_op jit(solution)/shard_map/pallas_call | solution.py:371
  9.6 3.8 %collective-permute-done.2.d_ref = bf16[64,128]{1,0:T(8,128)(2,1)S(1)} collective-permute-done((bf16[64,128]{1,0:T(8,128)(2,1)}, bf16[64,128]{1,0:T(8,128)(2,1)S(1)}, u32[]{:S(2)}, u32[]{:S(2)}) %collective-permute-start.2) | collective-permute-done | bytes 16416 | tf_op jit(solution)/shard_map/ppermute | solution.py:345
  13.5 0.1 collective-permute-done.1.y_ref
  13.7 0.1 shard_map.67
  13.7 1.3 %collective-permute-start.7 = (bf16[2,2,16,4096]{3,2,1,0:T(8,128)(2,1)S(1)}, bf16[2,2,16,4096]{3,2,1,0:T(8,128)(2,1)S(1)}, u32[]{:S(2)}, u32[]{:S(2)}) collective-permute-start(bf16[2,2,16,4096]{3,2,1,0:T(8,128)(2,1)S(1)} %get-tuple-element.22.after_ref.refs_4_), channel_id=1, source_target_pairs={{0,2},{1,3},{2,0},{3,1},{4,6},{5,7},{6,4},{7,5},{8,10},{9,11},{10,... | collective-permute-start | bytes 1572872 | tf_op jit(solution)/shard_map/ppermute | solution.py:345
  15.0 0.8 %collective-permute-start.8 = (bf16[2,2,16,4096]{3,2,1,0:T(8,128)(2,1)S(1)}, bf16[2,2,16,4096]{3,2,1,0:T(8,128)(2,1)S(1)}, u32[]{:S(2)}, u32[]{:S(2)}) collective-permute-start(bf16[2,2,16,4096]{3,2,1,0:T(8,128)(2,1)S(1)} %get-tuple-element.27.refs_5_), channel_id=1, source_target_pairs={{0,4},{1,5},{2,6},{3,7},{4,0},{5,1},{6,2},{7,3},{8,12},{9,13},{10,... | collective-permute-start | bytes 1572872 | tf_op jit(solution)/shard_map/ppermute | solution.py:345
  15.9 1.3 %collective-permute-done.3.core_ref = bf16[4,64,128]{2,1,0:T(8,128)(2,1)S(1)} collective-permute-done((bf16[4,64,128]{2,1,0:T(8,128)(2,1)S(1)}, bf16[4,64,128]{2,1,0:T(8,128)(2,1)S(1)}, u32[]{:S(2)}, u32[]{:S(2)}) %collective-permute-start.3) | collective-permute-done | bytes 65568 | tf_op jit(solution)/shard_map/ppermute | solution.py:345
  17.1 0.8 %shard_map.68.density_ref = bf16[2,2,64,128]{3,2,1,0:T(8,128)(2,1)S(1)} custom-call(s32[2,16]{1,0:T(2,128)S(1)} %bitcast.7, bf16[4,64,128]{2,1,0:T(8,128)(2,1)S(1)} %shard_map.66.refs_1_.near_ref, bf16[4,64,128]{2,1,0:T(8,128)(2,1)S(1)} %collective-permute-done.3.core_ref, bf16[2,2,16,4096]{3,2,1,0:T(8,128)(2,1)S(1)} %get-tuple-element.22.after_ref.refs_4_), custom_call_target="tpu_custom_call" | custom-call | flops 1000000000 | tf_op jit(solution)/shard_map/pallas_call | solution.py:380
  17.9 1.6 %collective-permute-start.4 = (bf16[2,2,64,128]{3,2,1,0:T(8,128)(2,1)S(1)}, bf16[2,2,64,128]{3,2,1,0:T(8,128)(2,1)S(1)}, u32[]{:S(2)}, u32[]{:S(2)}) collective-permute-start(bf16[2,2,64,128]{3,2,1,0:T(8,128)(2,1)S(1)} %shard_map.68.density_ref), channel_id=1, source_target_pairs={{0,8},{8,0},{16,24},{24,16},{1,9},{9,1},{17,25},{25,17},{2,10},{10... | collective-permute-start | bytes 196616 | tf_op jit(solution)/shard_map/ppermute | solution.py:348
  19.5 2.6 %collective-permute-start.5 = (bf16[2,2,64,128]{3,2,1,0:T(8,128)(2,1)S(1)}, bf16[2,2,64,128]{3,2,1,0:T(8,128)(2,1)S(1)}, u32[]{:S(2)}, u32[]{:S(2)}) collective-permute-start(bf16[2,2,64,128]{3,2,1,0:T(8,128)(2,1)S(1)} %shard_map.68.density_ref), channel_id=1, source_target_pairs={{0,16},{8,24},{16,0},{24,8},{1,17},{9,25},{17,1},{25,9},{2,18},{10... | collective-permute-start | bytes 196616 | tf_op jit(solution)/shard_map/ppermute | solution.py:348
  22.1 0.2 collective-permute-start.6
  22.3 1.7 %shard_map.69 = (bf16[2,2,64,4096]{3,2,1,0:T(8,128)(2,1)S(1)}, f32[8,128]{1,0:T(8,128)S(1)}) custom-call(bf16[2,2,64,4096]{3,2,1,0:T(8,128)(2,1)S(1)} %shard_map.64.refs_0_.turned_ref, bf16[2,2,64,128]{3,2,1,0:T(8,128)(2,1)S(1)} %shard_map.68.density_ref), custom_call_target="tpu_custom_call" | custom-call | flops 100000000 | tf_op jit(solution)/shard_map/pallas_call | solution.py:391
  24.1 0.1 collective-permute-start.9
  24.2 1.7 %shard_map.70 = (bf16[2,2,64,4096]{3,2,1,0:T(8,128)(2,1)S(1)}, f32[8,128]{1,0:T(8,128)S(1)}) custom-call(bf16[2,2,64,4096]{3,2,1,0:T(8,128)(2,1)S(1)} %shard_map.64.refs_0_.turned_ref, bf16[2,2,64,128]{3,2,1,0:T(8,128)(2,1)S(1)} %collective-permute-done.4.density_ref), custom_call_target="tpu_custom_call" | custom-call | flops 100000000 | tf_op jit(solution)/shard_map/pallas_call | solution.py:391
  25.9 1.2 %collective-permute-done.5.density_ref = bf16[2,2,64,128]{3,2,1,0:T(8,128)(2,1)S(1)} collective-permute-done((bf16[2,2,64,128]{3,2,1,0:T(8,128)(2,1)S(1)}, bf16[2,2,64,128]{3,2,1,0:T(8,128)(2,1)S(1)}, u32[]{:S(2)}, u32[]{:S(2)}) %collective-permute-start.5) | collective-permute-done | bytes 65568 | tf_op jit(solution)/shard_map/ppermute | solution.py:348
  27.1 1.7 %shard_map.71 = (bf16[2,2,64,4096]{3,2,1,0:T(8,128)(2,1)S(1)}, f32[8,128]{1,0:T(8,128)S(1)}) custom-call(bf16[2,2,64,4096]{3,2,1,0:T(8,128)(2,1)S(1)} %shard_map.64.refs_0_.turned_ref, bf16[2,2,64,128]{3,2,1,0:T(8,128)(2,1)S(1)} %collective-permute-done.5.density_ref), custom_call_target="tpu_custom_call" | custom-call | flops 100000000 | tf_op jit(solution)/shard_map/pallas_call | solution.py:391
  28.9 0.1 shard_map.73
  28.9 0.6 %collective-permute-start.11 = (bf16[2,2,16,4096]{3,2,1,0:T(8,128)(2,1)S(1)}, bf16[2,2,16,4096]{3,2,1,0:T(8,128)(2,1)S(1)}, u32[]{:S(2)}, u32[]{:S(2)}) collective-permute-start(bf16[2,2,16,4096]{3,2,1,0:T(8,128)(2,1)S(1)} %get-tuple-element.31.refs_6_), channel_id=1, source_target_pairs={{0,1},{1,0},{2,3},{3,2},{4,5},{5,4},{6,7},{7,6},{8,9},{9,8},{10,11... | collective-permute-start | bytes 1572872 | tf_op jit(solution)/shard_map/ppermute | solution.py:345
  29.5 0.1 collective-permute-start.12
  29.6 1.7 %shard_map.72 = (bf16[2,2,64,4096]{3,2,1,0:T(8,128)(2,1)S(1)}, f32[8,128]{1,0:T(8,128)}) custom-call(bf16[2,2,64,4096]{3,2,1,0:T(8,128)(2,1)S(1)} %shard_map.64.refs_0_.turned_ref, bf16[2,2,64,128]{3,2,1,0:T(8,128)(2,1)S(1)} %collective-permute-done.6.density_ref.refs_3_), custom_call_target="tpu_custom_call" | custom-call | flops 100000000 | tf_op jit(solution)/shard_map/pallas_call | solution.py:391
  31.4 0.4 collective-permute-done.12.refs_11_
  31.8 3.1 %shard_map.74.chi_ref = bf16[4,128,256]{2,1,0:T(8,128)(2,1)S(1)} custom-call(f32[4,4]{1,0:T(4,128)S(1)} %copy-done.2, s32[2,16]{1,0:T(2,128)S(1)} %bitcast.8, bf16[2,2,64,4096]{3,2,1,0:T(8,128)(2,1)S(1)} %get-tuple-element.23.refs_0_, bf16[2,2,64,4096]{3,2,1,0:T(8,128)(2,1)S(1)} %get-tuple-element.24.refs_1_, ...), custom_call_target="tpu_custom_call" | custom-call | flops 3000000000 | tf_op jit(solution)/shard_map/pallas_call | solution.py:398
  34.9 0.5 %collective-permute-start.13 = (bf16[128,256]{1,0:T(8,128)(2,1)S(1)}, bf16[128,256]{1,0:T(8,128)(2,1)S(1)}, u32[]{:S(2)}, u32[]{:S(2)}) collective-permute-start(bf16[128,256]{1,0:T(8,128)(2,1)S(1)} %get-tuple-element.35), channel_id=1, source_target_pairs={{0,8},{8,0},{16,24},{24,16},{1,9},{9,1},{17,25},{25,17},{2,10},{10... | collective-permute-start | bytes 196616 | tf_op jit(solution)/shard_map/ppermute | solution.py:348
  35.4 3.4 %collective-permute-start.14 = (bf16[128,256]{1,0:T(8,128)(2,1)S(1)}, bf16[128,256]{1,0:T(8,128)(2,1)S(1)}, u32[]{:S(2)}, u32[]{:S(2)}) collective-permute-start(bf16[128,256]{1,0:T(8,128)(2,1)S(1)} %get-tuple-element.34), channel_id=1, source_target_pairs={{0,16},{8,24},{16,0},{24,8},{1,17},{9,25},{17,1},{25,9},{2,18},{10... | collective-permute-start | bytes 196616 | tf_op jit(solution)/shard_map/ppermute | solution.py:348
  38.8 0.6 %collective-permute-start.15 = (bf16[128,256]{1,0:T(8,128)(2,1)S(1)}, bf16[128,256]{1,0:T(8,128)(2,1)S(1)}, u32[]{:S(2)}, u32[]{:S(2)}) collective-permute-start(bf16[128,256]{1,0:T(8,128)(2,1)S(1)} %get-tuple-element.33), channel_id=1, source_target_pairs={{0,24},{8,16},{16,8},{24,0},{1,25},{9,17},{17,9},{25,1},{2,26},{10... | collective-permute-start | bytes 196616 | tf_op jit(solution)/shard_map/ppermute | solution.py:348
  39.4 3.5 %collective-permute-done.14.r2 = bf16[128,256]{1,0:T(8,128)(2,1)S(1)} collective-permute-done((bf16[128,256]{1,0:T(8,128)(2,1)S(1)}, bf16[128,256]{1,0:T(8,128)(2,1)S(1)}, u32[]{:S(2)}, u32[]{:S(2)}) %collective-permute-start.14) | collective-permute-done | bytes 65568 | tf_op jit(solution)/shard_map/ppermute | solution.py:348
  42.9 2.0 %collective-permute-done.15.r3 = bf16[128,256]{1,0:T(8,128)(2,1)S(1)} collective-permute-done((bf16[128,256]{1,0:T(8,128)(2,1)S(1)}, bf16[128,256]{1,0:T(8,128)(2,1)S(1)}, u32[]{:S(2)}, u32[]{:S(2)}) %collective-permute-start.15) | collective-permute-done | bytes 65568 | tf_op jit(solution)/shard_map/ppermute | solution.py:348
  44.9 1.3 %shard_map.75 = f32[1,128,1024]{2,1,0:T(8,128)} custom-call(bf16[4,128,256]{2,1,0:T(8,128)(2,1)S(1)} %shard_map.74.chi_ref, bf16[128,256]{1,0:T(8,128)(2,1)S(1)} %collective-permute-done.13.r1, bf16[128,256]{1,0:T(8,128)(2,1)S(1)} %collective-permute-done.14.r2, bf16[128,256]{1,0:T(8,128)(2,1)S(1)} %collective-permute-done.15.r3, f32[16,64,64]{2,1,0:T(8,128)S(1)} %copy-done.5), custom_call_target="tpu_custom_call" | custom-call | flops 1000000000 | tf_op jit(solution)/shard_map/pallas_call | solution.py:406
  (27 shorter events, 0.1 us)
Async XLA Ops:
  1.9 11.5 %collective-permute-start = (bf16[16,8704]{1,0:T(8,128)(2,1)}, bf16[16,8704]{1,0:T(8,128)(2,1)S(1)}, u32[]{:S(2)}, u32[]{:S(2)}) collective-permute-start(bf16[16,8704]{1,0:T(8,128)(2,1)} %get-tuple-element.20.low_ref), channel_id=1, source_target_pairs={{0,2},{1,3},{2,0},{3,1},{4,6},{5,7},{6,4},{7,5},{8,10},{9,11},{10,... | collective-permute-start | bytes 835592 | tf_op jit(solution)/shard_map/ppermute | solution.py:345
  4.9 8.7 %collective-permute-start.1 = (bf16[16,8704]{1,0:T(8,128)(2,1)}, bf16[16,8704]{1,0:T(8,128)(2,1)S(1)}, u32[]{:S(2)}, u32[]{:S(2)}) collective-permute-start(bf16[16,8704]{1,0:T(8,128)(2,1)} %get-tuple-element.21.high_ref), channel_id=1, source_target_pairs={{0,4},{1,5},{2,6},{3,7},{4,0},{5,1},{6,2},{7,3},{8,12},{9,13},{10,... | collective-permute-start | bytes 835592 | tf_op jit(solution)/shard_map/ppermute | solution.py:345
  6.5 7.2 %copy-start = (bf16[16,8704]{1,0:T(8,128)(2,1)S(1)}, bf16[16,8704]{1,0:T(8,128)(2,1)}, u32[]{:S(2)}) copy-start(bf16[16,8704]{1,0:T(8,128)(2,1)} %get-tuple-element.20.low_ref) | copy-start | bytes 835588
  6.5 7.2 %copy-start.1 = (bf16[16,8704]{1,0:T(8,128)(2,1)S(1)}, bf16[16,8704]{1,0:T(8,128)(2,1)}, u32[]{:S(2)}) copy-start(bf16[16,8704]{1,0:T(8,128)(2,1)} %get-tuple-element.21.high_ref) | copy-start | bytes 835588
  6.5 7.0 %collective-permute-start.2 = (bf16[64,128]{1,0:T(8,128)(2,1)}, bf16[64,128]{1,0:T(8,128)(2,1)S(1)}, u32[]{:S(2)}, u32[]{:S(2)}) collective-permute-start(bf16[64,128]{1,0:T(8,128)(2,1)} %get-tuple-element.19.density_ref), channel_id=1, source_target_pairs={{0,6},{1,7},{2,4},{3,5},{4,2},{5,3},{6,0},{7,1},{8,14},{9,15},{10,... | collective-permute-start | bytes 49160 | tf_op jit(solution)/shard_map/ppermute | solution.py:345
  6.5 1.6 %copy-start.4 = (bf16[128,2,4096]{2,1,0:T(2,128)(2,1)S(1)}, bf16[128,2,4096]{2,1,0:T(2,128)(2,1)}, u32[]{:S(2)}) copy-start(bf16[128,2,4096]{2,1,0:T(2,128)(2,1)} %rows_ref.3) | copy-start | bytes 6291460
  8.1 5.5 %copy-start.6 = (bf16[64,128]{1,0:T(8,128)(2,1)S(1)}, bf16[64,128]{1,0:T(8,128)(2,1)}, u32[]{:S(2)}) copy-start(bf16[64,128]{1,0:T(8,128)(2,1)} %get-tuple-element.19.density_ref) | copy-start | bytes 49156
  9.6 7.5 %copy-start.3 = (s32[16,2]{0,1:T(2,128)S(1)}, s32[16,2]{0,1:T(2,128)}, u32[]{:S(2)}) copy-start(s32[16,2]{0,1:T(2,128)} %param.7) | copy-start | bytes 388
  13.7 15.1 %collective-permute-start.7 = (bf16[2,2,16,4096]{3,2,1,0:T(8,128)(2,1)S(1)}, bf16[2,2,16,4096]{3,2,1,0:T(8,128)(2,1)S(1)}, u32[]{:S(2)}, u32[]{:S(2)}) collective-permute-start(bf16[2,2,16,4096]{3,2,1,0:T(8,128)(2,1)S(1)} %get-tuple-element.22.after_ref.refs_4_), channel_id=1, source_target_pairs={{0,2},{1,3},{2,0},{3,1},{4,6},{5,7},{6,4},{7,5},{8,10},{9,11},{10,... | collective-permute-start | bytes 1572872 | tf_op jit(solution)/shard_map/ppermute | solution.py:345
  15.0 13.8 %collective-permute-start.8 = (bf16[2,2,16,4096]{3,2,1,0:T(8,128)(2,1)S(1)}, bf16[2,2,16,4096]{3,2,1,0:T(8,128)(2,1)S(1)}, u32[]{:S(2)}, u32[]{:S(2)}) collective-permute-start(bf16[2,2,16,4096]{3,2,1,0:T(8,128)(2,1)S(1)} %get-tuple-element.27.refs_5_), channel_id=1, source_target_pairs={{0,4},{1,5},{2,6},{3,7},{4,0},{5,1},{6,2},{7,3},{8,12},{9,13},{10,... | collective-permute-start | bytes 1572872 | tf_op jit(solution)/shard_map/ppermute | solution.py:345
  15.9 1.3 %collective-permute-start.3 = (bf16[4,64,128]{2,1,0:T(8,128)(2,1)S(1)}, bf16[4,64,128]{2,1,0:T(8,128)(2,1)S(1)}, u32[]{:S(2)}, u32[]{:S(2)}) collective-permute-start(bf16[4,64,128]{2,1,0:T(8,128)(2,1)S(1)} %shard_map.66.refs_1_.near_ref), channel_id=1, source_target_pairs={{0,1},{1,0},{2,3},{3,2},{4,5},{5,4},{6,7},{7,6},{8,9},{9,8},{10,11... | collective-permute-start | bytes 196616 | tf_op jit(solution)/shard_map/ppermute | solution.py:345
  17.9 6.2 %collective-permute-start.4 = (bf16[2,2,64,128]{3,2,1,0:T(8,128)(2,1)S(1)}, bf16[2,2,64,128]{3,2,1,0:T(8,128)(2,1)S(1)}, u32[]{:S(2)}, u32[]{:S(2)}) collective-permute-start(bf16[2,2,64,128]{3,2,1,0:T(8,128)(2,1)S(1)} %shard_map.68.density_ref), channel_id=1, source_target_pairs={{0,8},{8,0},{16,24},{24,16},{1,9},{9,1},{17,25},{25,17},{2,10},{10... | collective-permute-start | bytes 196616 | tf_op jit(solution)/shard_map/ppermute | solution.py:348
  19.5 7.5 %collective-permute-start.5 = (bf16[2,2,64,128]{3,2,1,0:T(8,128)(2,1)S(1)}, bf16[2,2,64,128]{3,2,1,0:T(8,128)(2,1)S(1)}, u32[]{:S(2)}, u32[]{:S(2)}) collective-permute-start(bf16[2,2,64,128]{3,2,1,0:T(8,128)(2,1)S(1)} %shard_map.68.density_ref), channel_id=1, source_target_pairs={{0,16},{8,24},{16,0},{24,8},{1,17},{9,25},{17,1},{25,9},{2,18},{10... | collective-permute-start | bytes 196616 | tf_op jit(solution)/shard_map/ppermute | solution.py:348
  22.1 6.7 %collective-permute-start.6 = (bf16[2,2,64,128]{3,2,1,0:T(8,128)(2,1)S(1)}, bf16[2,2,64,128]{3,2,1,0:T(8,128)(2,1)S(1)}, u32[]{:S(2)}, u32[]{:S(2)}) collective-permute-start(bf16[2,2,64,128]{3,2,1,0:T(8,128)(2,1)S(1)} %shard_map.68.density_ref), channel_id=1, source_target_pairs={{0,24},{8,16},{16,8},{24,0},{1,25},{9,17},{17,9},{25,1},{2,26},{10... | collective-permute-start | bytes 196616 | tf_op jit(solution)/shard_map/ppermute | solution.py:348
  24.1 7.3 %collective-permute-start.9 = (bf16[2,2,16,4096]{3,2,1,0:T(8,128)(2,1)S(1)}, bf16[2,2,16,4096]{3,2,1,0:T(8,128)(2,1)S(1)}, u32[]{:S(2)}, u32[]{:S(2)}) collective-permute-start(bf16[2,2,16,4096]{3,2,1,0:T(8,128)(2,1)S(1)} %get-tuple-element.22.after_ref.refs_4_), channel_id=1, source_target_pairs={{0,1},{1,0},{2,3},{3,2},{4,5},{5,4},{6,7},{7,6},{8,9},{9,8},{10,11... | collective-permute-start | bytes 1572872 | tf_op jit(solution)/shard_map/ppermute | solution.py:345
  27.1 4.3 %collective-permute-start.10 = (bf16[2,2,16,4096]{3,2,1,0:T(8,128)(2,1)S(1)}, bf16[2,2,16,4096]{3,2,1,0:T(8,128)(2,1)S(1)}, u32[]{:S(2)}, u32[]{:S(2)}) collective-permute-start(bf16[2,2,16,4096]{3,2,1,0:T(8,128)(2,1)S(1)} %get-tuple-element.27.refs_5_), channel_id=1, source_target_pairs={{0,1},{1,0},{2,3},{3,2},{4,5},{5,4},{6,7},{7,6},{8,9},{9,8},{10,11... | collective-permute-start | bytes 1572872 | tf_op jit(solution)/shard_map/ppermute | solution.py:345
  28.8 3.0 %copy-start.2 = (f32[4,4]{1,0:T(4,128)S(1)}, f32[4,4]{1,0:T(4,128)}, u32[]{:S(2)}) copy-start(f32[4,4]{1,0:T(4,128)} %weights_ref.1) | copy-start | bytes 196
  28.9 2.4 %collective-permute-start.11 = (bf16[2,2,16,4096]{3,2,1,0:T(8,128)(2,1)S(1)}, bf16[2,2,16,4096]{3,2,1,0:T(8,128)(2,1)S(1)}, u32[]{:S(2)}, u32[]{:S(2)}) collective-permute-start(bf16[2,2,16,4096]{3,2,1,0:T(8,128)(2,1)S(1)} %get-tuple-element.31.refs_6_), channel_id=1, source_target_pairs={{0,1},{1,0},{2,3},{3,2},{4,5},{5,4},{6,7},{7,6},{8,9},{9,8},{10,11... | collective-permute-start | bytes 1572872 | tf_op jit(solution)/shard_map/ppermute | solution.py:345
  29.5 2.3 %collective-permute-start.12 = (bf16[2,2,16,4096]{3,2,1,0:T(8,128)(2,1)S(1)}, bf16[2,2,16,4096]{3,2,1,0:T(8,128)(2,1)S(1)}, u32[]{:S(2)}, u32[]{:S(2)}) collective-permute-start(bf16[2,2,16,4096]{3,2,1,0:T(8,128)(2,1)S(1)} %get-tuple-element.32.refs_7_), channel_id=1, source_target_pairs={{0,1},{1,0},{2,3},{3,2},{4,5},{5,4},{6,7},{7,6},{8,9},{9,8},{10,11... | collective-permute-start | bytes 1572872 | tf_op jit(solution)/shard_map/ppermute | solution.py:345
  31.8 13.1 %copy-start.5 = (f32[16,64,64]{2,1,0:T(8,128)S(1)}, f32[16,64,64]{2,1,0:T(8,128)}, u32[]{:S(2)}) copy-start(f32[16,64,64]{2,1,0:T(8,128)} %factor_ref.1) | copy-start | bytes 786436
  34.9 4.5 %collective-permute-start.13 = (bf16[128,256]{1,0:T(8,128)(2,1)S(1)}, bf16[128,256]{1,0:T(8,128)(2,1)S(1)}, u32[]{:S(2)}, u32[]{:S(2)}) collective-permute-start(bf16[128,256]{1,0:T(8,128)(2,1)S(1)} %get-tuple-element.35), channel_id=1, source_target_pairs={{0,8},{8,0},{16,24},{24,16},{1,9},{9,1},{17,25},{25,17},{2,10},{10... | collective-permute-start | bytes 196616 | tf_op jit(solution)/shard_map/ppermute | solution.py:348
  35.4 7.5 %collective-permute-start.14 = (bf16[128,256]{1,0:T(8,128)(2,1)S(1)}, bf16[128,256]{1,0:T(8,128)(2,1)S(1)}, u32[]{:S(2)}, u32[]{:S(2)}) collective-permute-start(bf16[128,256]{1,0:T(8,128)(2,1)S(1)} %get-tuple-element.34), channel_id=1, source_target_pairs={{0,16},{8,24},{16,0},{24,8},{1,17},{9,25},{17,1},{25,9},{2,18},{10... | collective-permute-start | bytes 196616 | tf_op jit(solution)/shard_map/ppermute | solution.py:348
  38.8 6.1 %collective-permute-start.15 = (bf16[128,256]{1,0:T(8,128)(2,1)S(1)}, bf16[128,256]{1,0:T(8,128)(2,1)S(1)}, u32[]{:S(2)}, u32[]{:S(2)}) collective-permute-start(bf16[128,256]{1,0:T(8,128)(2,1)S(1)} %get-tuple-element.33), channel_id=1, source_target_pairs={{0,24},{8,16},{16,8},{24,0},{1,25},{9,17},{17,9},{25,1},{2,26},{10... | collective-permute-start | bytes 196616 | tf_op jit(solution)/shard_map/ppermute | solution.py:348

commit v3 on v2

--- a/solution.py
+++ b/solution.py
@@ -129,7 +129,13 @@
         copy.start()
     for copy in copies[1:]:
         copy.wait()
-    both = jnp.concatenate([two_ref[0], two_ref[1]], axis=1)
+    row = lax.broadcasted_iota(jnp.int32, (HALF, HALF), 0)
+    col = lax.broadcasted_iota(jnp.int32, (HALF, HALF), 1)
+    source = 2 * (col % (HALF // 2)) + col // (HALF // 2)
+    order = (row == source).astype(jnp.float32).astype(jnp.bfloat16)
+    turned = two_ref[0].astype(jnp.float32).T.astype(jnp.bfloat16)
+    moved = jnp.dot(turned, order, preferred_element_type=jnp.float32)
+    both = jnp.concatenate([moved, two_ref[1].astype(jnp.float32)], axis=1).astype(jnp.bfloat16)
     density_ref[...] = both
     half = share // 2
     for piece in range(HALF // half):
@@ -199,18 +205,10 @@
     for move in range(4):
         all_ref[2 * move] = near_ref[move]
         all_ref[2 * move + 1] = core_ref[move]
-    row = lax.broadcasted_iota(jnp.int32, (HALF, HALF), 0)
-    col = lax.broadcasted_iota(jnp.int32, (HALF, HALF), 1)
-    source = 2 * (col % (HALF // 2)) + col // (HALF // 2)
-    order = (row == source).astype(jnp.float32).astype(jnp.bfloat16)
     for column in range(out_ref.shape[0]):
         for part in range(out_ref.shape[1]):
             pair = lists_ref[column, 2 * device + part]
-            chosen = all_ref[pair ^ device]
-            turned = chosen[:, :HALF].astype(jnp.float32).T.astype(jnp.bfloat16)
-            moved = jnp.dot(turned, order, preferred_element_type=jnp.float32)
-            both = jnp.concatenate([moved, chosen[:, HALF:].astype(jnp.float32)], axis=1)
-            out_ref[column, part] = both.astype(jnp.bfloat16)
+            out_ref[column, part] = all_ref[pair ^ device]
 
 
 def mix_kernel(turned_ref, density_ref, out_ref, mark_ref):
@@ -294,30 +292,44 @@
             out_ref[freq, part * HALF : (part + 1) * HALF, :] = value.astype(out_ref.dtype)
 
 
-def screen_kernel(chi_ref, r1, r2, r3, factor_ref, out_ref):
+def factor_kernel(factor_ref, out_ref):
     plane = lax.axis_index("tm")
     device = lax.axis_index("tensor")
-    share = r1.shape[1] // 8
-    for move in range(8):
-        owner = device ^ move
-        sums = []
-        for pair in ((0, 1), (2, 3)):
-            total = None
-            for slot in pair:
-                other = plane ^ slot
-                source = chi_ref.at[0] if slot == 0 else (r1, r2, r3)[slot - 1]
-                left = source[:, move * share : (move + 1) * share]
-                first = pl.multiple_of((other % 2) * share, share)
-                factor = factor_ref[2 * owner + other // 2, pl.ds(first, share), :]
-                term = jnp.dot(
-                    left, factor.astype(jnp.bfloat16), preferred_element_type=jnp.float32
-                )
-                total = term if total is None else total + term
-            sums.append(total)
-        low = jnp.where(plane < 2, sums[0], sums[1])
-        high = jnp.where(plane < 2, sums[1], sums[0])
-        place = pl.ds(pl.multiple_of(owner * LANES, LANES), LANES)
-        out_ref[0, :, place] = jnp.concatenate([low, high], axis=1)
+    share = out_ref.shape[1] // 8
+    out_ref[...] = jnp.zeros_like(out_ref)
+    right = lax.broadcasted_iota(jnp.int32, (share, LANES), 1) // HALF
+    for slot in range(4):
+        other = plane ^ slot
+        first = pl.multiple_of((other % 2) * share, share)
+        for move in range(8):
+            factor = factor_ref[2 * (device ^ move) + other // 2, pl.ds(first, share), :]
+            wide = jnp.where(right == other // 2, jnp.concatenate([factor, factor], axis=1), 0.0)
+            rows = slice(move * share, (move + 1) * share)
+            out_ref[slot, rows, move * LANES : (move + 1) * LANES] = wide.astype(out_ref.dtype)
+
+
+def screen_kernel(chi_ref, r1, r2, r3, factor_ref, out_ref, block_ref, done):
+    device = lax.axis_index("tensor")
+    sources = [chi_ref[0], r1[...], r2[...], r3[...]]
+    copies = []
+    for pair in range(4):
+        lanes = slice(2 * pair * LANES, 2 * (pair + 1) * LANES)
+        total = None
+        for slot in range(4):
+            term = jnp.dot(
+                sources[slot], factor_ref[slot, :, lanes], preferred_element_type=jnp.float32
+            )
+            total = term if total is None else total + term
+        for side in range(2):
+            move = 2 * pair + side
+            block_ref[move] = total[:, side * LANES : (side + 1) * LANES]
+            place = pl.ds(pl.multiple_of((device ^ move) * LANES, LANES), LANES)
+            copies.append(
+                pltpu.make_async_copy(block_ref.at[move], out_ref.at[0, :, place], done.at[move])
+            )
+            copies[-1].start()
+    for copy in copies:
+        copy.wait()
 
 
 def small_slice(integrals, pair_lists, occ_density, virt_density, cosine_weights, coulomb_blocks):
@@ -328,17 +340,18 @@
     smem = pl.BlockSpec(memory_space=pltpu.SMEM)
     tiles = jax.ShapeDtypeStruct((caps, 2, HALF, pair_width), jnp.bfloat16)
 
-    def kernel(body, out_shape, in_specs, microseconds, scratch=(), room=16):
+    def kernel(body, out_shape, in_specs, microseconds, scratch=(), room=16, **options):
+        options = {"out_specs": jax.tree.map(lambda _: vmem, out_shape), **options}
         return pl.pallas_call(
             body,
             out_shape=out_shape,
             in_specs=in_specs,
-            out_specs=jax.tree.map(lambda _: vmem, out_shape),
             scratch_shapes=list(scratch),
             compiler_params=pltpu.CompilerParams(vmem_limit_bytes=room * 1024 * 1024),
             cost_estimate=pl.CostEstimate(
                 flops=int(microseconds * 1e9), bytes_accessed=0, transcendentals=0
             ),
+            **options,
         )
 
     def across(array, move):
@@ -364,7 +377,7 @@
             pltpu.VMEM((2, HALF, HALF), jnp.bfloat16),
             pltpu.SemaphoreType.DMA((3,)),
         ],
-        room=62,
+        room=61,
     )(integrals, occ_density, virt_density)
     x_low = across(low, 2)
     y_high = across(high, 4)
@@ -374,8 +387,11 @@
     near = kernel(
         gather_kernel, jax.ShapeDtypeStruct((4, HALF, LANES), jnp.bfloat16), [vmem] * 4, 0.2
     )(density, x_low, y_high, across(density, 6))
-    to_x, to_y = kernel(pair_kernel, [both] * 2, [vmem] * 6, 0.3)(
-        low, high, x_low, y_high, turned, near
+    factors = kernel(
+        factor_kernel, jax.ShapeDtypeStruct((4, columns, 8 * LANES), jnp.bfloat16), [vmem], 1
+    )(coulomb_blocks)
+    to_x, to_y = kernel(pair_kernel, [both] * 2, [vmem] * 7, 0.3)(
+        low, high, x_low, y_high, turned, near, factors
     )
     picked = kernel(
         pick_kernel,
@@ -408,7 +424,9 @@
         jax.ShapeDtypeStruct((1, local_count, 8 * LANES), jnp.float32),
         [vmem] * 5,
         1,
-    )(chi, *received, coulomb_blocks)
+        [pltpu.VMEM((8, local_count, LANES), jnp.float32), pltpu.SemaphoreType.DMA((8,))],
+        out_specs=pl.BlockSpec(memory_space=pltpu.HBM),
+    )(chi, *received, factors)
 
 
 def per_device(integrals, pair_lists, occ_density, virt_density, cosine_weights, coulomb_blocks):

time: 46.5 us -> 46.4 us (level)
  local copies, waits for them, and re-layouts: 1.69 us -> 0.05 us
  waiting for transfers between devices: 12.4 us -> 13.7 us
    unnamed x14, local copies, waits for them, and re-layouts: 1.67 us -> 0.03 us
    ppermute x10, waiting for transfers between devices: 5.69 us -> 7.06 us  [across(): return lax.ppermute(array, 'tensor', [(i, i ^ move) for i in range(8)])]
where the time goes in v3:
time: 46.4 us; the launch traced here: 46.2 us
  starting transfers between devices  16.3 us (35%)
  Pallas kernels  15.8 us (34%)
  waiting for transfers between devices  13.7 us (30%)
    ppermute x6, starting transfers between devices, planes(): return lax.ppermute(array, 'tm', [(i, i ^ move) for i in range(4)])  8.92 us
    ppermute x10, starting transfers between devices, across(): return lax.ppermute(array, 'tensor', [(i, i ^ move) for i in range(8)])  7.38 us
    ppermute x10, waiting for transfers between devices, across(): return lax.ppermute(array, 'tensor', [(i, i ^ move) for i in range(8)])  7.06 us
    pallas_call x4, Pallas kernels, small_slice(): kernel(mix_kernel, [tiles, mark], [vmem] * 2, 0.1)(turned, each)  6.94 us
    ppermute x6, waiting for transfers between devices, planes(): return lax.ppermute(array, 'tm', [(i, i ^ move) for i in range(4)])  6.67 us
    pallas_call x1, Pallas kernels, small_slice(): kernel(gram_kernel, jax.ShapeDtypeStruct((4, local_count, columns), jnp.b...  3.08 us
    pallas_call x1, Pallas kernels, small_slice(): kernel(own_kernel, [message, message, block], [pl.BlockSpec(memory_space=...  2.13 us
    pallas_call x1, Pallas kernels, small_slice(): kernel(turn_kernel, tiles, [vmem], 1.2, [pltpu.VMEM((caps, local_count, p...  1.47 us
  transfers between devices with their start and end apart: 16, of which 7 were waited for; matrix products, arithmetic and copies ran while one was open for 0% of the time, Pallas kernels for 20%

profile of v3, /device:TPU:0, one launch (start us, length us, event | category | flops | bytes accessed | tf_op | source)
XLA Modules:
  0.0 46.2 jit_solution(5026347174846311494)
XLA Ops:
  0.0 2.1 %shard_map.65 = (bf16[16,8704]{1,0:T(8,128)(2,1)}, bf16[16,8704]{1,0:T(8,128)(2,1)}, bf16[64,128]{1,0:T(8,128)(2,1)}) custom-call(bf16[128,2,4096]{2,1,0:T(2,128)(2,1)} %rows_ref.3, bf16[1,1,64,64]{3,2,1,0:T(8,128)(2,1)} %occupied_ref.1, bf16[1,1,64,64]{3,2,1,0:T(8,128)(2,1)} %virtual_ref.1), custom_call_target="tpu_custom_call" | custom-call | flops 2000000000 | tf_op jit(solution)/shard_map/pallas_call | solution.py:370
  2.1 3.0 %collective-permute-start = (bf16[16,8704]{1,0:T(8,128)(2,1)}, bf16[16,8704]{1,0:T(8,128)(2,1)S(1)}, u32[]{:S(2)}, u32[]{:S(2)}) collective-permute-start(bf16[16,8704]{1,0:T(8,128)(2,1)} %get-tuple-element.20.low_ref), channel_id=1, source_target_pairs={{0,2},{1,3},{2,0},{3,1},{4,6},{5,7},{6,4},{7,5},{8,10},{9,11},{10,... | collective-permute-start | bytes 835592 | tf_op jit(solution)/shard_map/ppermute | solution.py:358
  5.1 1.5 %collective-permute-start.1 = (bf16[16,8704]{1,0:T(8,128)(2,1)}, bf16[16,8704]{1,0:T(8,128)(2,1)S(1)}, u32[]{:S(2)}, u32[]{:S(2)}) collective-permute-start(bf16[16,8704]{1,0:T(8,128)(2,1)} %get-tuple-element.21.high_ref), channel_id=1, source_target_pairs={{0,4},{1,5},{2,6},{3,7},{4,0},{5,1},{6,2},{7,3},{8,12},{9,13},{10,... | collective-permute-start | bytes 835592 | tf_op jit(solution)/shard_map/ppermute | solution.py:358
  6.7 1.5 %shard_map.64.refs_0_.turned_ref = bf16[2,2,64,4096]{3,2,1,0:T(8,128)(2,1)S(1)} custom-call(bf16[128,2,4096]{2,1,0:T(2,128)(2,1)S(1)} %copy-done.4), custom_call_target="tpu_custom_call" | custom-call | flops 1200000000 | tf_op jit(solution)/shard_map/pallas_call | solution.py:384
  8.2 0.2 shard_map.67.refs_2_.factor_ref
  8.5 5.2 %collective-permute-done.2.d_ref = bf16[64,128]{1,0:T(8,128)(2,1)S(1)} collective-permute-done((bf16[64,128]{1,0:T(8,128)(2,1)}, bf16[64,128]{1,0:T(8,128)(2,1)S(1)}, u32[]{:S(2)}, u32[]{:S(2)}) %collective-permute-start.2) | collective-permute-done | bytes 16416 | tf_op jit(solution)/shard_map/ppermute | solution.py:358
  13.7 0.1 collective-permute-done.1.y_ref
  13.9 0.1 shard_map.68
  13.9 1.3 %collective-permute-start.7 = (bf16[2,2,16,4096]{3,2,1,0:T(8,128)(2,1)S(1)}, bf16[2,2,16,4096]{3,2,1,0:T(8,128)(2,1)S(1)}, u32[]{:S(2)}, u32[]{:S(2)}) collective-permute-start(bf16[2,2,16,4096]{3,2,1,0:T(8,128)(2,1)S(1)} %get-tuple-element.22.after_ref.refs_4_), channel_id=1, source_target_pairs={{0,2},{1,3},{2,0},{3,1},{4,6},{5,7},{6,4},{7,5},{8,10},{9,11},{10,... | collective-permute-start | bytes 1572872 | tf_op jit(solution)/shard_map/ppermute | solution.py:358
  15.3 0.8 %collective-permute-start.8 = (bf16[2,2,16,4096]{3,2,1,0:T(8,128)(2,1)S(1)}, bf16[2,2,16,4096]{3,2,1,0:T(8,128)(2,1)S(1)}, u32[]{:S(2)}, u32[]{:S(2)}) collective-permute-start(bf16[2,2,16,4096]{3,2,1,0:T(8,128)(2,1)S(1)} %get-tuple-element.27.refs_5_), channel_id=1, source_target_pairs={{0,4},{1,5},{2,6},{3,7},{4,0},{5,1},{6,2},{7,3},{8,12},{9,13},{10,... | collective-permute-start | bytes 1572872 | tf_op jit(solution)/shard_map/ppermute | solution.py:358
  16.1 1.3 %collective-permute-done.3.core_ref = bf16[4,64,128]{2,1,0:T(8,128)(2,1)S(1)} collective-permute-done((bf16[4,64,128]{2,1,0:T(8,128)(2,1)S(1)}, bf16[4,64,128]{2,1,0:T(8,128)(2,1)S(1)}, u32[]{:S(2)}, u32[]{:S(2)}) %collective-permute-start.3) | collective-permute-done | bytes 65568 | tf_op jit(solution)/shard_map/ppermute | solution.py:358
  17.3 0.6 %shard_map.69.density_ref = bf16[2,2,64,128]{3,2,1,0:T(8,128)(2,1)S(1)} custom-call(s32[2,16]{1,0:T(2,128)S(1)} %bitcast.7, bf16[4,64,128]{2,1,0:T(8,128)(2,1)S(1)} %shard_map.66.refs_1_.near_ref, bf16[4,64,128]{2,1,0:T(8,128)(2,1)S(1)} %collective-permute-done.3.core_ref, bf16[2,2,16,4096]{3,2,1,0:T(8,128)(2,1)S(1)} %get-tuple-element.22.after_ref.refs_4_), custom_call_target="tpu_custom_call" | custom-call | flops 1000000000 | tf_op jit(solution)/shard_map/pallas_call | solution.py:396
  17.9 1.6 %collective-permute-start.4 = (bf16[2,2,64,128]{3,2,1,0:T(8,128)(2,1)S(1)}, bf16[2,2,64,128]{3,2,1,0:T(8,128)(2,1)S(1)}, u32[]{:S(2)}, u32[]{:S(2)}) collective-permute-start(bf16[2,2,64,128]{3,2,1,0:T(8,128)(2,1)S(1)} %shard_map.69.density_ref), channel_id=1, source_target_pairs={{0,8},{8,0},{16,24},{24,16},{1,9},{9,1},{17,25},{25,17},{2,10},{10... | collective-permute-start | bytes 196616 | tf_op jit(solution)/shard_map/ppermute | solution.py:361
  19.5 2.6 %collective-permute-start.5 = (bf16[2,2,64,128]{3,2,1,0:T(8,128)(2,1)S(1)}, bf16[2,2,64,128]{3,2,1,0:T(8,128)(2,1)S(1)}, u32[]{:S(2)}, u32[]{:S(2)}) collective-permute-start(bf16[2,2,64,128]{3,2,1,0:T(8,128)(2,1)S(1)} %shard_map.69.density_ref), channel_id=1, source_target_pairs={{0,16},{8,24},{16,0},{24,8},{1,17},{9,25},{17,1},{25,9},{2,18},{10... | collective-permute-start | bytes 196616 | tf_op jit(solution)/shard_map/ppermute | solution.py:361
  22.1 0.2 collective-permute-start.6
  22.4 1.7 %shard_map.70 = (bf16[2,2,64,4096]{3,2,1,0:T(8,128)(2,1)S(1)}, f32[8,128]{1,0:T(8,128)S(1)}) custom-call(bf16[2,2,64,4096]{3,2,1,0:T(8,128)(2,1)S(1)} %shard_map.64.refs_0_.turned_ref, bf16[2,2,64,128]{3,2,1,0:T(8,128)(2,1)S(1)} %shard_map.69.density_ref), custom_call_target="tpu_custom_call" | custom-call | flops 100000000 | tf_op jit(solution)/shard_map/pallas_call | solution.py:407
  24.1 0.1 collective-permute-start.9
  24.2 1.7 %shard_map.71 = (bf16[2,2,64,4096]{3,2,1,0:T(8,128)(2,1)S(1)}, f32[8,128]{1,0:T(8,128)S(1)}) custom-call(bf16[2,2,64,4096]{3,2,1,0:T(8,128)(2,1)S(1)} %shard_map.64.refs_0_.turned_ref, bf16[2,2,64,128]{3,2,1,0:T(8,128)(2,1)S(1)} %collective-permute-done.4.density_ref), custom_call_target="tpu_custom_call" | custom-call | flops 100000000 | tf_op jit(solution)/shard_map/pallas_call | solution.py:407
  25.9 1.2 %collective-permute-done.5.density_ref = bf16[2,2,64,128]{3,2,1,0:T(8,128)(2,1)S(1)} collective-permute-done((bf16[2,2,64,128]{3,2,1,0:T(8,128)(2,1)S(1)}, bf16[2,2,64,128]{3,2,1,0:T(8,128)(2,1)S(1)}, u32[]{:S(2)}, u32[]{:S(2)}) %collective-permute-start.5) | collective-permute-done | bytes 65568 | tf_op jit(solution)/shard_map/ppermute | solution.py:361
  27.1 1.7 %shard_map.72 = (bf16[2,2,64,4096]{3,2,1,0:T(8,128)(2,1)S(1)}, f32[8,128]{1,0:T(8,128)S(1)}) custom-call(bf16[2,2,64,4096]{3,2,1,0:T(8,128)(2,1)S(1)} %shard_map.64.refs_0_.turned_ref, bf16[2,2,64,128]{3,2,1,0:T(8,128)(2,1)S(1)} %collective-permute-done.5.density_ref), custom_call_target="tpu_custom_call" | custom-call | flops 100000000 | tf_op jit(solution)/shard_map/pallas_call | solution.py:407
  28.9 0.1 shard_map.74
  29.0 0.6 %collective-permute-start.11 = (bf16[2,2,16,4096]{3,2,1,0:T(8,128)(2,1)S(1)}, bf16[2,2,16,4096]{3,2,1,0:T(8,128)(2,1)S(1)}, u32[]{:S(2)}, u32[]{:S(2)}) collective-permute-start(bf16[2,2,16,4096]{3,2,1,0:T(8,128)(2,1)S(1)} %get-tuple-element.31.refs_6_), channel_id=1, source_target_pairs={{0,1},{1,0},{2,3},{3,2},{4,5},{5,4},{6,7},{7,6},{8,9},{9,8},{10,11... | collective-permute-start | bytes 1572872 | tf_op jit(solution)/shard_map/ppermute | solution.py:358
  29.5 0.1 collective-permute-start.12
  29.6 1.7 %shard_map.73 = (bf16[2,2,64,4096]{3,2,1,0:T(8,128)(2,1)S(1)}, f32[8,128]{1,0:T(8,128)}) custom-call(bf16[2,2,64,4096]{3,2,1,0:T(8,128)(2,1)S(1)} %shard_map.64.refs_0_.turned_ref, bf16[2,2,64,128]{3,2,1,0:T(8,128)(2,1)S(1)} %collective-permute-done.6.density_ref.refs_3_), custom_call_target="tpu_custom_call" | custom-call | flops 100000000 | tf_op jit(solution)/shard_map/pallas_call | solution.py:407
  31.4 0.4 collective-permute-done.12.refs_11_
  31.8 3.1 %shard_map.75.chi_ref = bf16[4,128,256]{2,1,0:T(8,128)(2,1)S(1)} custom-call(f32[4,4]{1,0:T(4,128)S(1)} %copy-done.2, s32[2,16]{1,0:T(2,128)S(1)} %bitcast.8, bf16[2,2,64,4096]{3,2,1,0:T(8,128)(2,1)S(1)} %get-tuple-element.23.refs_0_, bf16[2,2,64,4096]{3,2,1,0:T(8,128)(2,1)S(1)} %get-tuple-element.24.refs_1_, ...), custom_call_target="tpu_custom_call" | custom-call | flops 3000000000 | tf_op jit(solution)/shard_map/pallas_call | solution.py:414
  34.9 0.5 %collective-permute-start.13 = (bf16[128,256]{1,0:T(8,128)(2,1)S(1)}, bf16[128,256]{1,0:T(8,128)(2,1)S(1)}, u32[]{:S(2)}, u32[]{:S(2)}) collective-permute-start(bf16[128,256]{1,0:T(8,128)(2,1)S(1)} %get-tuple-element.35), channel_id=1, source_target_pairs={{0,8},{8,0},{16,24},{24,16},{1,9},{9,1},{17,25},{25,17},{2,10},{10... | collective-permute-start | bytes 196616 | tf_op jit(solution)/shard_map/ppermute | solution.py:361
  35.4 3.4 %collective-permute-start.14 = (bf16[128,256]{1,0:T(8,128)(2,1)S(1)}, bf16[128,256]{1,0:T(8,128)(2,1)S(1)}, u32[]{:S(2)}, u32[]{:S(2)}) collective-permute-start(bf16[128,256]{1,0:T(8,128)(2,1)S(1)} %get-tuple-element.34), channel_id=1, source_target_pairs={{0,16},{8,24},{16,0},{24,8},{1,17},{9,25},{17,1},{25,9},{2,18},{10... | collective-permute-start | bytes 196616 | tf_op jit(solution)/shard_map/ppermute | solution.py:361
  38.8 0.6 %collective-permute-start.15 = (bf16[128,256]{1,0:T(8,128)(2,1)S(1)}, bf16[128,256]{1,0:T(8,128)(2,1)S(1)}, u32[]{:S(2)}, u32[]{:S(2)}) collective-permute-start(bf16[128,256]{1,0:T(8,128)(2,1)S(1)} %get-tuple-element.33), channel_id=1, source_target_pairs={{0,24},{8,16},{16,8},{24,0},{1,25},{9,17},{17,9},{25,1},{2,26},{10... | collective-permute-start | bytes 196616 | tf_op jit(solution)/shard_map/ppermute | solution.py:361
  39.4 3.5 %collective-permute-done.14.r2 = bf16[128,256]{1,0:T(8,128)(2,1)S(1)} collective-permute-done((bf16[128,256]{1,0:T(8,128)(2,1)S(1)}, bf16[128,256]{1,0:T(8,128)(2,1)S(1)}, u32[]{:S(2)}, u32[]{:S(2)}) %collective-permute-start.14) | collective-permute-done | bytes 65568 | tf_op jit(solution)/shard_map/ppermute | solution.py:361
  42.9 2.0 %collective-permute-done.15.r3 = bf16[128,256]{1,0:T(8,128)(2,1)S(1)} collective-permute-done((bf16[128,256]{1,0:T(8,128)(2,1)S(1)}, bf16[128,256]{1,0:T(8,128)(2,1)S(1)}, u32[]{:S(2)}, u32[]{:S(2)}) %collective-permute-start.15) | collective-permute-done | bytes 65568 | tf_op jit(solution)/shard_map/ppermute | solution.py:361
  44.9 1.2 %shard_map.76 = f32[1,128,1024]{2,1,0:T(8,128)} custom-call(bf16[4,128,256]{2,1,0:T(8,128)(2,1)S(1)} %shard_map.75.chi_ref, bf16[128,256]{1,0:T(8,128)(2,1)S(1)} %collective-permute-done.13.r1, bf16[128,256]{1,0:T(8,128)(2,1)S(1)} %collective-permute-done.14.r2, bf16[128,256]{1,0:T(8,128)(2,1)S(1)} %collective-permute-done.15.r3, ...), custom_call_target="tpu_custom_call" | custom-call | flops 1000000000 | tf_op jit(solution)/shard_map/pallas_call | solution.py:422
  (28 shorter events, 0.1 us)
Async XLA Ops:
  0.0 6.7 %copy-start.4 = (bf16[128,2,4096]{2,1,0:T(2,128)(2,1)S(1)}, bf16[128,2,4096]{2,1,0:T(2,128)(2,1)}, u32[]{:S(2)}) copy-start(bf16[128,2,4096]{2,1,0:T(2,128)(2,1)} %rows_ref.3) | copy-start | bytes 6291460
  2.1 11.5 %collective-permute-start = (bf16[16,8704]{1,0:T(8,128)(2,1)}, bf16[16,8704]{1,0:T(8,128)(2,1)S(1)}, u32[]{:S(2)}, u32[]{:S(2)}) collective-permute-start(bf16[16,8704]{1,0:T(8,128)(2,1)} %get-tuple-element.20.low_ref), channel_id=1, source_target_pairs={{0,2},{1,3},{2,0},{3,1},{4,6},{5,7},{6,4},{7,5},{8,10},{9,11},{10,... | collective-permute-start | bytes 835592 | tf_op jit(solution)/shard_map/ppermute | solution.py:358
  5.1 8.7 %collective-permute-start.1 = (bf16[16,8704]{1,0:T(8,128)(2,1)}, bf16[16,8704]{1,0:T(8,128)(2,1)S(1)}, u32[]{:S(2)}, u32[]{:S(2)}) collective-permute-start(bf16[16,8704]{1,0:T(8,128)(2,1)} %get-tuple-element.21.high_ref), channel_id=1, source_target_pairs={{0,4},{1,5},{2,6},{3,7},{4,0},{5,1},{6,2},{7,3},{8,12},{9,13},{10,... | collective-permute-start | bytes 835592 | tf_op jit(solution)/shard_map/ppermute | solution.py:358
  6.7 1.5 %copy-start.5 = (f32[16,64,64]{2,1,0:T(8,128)S(1)}, f32[16,64,64]{2,1,0:T(8,128)}, u32[]{:S(2)}) copy-start(f32[16,64,64]{2,1,0:T(8,128)} %factor_ref.1) | copy-start | bytes 786436
  6.7 7.0 %collective-permute-start.2 = (bf16[64,128]{1,0:T(8,128)(2,1)}, bf16[64,128]{1,0:T(8,128)(2,1)S(1)}, u32[]{:S(2)}, u32[]{:S(2)}) collective-permute-start(bf16[64,128]{1,0:T(8,128)(2,1)} %get-tuple-element.19.density_ref), channel_id=1, source_target_pairs={{0,6},{1,7},{2,4},{3,5},{4,2},{5,3},{6,0},{7,1},{8,14},{9,15},{10,... | collective-permute-start | bytes 49160 | tf_op jit(solution)/shard_map/ppermute | solution.py:358
  8.2 5.6 %copy-start.6 = (bf16[64,128]{1,0:T(8,128)(2,1)S(1)}, bf16[64,128]{1,0:T(8,128)(2,1)}, u32[]{:S(2)}) copy-start(bf16[64,128]{1,0:T(8,128)(2,1)} %get-tuple-element.19.density_ref) | copy-start | bytes 49156
  8.2 5.7 %copy-start = (bf16[16,8704]{1,0:T(8,128)(2,1)S(1)}, bf16[16,8704]{1,0:T(8,128)(2,1)}, u32[]{:S(2)}) copy-start(bf16[16,8704]{1,0:T(8,128)(2,1)} %get-tuple-element.20.low_ref) | copy-start | bytes 835588
  8.2 5.7 %copy-start.1 = (bf16[16,8704]{1,0:T(8,128)(2,1)S(1)}, bf16[16,8704]{1,0:T(8,128)(2,1)}, u32[]{:S(2)}) copy-start(bf16[16,8704]{1,0:T(8,128)(2,1)} %get-tuple-element.21.high_ref) | copy-start | bytes 835588
  13.9 3.5 %copy-start.3 = (s32[16,2]{0,1:T(2,128)S(1)}, s32[16,2]{0,1:T(2,128)}, u32[]{:S(2)}) copy-start(s32[16,2]{0,1:T(2,128)} %param.7) | copy-start | bytes 388
  13.9 14.9 %collective-permute-start.7 = (bf16[2,2,16,4096]{3,2,1,0:T(8,128)(2,1)S(1)}, bf16[2,2,16,4096]{3,2,1,0:T(8,128)(2,1)S(1)}, u32[]{:S(2)}, u32[]{:S(2)}) collective-permute-start(bf16[2,2,16,4096]{3,2,1,0:T(8,128)(2,1)S(1)} %get-tuple-element.22.after_ref.refs_4_), channel_id=1, source_target_pairs={{0,2},{1,3},{2,0},{3,1},{4,6},{5,7},{6,4},{7,5},{8,10},{9,11},{10,... | collective-permute-start | bytes 1572872 | tf_op jit(solution)/shard_map/ppermute | solution.py:358
  15.3 13.6 %collective-permute-start.8 = (bf16[2,2,16,4096]{3,2,1,0:T(8,128)(2,1)S(1)}, bf16[2,2,16,4096]{3,2,1,0:T(8,128)(2,1)S(1)}, u32[]{:S(2)}, u32[]{:S(2)}) collective-permute-start(bf16[2,2,16,4096]{3,2,1,0:T(8,128)(2,1)S(1)} %get-tuple-element.27.refs_5_), channel_id=1, source_target_pairs={{0,4},{1,5},{2,6},{3,7},{4,0},{5,1},{6,2},{7,3},{8,12},{9,13},{10,... | collective-permute-start | bytes 1572872 | tf_op jit(solution)/shard_map/ppermute | solution.py:358
  16.1 1.3 %collective-permute-start.3 = (bf16[4,64,128]{2,1,0:T(8,128)(2,1)S(1)}, bf16[4,64,128]{2,1,0:T(8,128)(2,1)S(1)}, u32[]{:S(2)}, u32[]{:S(2)}) collective-permute-start(bf16[4,64,128]{2,1,0:T(8,128)(2,1)S(1)} %shard_map.66.refs_1_.near_ref), channel_id=1, source_target_pairs={{0,1},{1,0},{2,3},{3,2},{4,5},{5,4},{6,7},{7,6},{8,9},{9,8},{10,11... | collective-permute-start | bytes 196616 | tf_op jit(solution)/shard_map/ppermute | solution.py:358
  17.9 6.2 %collective-permute-start.4 = (bf16[2,2,64,128]{3,2,1,0:T(8,128)(2,1)S(1)}, bf16[2,2,64,128]{3,2,1,0:T(8,128)(2,1)S(1)}, u32[]{:S(2)}, u32[]{:S(2)}) collective-permute-start(bf16[2,2,64,128]{3,2,1,0:T(8,128)(2,1)S(1)} %shard_map.69.density_ref), channel_id=1, source_target_pairs={{0,8},{8,0},{16,24},{24,16},{1,9},{9,1},{17,25},{25,17},{2,10},{10... | collective-permute-start | bytes 196616 | tf_op jit(solution)/shard_map/ppermute | solution.py:361
  19.5 7.5 %collective-permute-start.5 = (bf16[2,2,64,128]{3,2,1,0:T(8,128)(2,1)S(1)}, bf16[2,2,64,128]{3,2,1,0:T(8,128)(2,1)S(1)}, u32[]{:S(2)}, u32[]{:S(2)}) collective-permute-start(bf16[2,2,64,128]{3,2,1,0:T(8,128)(2,1)S(1)} %shard_map.69.density_ref), channel_id=1, source_target_pairs={{0,16},{8,24},{16,0},{24,8},{1,17},{9,25},{17,1},{25,9},{2,18},{10... | collective-permute-start | bytes 196616 | tf_op jit(solution)/shard_map/ppermute | solution.py:361
  22.1 6.7 %collective-permute-start.6 = (bf16[2,2,64,128]{3,2,1,0:T(8,128)(2,1)S(1)}, bf16[2,2,64,128]{3,2,1,0:T(8,128)(2,1)S(1)}, u32[]{:S(2)}, u32[]{:S(2)}) collective-permute-start(bf16[2,2,64,128]{3,2,1,0:T(8,128)(2,1)S(1)} %shard_map.69.density_ref), channel_id=1, source_target_pairs={{0,24},{8,16},{16,8},{24,0},{1,25},{9,17},{17,9},{25,1},{2,26},{10... | collective-permute-start | bytes 196616 | tf_op jit(solution)/shard_map/ppermute | solution.py:361
  24.1 7.2 %collective-permute-start.9 = (bf16[2,2,16,4096]{3,2,1,0:T(8,128)(2,1)S(1)}, bf16[2,2,16,4096]{3,2,1,0:T(8,128)(2,1)S(1)}, u32[]{:S(2)}, u32[]{:S(2)}) collective-permute-start(bf16[2,2,16,4096]{3,2,1,0:T(8,128)(2,1)S(1)} %get-tuple-element.22.after_ref.refs_4_), channel_id=1, source_target_pairs={{0,1},{1,0},{2,3},{3,2},{4,5},{5,4},{6,7},{7,6},{8,9},{9,8},{10,11... | collective-permute-start | bytes 1572872 | tf_op jit(solution)/shard_map/ppermute | solution.py:358
  27.1 4.3 %collective-permute-start.10 = (bf16[2,2,16,4096]{3,2,1,0:T(8,128)(2,1)S(1)}, bf16[2,2,16,4096]{3,2,1,0:T(8,128)(2,1)S(1)}, u32[]{:S(2)}, u32[]{:S(2)}) collective-permute-start(bf16[2,2,16,4096]{3,2,1,0:T(8,128)(2,1)S(1)} %get-tuple-element.27.refs_5_), channel_id=1, source_target_pairs={{0,1},{1,0},{2,3},{3,2},{4,5},{5,4},{6,7},{7,6},{8,9},{9,8},{10,11... | collective-permute-start | bytes 1572872 | tf_op jit(solution)/shard_map/ppermute | solution.py:358
  28.8 3.0 %copy-start.2 = (f32[4,4]{1,0:T(4,128)S(1)}, f32[4,4]{1,0:T(4,128)}, u32[]{:S(2)}) copy-start(f32[4,4]{1,0:T(4,128)} %weights_ref.1) | copy-start | bytes 196
  29.0 2.4 %collective-permute-start.11 = (bf16[2,2,16,4096]{3,2,1,0:T(8,128)(2,1)S(1)}, bf16[2,2,16,4096]{3,2,1,0:T(8,128)(2,1)S(1)}, u32[]{:S(2)}, u32[]{:S(2)}) collective-permute-start(bf16[2,2,16,4096]{3,2,1,0:T(8,128)(2,1)S(1)} %get-tuple-element.31.refs_6_), channel_id=1, source_target_pairs={{0,1},{1,0},{2,3},{3,2},{4,5},{5,4},{6,7},{7,6},{8,9},{9,8},{10,11... | collective-permute-start | bytes 1572872 | tf_op jit(solution)/shard_map/ppermute | solution.py:358
  29.5 2.3 %collective-permute-start.12 = (bf16[2,2,16,4096]{3,2,1,0:T(8,128)(2,1)S(1)}, bf16[2,2,16,4096]{3,2,1,0:T(8,128)(2,1)S(1)}, u32[]{:S(2)}, u32[]{:S(2)}) collective-permute-start(bf16[2,2,16,4096]{3,2,1,0:T(8,128)(2,1)S(1)} %get-tuple-element.32.refs_7_), channel_id=1, source_target_pairs={{0,1},{1,0},{2,3},{3,2},{4,5},{5,4},{6,7},{7,6},{8,9},{9,8},{10,11... | collective-permute-start | bytes 1572872 | tf_op jit(solution)/shard_map/ppermute | solution.py:358
  34.9 4.5 %collective-permute-start.13 = (bf16[128,256]{1,0:T(8,128)(2,1)S(1)}, bf16[128,256]{1,0:T(8,128)(2,1)S(1)}, u32[]{:S(2)}, u32[]{:S(2)}) collective-permute-start(bf16[128,256]{1,0:T(8,128)(2,1)S(1)} %get-tuple-element.35), channel_id=1, source_target_pairs={{0,8},{8,0},{16,24},{24,16},{1,9},{9,1},{17,25},{25,17},{2,10},{10... | collective-permute-start | bytes 196616 | tf_op jit(solution)/shard_map/ppermute | solution.py:361
  35.4 7.5 %collective-permute-start.14 = (bf16[128,256]{1,0:T(8,128)(2,1)S(1)}, bf16[128,256]{1,0:T(8,128)(2,1)S(1)}, u32[]{:S(2)}, u32[]{:S(2)}) collective-permute-start(bf16[128,256]{1,0:T(8,128)(2,1)S(1)} %get-tuple-element.34), channel_id=1, source_target_pairs={{0,16},{8,24},{16,0},{24,8},{1,17},{9,25},{17,1},{25,9},{2,18},{10... | collective-permute-start | bytes 196616 | tf_op jit(solution)/shard_map/ppermute | solution.py:361
  38.8 6.1 %collective-permute-start.15 = (bf16[128,256]{1,0:T(8,128)(2,1)S(1)}, bf16[128,256]{1,0:T(8,128)(2,1)S(1)}, u32[]{:S(2)}, u32[]{:S(2)}) collective-permute-start(bf16[128,256]{1,0:T(8,128)(2,1)S(1)} %get-tuple-element.33), channel_id=1, source_target_pairs={{0,24},{8,16},{16,8},{24,0},{1,25},{9,17},{17,9},{25,1},{2,26},{10... | collective-permute-start | bytes 196616 | tf_op jit(solution)/shard_map/ppermute | solution.py:361

commit v4 on v3

--- a/solution.py
+++ b/solution.py
@@ -308,7 +308,7 @@
             out_ref[slot, rows, move * LANES : (move + 1) * LANES] = wide.astype(out_ref.dtype)
 
 
-def screen_kernel(chi_ref, r1, r2, r3, factor_ref, out_ref, block_ref, done):
+def screen_kernel(chi_ref, r3, r2, r1, factor_ref, out_ref, block_ref, done):
     device = lax.axis_index("tensor")
     sources = [chi_ref[0], r1[...], r2[...], r3[...]]
     copies = []
@@ -418,7 +418,7 @@
         3,
     )(cosine_weights, lists, *mixed, *pieces, *[across(piece, 1) for piece in pieces])
 
-    received = [planes(chi[move], move) for move in range(1, 4)]
+    received = [planes(chi[move], move) for move in (3, 2, 1)]
     return kernel(
         screen_kernel,
         jax.ShapeDtypeStruct((1, local_count, 8 * LANES), jnp.float32),

time: 46.4 us -> 45.6 us (0.983)
  waiting for transfers between devices: 13.7 us -> 12.9 us
    ppermute x6, waiting for transfers between devices: 6.67 us -> 5.89 us  [planes(): return lax.ppermute(array, 'tm', [(i, i ^ move) for i in range(4)])]
where the time goes in v4:
time: 45.6 us; the launch traced here: 45.4 us
  starting transfers between devices  16.3 us (36%)
  Pallas kernels  15.8 us (35%)
  waiting for transfers between devices  12.9 us (28%)
    ppermute x6, starting transfers between devices, planes(): return lax.ppermute(array, 'tm', [(i, i ^ move) for i in range(4)])  8.92 us
    ppermute x10, starting transfers between devices, across(): return lax.ppermute(array, 'tensor', [(i, i ^ move) for i in range(8)])  7.38 us
    ppermute x10, waiting for transfers between devices, across(): return lax.ppermute(array, 'tensor', [(i, i ^ move) for i in range(8)])  7.06 us
    pallas_call x4, Pallas kernels, small_slice(): kernel(mix_kernel, [tiles, mark], [vmem] * 2, 0.1)(turned, each)  6.94 us
    ppermute x6, waiting for transfers between devices, planes(): return lax.ppermute(array, 'tm', [(i, i ^ move) for i in range(4)])  5.89 us
    pallas_call x1, Pallas kernels, small_slice(): kernel(gram_kernel, jax.ShapeDtypeStruct((4, local_count, columns), jnp.b...  3.08 us
    pallas_call x1, Pallas kernels, small_slice(): kernel(own_kernel, [message, message, block], [pl.BlockSpec(memory_space=...  2.13 us
    pallas_call x1, Pallas kernels, small_slice(): kernel(turn_kernel, tiles, [vmem], 1.2, [pltpu.VMEM((caps, local_count, p...  1.47 us
  transfers between devices with their start and end apart: 16, of which 7 were waited for; matrix products, arithmetic and copies ran while one was open for 0% of the time, Pallas kernels for 20%

profile of v4, /device:TPU:0, one launch (start us, length us, event | category | flops | bytes accessed | tf_op | source)
XLA Modules:
  0.0 45.4 jit_solution(16029000069132015743)
XLA Ops:
  0.0 2.1 %shard_map.65 = (bf16[16,8704]{1,0:T(8,128)(2,1)}, bf16[16,8704]{1,0:T(8,128)(2,1)}, bf16[64,128]{1,0:T(8,128)(2,1)}) custom-call(bf16[128,2,4096]{2,1,0:T(2,128)(2,1)} %rows_ref.3, bf16[1,1,64,64]{3,2,1,0:T(8,128)(2,1)} %occupied_ref.1, bf16[1,1,64,64]{3,2,1,0:T(8,128)(2,1)} %virtual_ref.1), custom_call_target="tpu_custom_call" | custom-call | flops 2000000000 | tf_op jit(solution)/shard_map/pallas_call | solution.py:370
  2.1 3.0 %collective-permute-start = (bf16[16,8704]{1,0:T(8,128)(2,1)}, bf16[16,8704]{1,0:T(8,128)(2,1)S(1)}, u32[]{:S(2)}, u32[]{:S(2)}) collective-permute-start(bf16[16,8704]{1,0:T(8,128)(2,1)} %get-tuple-element.20.low_ref), channel_id=1, source_target_pairs={{0,2},{1,3},{2,0},{3,1},{4,6},{5,7},{6,4},{7,5},{8,10},{9,11},{10,... | collective-permute-start | bytes 835592 | tf_op jit(solution)/shard_map/ppermute | solution.py:358
  5.1 1.5 %collective-permute-start.1 = (bf16[16,8704]{1,0:T(8,128)(2,1)}, bf16[16,8704]{1,0:T(8,128)(2,1)S(1)}, u32[]{:S(2)}, u32[]{:S(2)}) collective-permute-start(bf16[16,8704]{1,0:T(8,128)(2,1)} %get-tuple-element.21.high_ref), channel_id=1, source_target_pairs={{0,4},{1,5},{2,6},{3,7},{4,0},{5,1},{6,2},{7,3},{8,12},{9,13},{10,... | collective-permute-start | bytes 835592 | tf_op jit(solution)/shard_map/ppermute | solution.py:358
  6.7 1.5 %shard_map.64.refs_0_.turned_ref = bf16[2,2,64,4096]{3,2,1,0:T(8,128)(2,1)S(1)} custom-call(bf16[128,2,4096]{2,1,0:T(2,128)(2,1)S(1)} %copy-done.4), custom_call_target="tpu_custom_call" | custom-call | flops 1200000000 | tf_op jit(solution)/shard_map/pallas_call | solution.py:384
  8.2 0.2 shard_map.67.refs_2_.factor_ref
  8.5 5.2 %collective-permute-done.2.d_ref = bf16[64,128]{1,0:T(8,128)(2,1)S(1)} collective-permute-done((bf16[64,128]{1,0:T(8,128)(2,1)}, bf16[64,128]{1,0:T(8,128)(2,1)S(1)}, u32[]{:S(2)}, u32[]{:S(2)}) %collective-permute-start.2) | collective-permute-done | bytes 16416 | tf_op jit(solution)/shard_map/ppermute | solution.py:358
  13.7 0.1 collective-permute-done.1.y_ref
  13.9 0.1 shard_map.68
  13.9 1.3 %collective-permute-start.7 = (bf16[2,2,16,4096]{3,2,1,0:T(8,128)(2,1)S(1)}, bf16[2,2,16,4096]{3,2,1,0:T(8,128)(2,1)S(1)}, u32[]{:S(2)}, u32[]{:S(2)}) collective-permute-start(bf16[2,2,16,4096]{3,2,1,0:T(8,128)(2,1)S(1)} %get-tuple-element.22.after_ref.refs_4_), channel_id=1, source_target_pairs={{0,2},{1,3},{2,0},{3,1},{4,6},{5,7},{6,4},{7,5},{8,10},{9,11},{10,... | collective-permute-start | bytes 1572872 | tf_op jit(solution)/shard_map/ppermute | solution.py:358
  15.3 0.8 %collective-permute-start.8 = (bf16[2,2,16,4096]{3,2,1,0:T(8,128)(2,1)S(1)}, bf16[2,2,16,4096]{3,2,1,0:T(8,128)(2,1)S(1)}, u32[]{:S(2)}, u32[]{:S(2)}) collective-permute-start(bf16[2,2,16,4096]{3,2,1,0:T(8,128)(2,1)S(1)} %get-tuple-element.27.refs_5_), channel_id=1, source_target_pairs={{0,4},{1,5},{2,6},{3,7},{4,0},{5,1},{6,2},{7,3},{8,12},{9,13},{10,... | collective-permute-start | bytes 1572872 | tf_op jit(solution)/shard_map/ppermute | solution.py:358
  16.1 1.3 %collective-permute-done.3.core_ref = bf16[4,64,128]{2,1,0:T(8,128)(2,1)S(1)} collective-permute-done((bf16[4,64,128]{2,1,0:T(8,128)(2,1)S(1)}, bf16[4,64,128]{2,1,0:T(8,128)(2,1)S(1)}, u32[]{:S(2)}, u32[]{:S(2)}) %collective-permute-start.3) | collective-permute-done | bytes 65568 | tf_op jit(solution)/shard_map/ppermute | solution.py:358
  17.3 0.6 %shard_map.69.density_ref = bf16[2,2,64,128]{3,2,1,0:T(8,128)(2,1)S(1)} custom-call(s32[2,16]{1,0:T(2,128)S(1)} %bitcast.7, bf16[4,64,128]{2,1,0:T(8,128)(2,1)S(1)} %shard_map.66.refs_1_.near_ref, bf16[4,64,128]{2,1,0:T(8,128)(2,1)S(1)} %collective-permute-done.3.core_ref, bf16[2,2,16,4096]{3,2,1,0:T(8,128)(2,1)S(1)} %get-tuple-element.22.after_ref.refs_4_), custom_call_target="tpu_custom_call" | custom-call | flops 1000000000 | tf_op jit(solution)/shard_map/pallas_call | solution.py:396
  17.9 1.6 %collective-permute-start.4 = (bf16[2,2,64,128]{3,2,1,0:T(8,128)(2,1)S(1)}, bf16[2,2,64,128]{3,2,1,0:T(8,128)(2,1)S(1)}, u32[]{:S(2)}, u32[]{:S(2)}) collective-permute-start(bf16[2,2,64,128]{3,2,1,0:T(8,128)(2,1)S(1)} %shard_map.69.density_ref), channel_id=1, source_target_pairs={{0,8},{8,0},{16,24},{24,16},{1,9},{9,1},{17,25},{25,17},{2,10},{10... | collective-permute-start | bytes 196616 | tf_op jit(solution)/shard_map/ppermute | solution.py:361
  19.5 2.6 %collective-permute-start.5 = (bf16[2,2,64,128]{3,2,1,0:T(8,128)(2,1)S(1)}, bf16[2,2,64,128]{3,2,1,0:T(8,128)(2,1)S(1)}, u32[]{:S(2)}, u32[]{:S(2)}) collective-permute-start(bf16[2,2,64,128]{3,2,1,0:T(8,128)(2,1)S(1)} %shard_map.69.density_ref), channel_id=1, source_target_pairs={{0,16},{8,24},{16,0},{24,8},{1,17},{9,25},{17,1},{25,9},{2,18},{10... | collective-permute-start | bytes 196616 | tf_op jit(solution)/shard_map/ppermute | solution.py:361
  22.1 0.2 collective-permute-start.6
  22.4 1.7 %shard_map.70 = (bf16[2,2,64,4096]{3,2,1,0:T(8,128)(2,1)S(1)}, f32[8,128]{1,0:T(8,128)S(1)}) custom-call(bf16[2,2,64,4096]{3,2,1,0:T(8,128)(2,1)S(1)} %shard_map.64.refs_0_.turned_ref, bf16[2,2,64,128]{3,2,1,0:T(8,128)(2,1)S(1)} %shard_map.69.density_ref), custom_call_target="tpu_custom_call" | custom-call | flops 100000000 | tf_op jit(solution)/shard_map/pallas_call | solution.py:407
  24.1 0.1 collective-permute-start.9
  24.2 1.7 %shard_map.71 = (bf16[2,2,64,4096]{3,2,1,0:T(8,128)(2,1)S(1)}, f32[8,128]{1,0:T(8,128)S(1)}) custom-call(bf16[2,2,64,4096]{3,2,1,0:T(8,128)(2,1)S(1)} %shard_map.64.refs_0_.turned_ref, bf16[2,2,64,128]{3,2,1,0:T(8,128)(2,1)S(1)} %collective-permute-done.4.density_ref), custom_call_target="tpu_custom_call" | custom-call | flops 100000000 | tf_op jit(solution)/shard_map/pallas_call | solution.py:407
  25.9 1.2 %collective-permute-done.5.density_ref = bf16[2,2,64,128]{3,2,1,0:T(8,128)(2,1)S(1)} collective-permute-done((bf16[2,2,64,128]{3,2,1,0:T(8,128)(2,1)S(1)}, bf16[2,2,64,128]{3,2,1,0:T(8,128)(2,1)S(1)}, u32[]{:S(2)}, u32[]{:S(2)}) %collective-permute-start.5) | collective-permute-done | bytes 65568 | tf_op jit(solution)/shard_map/ppermute | solution.py:361
  27.1 1.7 %shard_map.72 = (bf16[2,2,64,4096]{3,2,1,0:T(8,128)(2,1)S(1)}, f32[8,128]{1,0:T(8,128)S(1)}) custom-call(bf16[2,2,64,4096]{3,2,1,0:T(8,128)(2,1)S(1)} %shard_map.64.refs_0_.turned_ref, bf16[2,2,64,128]{3,2,1,0:T(8,128)(2,1)S(1)} %collective-permute-done.5.density_ref), custom_call_target="tpu_custom_call" | custom-call | flops 100000000 | tf_op jit(solution)/shard_map/pallas_call | solution.py:407
  28.9 0.1 shard_map.74
  29.0 0.6 %collective-permute-start.11 = (bf16[2,2,16,4096]{3,2,1,0:T(8,128)(2,1)S(1)}, bf16[2,2,16,4096]{3,2,1,0:T(8,128)(2,1)S(1)}, u32[]{:S(2)}, u32[]{:S(2)}) collective-permute-start(bf16[2,2,16,4096]{3,2,1,0:T(8,128)(2,1)S(1)} %get-tuple-element.31.refs_6_), channel_id=1, source_target_pairs={{0,1},{1,0},{2,3},{3,2},{4,5},{5,4},{6,7},{7,6},{8,9},{9,8},{10,11... | collective-permute-start | bytes 1572872 | tf_op jit(solution)/shard_map/ppermute | solution.py:358
  29.5 0.1 collective-permute-start.12
  29.6 1.7 %shard_map.73 = (bf16[2,2,64,4096]{3,2,1,0:T(8,128)(2,1)S(1)}, f32[8,128]{1,0:T(8,128)}) custom-call(bf16[2,2,64,4096]{3,2,1,0:T(8,128)(2,1)S(1)} %shard_map.64.refs_0_.turned_ref, bf16[2,2,64,128]{3,2,1,0:T(8,128)(2,1)S(1)} %collective-permute-done.6.density_ref.refs_3_), custom_call_target="tpu_custom_call" | custom-call | flops 100000000 | tf_op jit(solution)/shard_map/pallas_call | solution.py:407
  31.4 0.4 collective-permute-done.12.refs_11_
  31.8 3.1 %shard_map.75.chi_ref = bf16[4,128,256]{2,1,0:T(8,128)(2,1)S(1)} custom-call(f32[4,4]{1,0:T(4,128)S(1)} %copy-done.2, s32[2,16]{1,0:T(2,128)S(1)} %bitcast.8, bf16[2,2,64,4096]{3,2,1,0:T(8,128)(2,1)S(1)} %get-tuple-element.23.refs_0_, bf16[2,2,64,4096]{3,2,1,0:T(8,128)(2,1)S(1)} %get-tuple-element.24.refs_1_, ...), custom_call_target="tpu_custom_call" | custom-call | flops 3000000000 | tf_op jit(solution)/shard_map/pallas_call | solution.py:414
  34.9 3.3 %collective-permute-start.13 = (bf16[128,256]{1,0:T(8,128)(2,1)S(1)}, bf16[128,256]{1,0:T(8,128)(2,1)S(1)}, u32[]{:S(2)}, u32[]{:S(2)}) collective-permute-start(bf16[128,256]{1,0:T(8,128)(2,1)S(1)} %get-tuple-element.35), channel_id=1, source_target_pairs={{0,24},{8,16},{16,8},{24,0},{1,25},{9,17},{17,9},{25,1},{2,26},{10... | collective-permute-start | bytes 196616 | tf_op jit(solution)/shard_map/ppermute | solution.py:361
  38.2 1.2 %collective-permute-start.15 = (bf16[128,256]{1,0:T(8,128)(2,1)S(1)}, bf16[128,256]{1,0:T(8,128)(2,1)S(1)}, u32[]{:S(2)}, u32[]{:S(2)}) collective-permute-start(bf16[128,256]{1,0:T(8,128)(2,1)S(1)} %get-tuple-element.33), channel_id=1, source_target_pairs={{0,8},{8,0},{16,24},{24,16},{1,9},{9,1},{17,25},{25,17},{2,10},{10... | collective-permute-start | bytes 196616 | tf_op jit(solution)/shard_map/ppermute | solution.py:361
  39.4 2.3 %collective-permute-done.13.r3 = bf16[128,256]{1,0:T(8,128)(2,1)S(1)} collective-permute-done((bf16[128,256]{1,0:T(8,128)(2,1)S(1)}, bf16[128,256]{1,0:T(8,128)(2,1)S(1)}, u32[]{:S(2)}, u32[]{:S(2)}) %collective-permute-start.13) | collective-permute-done | bytes 65568 | tf_op jit(solution)/shard_map/ppermute | solution.py:361
  41.7 2.4 %collective-permute-done.14.r2 = bf16[128,256]{1,0:T(8,128)(2,1)S(1)} collective-permute-done((bf16[128,256]{1,0:T(8,128)(2,1)S(1)}, bf16[128,256]{1,0:T(8,128)(2,1)S(1)}, u32[]{:S(2)}, u32[]{:S(2)}) %collective-permute-start.14) | collective-permute-done | bytes 65568 | tf_op jit(solution)/shard_map/ppermute | solution.py:361
  44.1 0.0 collective-permute-done.15.r1
  44.1 1.2 %shard_map.76 = f32[1,128,1024]{2,1,0:T(8,128)} custom-call(bf16[4,128,256]{2,1,0:T(8,128)(2,1)S(1)} %shard_map.75.chi_ref, bf16[128,256]{1,0:T(8,128)(2,1)S(1)} %collective-permute-done.13.r3, bf16[128,256]{1,0:T(8,128)(2,1)S(1)} %collective-permute-done.14.r2, bf16[128,256]{1,0:T(8,128)(2,1)S(1)} %collective-permute-done.15.r1, ...), custom_call_target="tpu_custom_call" | custom-call | flops 1000000000 | tf_op jit(solution)/shard_map/pallas_call | solution.py:422
  (28 shorter events, 0.1 us)
Async XLA Ops:
  0.0 6.7 %copy-start.4 = (bf16[128,2,4096]{2,1,0:T(2,128)(2,1)S(1)}, bf16[128,2,4096]{2,1,0:T(2,128)(2,1)}, u32[]{:S(2)}) copy-start(bf16[128,2,4096]{2,1,0:T(2,128)(2,1)} %rows_ref.3) | copy-start | bytes 6291460
  2.1 11.5 %collective-permute-start = (bf16[16,8704]{1,0:T(8,128)(2,1)}, bf16[16,8704]{1,0:T(8,128)(2,1)S(1)}, u32[]{:S(2)}, u32[]{:S(2)}) collective-permute-start(bf16[16,8704]{1,0:T(8,128)(2,1)} %get-tuple-element.20.low_ref), channel_id=1, source_target_pairs={{0,2},{1,3},{2,0},{3,1},{4,6},{5,7},{6,4},{7,5},{8,10},{9,11},{10,... | collective-permute-start | bytes 835592 | tf_op jit(solution)/shard_map/ppermute | solution.py:358
  5.1 8.7 %collective-permute-start.1 = (bf16[16,8704]{1,0:T(8,128)(2,1)}, bf16[16,8704]{1,0:T(8,128)(2,1)S(1)}, u32[]{:S(2)}, u32[]{:S(2)}) collective-permute-start(bf16[16,8704]{1,0:T(8,128)(2,1)} %get-tuple-element.21.high_ref), channel_id=1, source_target_pairs={{0,4},{1,5},{2,6},{3,7},{4,0},{5,1},{6,2},{7,3},{8,12},{9,13},{10,... | collective-permute-start | bytes 835592 | tf_op jit(solution)/shard_map/ppermute | solution.py:358
  6.7 1.5 %copy-start.5 = (f32[16,64,64]{2,1,0:T(8,128)S(1)}, f32[16,64,64]{2,1,0:T(8,128)}, u32[]{:S(2)}) copy-start(f32[16,64,64]{2,1,0:T(8,128)} %factor_ref.1) | copy-start | bytes 786436
  6.7 7.0 %collective-permute-start.2 = (bf16[64,128]{1,0:T(8,128)(2,1)}, bf16[64,128]{1,0:T(8,128)(2,1)S(1)}, u32[]{:S(2)}, u32[]{:S(2)}) collective-permute-start(bf16[64,128]{1,0:T(8,128)(2,1)} %get-tuple-element.19.density_ref), channel_id=1, source_target_pairs={{0,6},{1,7},{2,4},{3,5},{4,2},{5,3},{6,0},{7,1},{8,14},{9,15},{10,... | collective-permute-start | bytes 49160 | tf_op jit(solution)/shard_map/ppermute | solution.py:358
  8.2 5.6 %copy-start.6 = (bf16[64,128]{1,0:T(8,128)(2,1)S(1)}, bf16[64,128]{1,0:T(8,128)(2,1)}, u32[]{:S(2)}) copy-start(bf16[64,128]{1,0:T(8,128)(2,1)} %get-tuple-element.19.density_ref) | copy-start | bytes 49156
  8.2 5.7 %copy-start = (bf16[16,8704]{1,0:T(8,128)(2,1)S(1)}, bf16[16,8704]{1,0:T(8,128)(2,1)}, u32[]{:S(2)}) copy-start(bf16[16,8704]{1,0:T(8,128)(2,1)} %get-tuple-element.20.low_ref) | copy-start | bytes 835588
  8.2 5.7 %copy-start.1 = (bf16[16,8704]{1,0:T(8,128)(2,1)S(1)}, bf16[16,8704]{1,0:T(8,128)(2,1)}, u32[]{:S(2)}) copy-start(bf16[16,8704]{1,0:T(8,128)(2,1)} %get-tuple-element.21.high_ref) | copy-start | bytes 835588
  13.9 3.5 %copy-start.3 = (s32[16,2]{0,1:T(2,128)S(1)}, s32[16,2]{0,1:T(2,128)}, u32[]{:S(2)}) copy-start(s32[16,2]{0,1:T(2,128)} %param.7) | copy-start | bytes 388
  13.9 14.9 %collective-permute-start.7 = (bf16[2,2,16,4096]{3,2,1,0:T(8,128)(2,1)S(1)}, bf16[2,2,16,4096]{3,2,1,0:T(8,128)(2,1)S(1)}, u32[]{:S(2)}, u32[]{:S(2)}) collective-permute-start(bf16[2,2,16,4096]{3,2,1,0:T(8,128)(2,1)S(1)} %get-tuple-element.22.after_ref.refs_4_), channel_id=1, source_target_pairs={{0,2},{1,3},{2,0},{3,1},{4,6},{5,7},{6,4},{7,5},{8,10},{9,11},{10,... | collective-permute-start | bytes 1572872 | tf_op jit(solution)/shard_map/ppermute | solution.py:358
  15.3 13.6 %collective-permute-start.8 = (bf16[2,2,16,4096]{3,2,1,0:T(8,128)(2,1)S(1)}, bf16[2,2,16,4096]{3,2,1,0:T(8,128)(2,1)S(1)}, u32[]{:S(2)}, u32[]{:S(2)}) collective-permute-start(bf16[2,2,16,4096]{3,2,1,0:T(8,128)(2,1)S(1)} %get-tuple-element.27.refs_5_), channel_id=1, source_target_pairs={{0,4},{1,5},{2,6},{3,7},{4,0},{5,1},{6,2},{7,3},{8,12},{9,13},{10,... | collective-permute-start | bytes 1572872 | tf_op jit(solution)/shard_map/ppermute | solution.py:358
  16.1 1.3 %collective-permute-start.3 = (bf16[4,64,128]{2,1,0:T(8,128)(2,1)S(1)}, bf16[4,64,128]{2,1,0:T(8,128)(2,1)S(1)}, u32[]{:S(2)}, u32[]{:S(2)}) collective-permute-start(bf16[4,64,128]{2,1,0:T(8,128)(2,1)S(1)} %shard_map.66.refs_1_.near_ref), channel_id=1, source_target_pairs={{0,1},{1,0},{2,3},{3,2},{4,5},{5,4},{6,7},{7,6},{8,9},{9,8},{10,11... | collective-permute-start | bytes 196616 | tf_op jit(solution)/shard_map/ppermute | solution.py:358
  17.9 6.2 %collective-permute-start.4 = (bf16[2,2,64,128]{3,2,1,0:T(8,128)(2,1)S(1)}, bf16[2,2,64,128]{3,2,1,0:T(8,128)(2,1)S(1)}, u32[]{:S(2)}, u32[]{:S(2)}) collective-permute-start(bf16[2,2,64,128]{3,2,1,0:T(8,128)(2,1)S(1)} %shard_map.69.density_ref), channel_id=1, source_target_pairs={{0,8},{8,0},{16,24},{24,16},{1,9},{9,1},{17,25},{25,17},{2,10},{10... | collective-permute-start | bytes 196616 | tf_op jit(solution)/shard_map/ppermute | solution.py:361
  19.5 7.5 %collective-permute-start.5 = (bf16[2,2,64,128]{3,2,1,0:T(8,128)(2,1)S(1)}, bf16[2,2,64,128]{3,2,1,0:T(8,128)(2,1)S(1)}, u32[]{:S(2)}, u32[]{:S(2)}) collective-permute-start(bf16[2,2,64,128]{3,2,1,0:T(8,128)(2,1)S(1)} %shard_map.69.density_ref), channel_id=1, source_target_pairs={{0,16},{8,24},{16,0},{24,8},{1,17},{9,25},{17,1},{25,9},{2,18},{10... | collective-permute-start | bytes 196616 | tf_op jit(solution)/shard_map/ppermute | solution.py:361
  22.1 6.7 %collective-permute-start.6 = (bf16[2,2,64,128]{3,2,1,0:T(8,128)(2,1)S(1)}, bf16[2,2,64,128]{3,2,1,0:T(8,128)(2,1)S(1)}, u32[]{:S(2)}, u32[]{:S(2)}) collective-permute-start(bf16[2,2,64,128]{3,2,1,0:T(8,128)(2,1)S(1)} %shard_map.69.density_ref), channel_id=1, source_target_pairs={{0,24},{8,16},{16,8},{24,0},{1,25},{9,17},{17,9},{25,1},{2,26},{10... | collective-permute-start | bytes 196616 | tf_op jit(solution)/shard_map/ppermute | solution.py:361
  24.1 7.2 %collective-permute-start.9 = (bf16[2,2,16,4096]{3,2,1,0:T(8,128)(2,1)S(1)}, bf16[2,2,16,4096]{3,2,1,0:T(8,128)(2,1)S(1)}, u32[]{:S(2)}, u32[]{:S(2)}) collective-permute-start(bf16[2,2,16,4096]{3,2,1,0:T(8,128)(2,1)S(1)} %get-tuple-element.22.after_ref.refs_4_), channel_id=1, source_target_pairs={{0,1},{1,0},{2,3},{3,2},{4,5},{5,4},{6,7},{7,6},{8,9},{9,8},{10,11... | collective-permute-start | bytes 1572872 | tf_op jit(solution)/shard_map/ppermute | solution.py:358
  27.1 4.3 %collective-permute-start.10 = (bf16[2,2,16,4096]{3,2,1,0:T(8,128)(2,1)S(1)}, bf16[2,2,16,4096]{3,2,1,0:T(8,128)(2,1)S(1)}, u32[]{:S(2)}, u32[]{:S(2)}) collective-permute-start(bf16[2,2,16,4096]{3,2,1,0:T(8,128)(2,1)S(1)} %get-tuple-element.27.refs_5_), channel_id=1, source_target_pairs={{0,1},{1,0},{2,3},{3,2},{4,5},{5,4},{6,7},{7,6},{8,9},{9,8},{10,11... | collective-permute-start | bytes 1572872 | tf_op jit(solution)/shard_map/ppermute | solution.py:358
  28.8 3.0 %copy-start.2 = (f32[4,4]{1,0:T(4,128)S(1)}, f32[4,4]{1,0:T(4,128)}, u32[]{:S(2)}) copy-start(f32[4,4]{1,0:T(4,128)} %weights_ref.1) | copy-start | bytes 196
  29.0 2.4 %collective-permute-start.11 = (bf16[2,2,16,4096]{3,2,1,0:T(8,128)(2,1)S(1)}, bf16[2,2,16,4096]{3,2,1,0:T(8,128)(2,1)S(1)}, u32[]{:S(2)}, u32[]{:S(2)}) collective-permute-start(bf16[2,2,16,4096]{3,2,1,0:T(8,128)(2,1)S(1)} %get-tuple-element.31.refs_6_), channel_id=1, source_target_pairs={{0,1},{1,0},{2,3},{3,2},{4,5},{5,4},{6,7},{7,6},{8,9},{9,8},{10,11... | collective-permute-start | bytes 1572872 | tf_op jit(solution)/shard_map/ppermute | solution.py:358
  29.5 2.3 %collective-permute-start.12 = (bf16[2,2,16,4096]{3,2,1,0:T(8,128)(2,1)S(1)}, bf16[2,2,16,4096]{3,2,1,0:T(8,128)(2,1)S(1)}, u32[]{:S(2)}, u32[]{:S(2)}) collective-permute-start(bf16[2,2,16,4096]{3,2,1,0:T(8,128)(2,1)S(1)} %get-tuple-element.32.refs_7_), channel_id=1, source_target_pairs={{0,1},{1,0},{2,3},{3,2},{4,5},{5,4},{6,7},{7,6},{8,9},{9,8},{10,11... | collective-permute-start | bytes 1572872 | tf_op jit(solution)/shard_map/ppermute | solution.py:358
  34.9 6.8 %collective-permute-start.13 = (bf16[128,256]{1,0:T(8,128)(2,1)S(1)}, bf16[128,256]{1,0:T(8,128)(2,1)S(1)}, u32[]{:S(2)}, u32[]{:S(2)}) collective-permute-start(bf16[128,256]{1,0:T(8,128)(2,1)S(1)} %get-tuple-element.35), channel_id=1, source_target_pairs={{0,24},{8,16},{16,8},{24,0},{1,25},{9,17},{17,9},{25,1},{2,26},{10... | collective-permute-start | bytes 196616 | tf_op jit(solution)/shard_map/ppermute | solution.py:361
  38.2 5.9 %collective-permute-start.14 = (bf16[128,256]{1,0:T(8,128)(2,1)S(1)}, bf16[128,256]{1,0:T(8,128)(2,1)S(1)}, u32[]{:S(2)}, u32[]{:S(2)}) collective-permute-start(bf16[128,256]{1,0:T(8,128)(2,1)S(1)} %get-tuple-element.34), channel_id=1, source_target_pairs={{0,16},{8,24},{16,0},{24,8},{1,17},{9,25},{17,1},{25,9},{2,18},{10... | collective-permute-start | bytes 196616 | tf_op jit(solution)/shard_map/ppermute | solution.py:361
  38.2 5.9 %collective-permute-start.15 = (bf16[128,256]{1,0:T(8,128)(2,1)S(1)}, bf16[128,256]{1,0:T(8,128)(2,1)S(1)}, u32[]{:S(2)}, u32[]{:S(2)}) collective-permute-start(bf16[128,256]{1,0:T(8,128)(2,1)S(1)} %get-tuple-element.33), channel_id=1, source_target_pairs={{0,8},{8,0},{16,24},{24,16},{1,9},{9,1},{17,25},{25,17},{2,10},{10... | collective-permute-start | bytes 196616 | tf_op jit(solution)/shard_map/ppermute | solution.py:361

commit v5 on v4

--- a/solution.py
+++ b/solution.py
@@ -377,7 +377,7 @@
             pltpu.VMEM((2, HALF, HALF), jnp.bfloat16),
             pltpu.SemaphoreType.DMA((3,)),
         ],
-        room=61,
+        room=62,
     )(integrals, occ_density, virt_density)
     x_low = across(low, 2)
     y_high = across(high, 4)

time: 45.6 us -> 45.4 us (level)
  waiting for transfers between devices: 12.9 us -> 11.3 us
  local copies, waits for them, and re-layouts: 0.05 us -> 1.64 us
    ppermute x10, waiting for transfers between devices: 7.06 us -> 5.47 us  [across(): return lax.ppermute(array, 'tensor', [(i, i ^ move) for i in range(8)])]
    unnamed x14, local copies, waits for them, and re-layouts: 0.03 us -> 1.62 us
  transfers between devices with their start and end apart: 16 -> 16, of which waited for: 7 -> 7; matrix products, arithmetic and copies ran while one was open for 0% -> 0% of each run, Pallas kernels for 20% -> 21%
where the time goes in v5:
time: 45.4 us; the launch traced here: 45.2 us
  starting transfers between devices  16.3 us (36%)
  Pallas kernels  15.7 us (35%)
  waiting for transfers between devices  11.3 us (25%)
  local copies, waits for them, and re-layouts  1.64 us (4%)
    ppermute x6, starting transfers between devices, planes(): return lax.ppermute(array, 'tm', [(i, i ^ move) for i in range(4)])  8.92 us
    ppermute x10, starting transfers between devices, across(): return lax.ppermute(array, 'tensor', [(i, i ^ move) for i in range(8)])  7.38 us
    pallas_call x4, Pallas kernels, small_slice(): kernel(mix_kernel, [tiles, mark], [vmem] * 2, 0.1)(turned, each)  6.95 us
    ppermute x6, waiting for transfers between devices, planes(): return lax.ppermute(array, 'tm', [(i, i ^ move) for i in range(4)])  5.84 us
    ppermute x10, waiting for transfers between devices, across(): return lax.ppermute(array, 'tensor', [(i, i ^ move) for i in range(8)])  5.47 us
    pallas_call x1, Pallas kernels, small_slice(): kernel(gram_kernel, jax.ShapeDtypeStruct((4, local_count, columns), jnp.b...  3.08 us
    pallas_call x1, Pallas kernels, small_slice(): kernel(own_kernel, [message, message, block], [pl.BlockSpec(memory_space=...  2.02 us
    unnamed x14, local copies, waits for them, and re-layouts  1.62 us
  transfers between devices with their start and end apart: 16, of which 7 were waited for; matrix products, arithmetic and copies ran while one was open for 0% of the time, Pallas kernels for 21%

profile of v5, /device:TPU:0, one launch (start us, length us, event | category | flops | bytes accessed | tf_op | source)
XLA Modules:
  0.0 45.2 jit_solution(16786519334238307823)
XLA Ops:
  0.0 2.0 %shard_map.65 = (bf16[16,8704]{1,0:T(8,128)(2,1)}, bf16[16,8704]{1,0:T(8,128)(2,1)}, bf16[64,128]{1,0:T(8,128)(2,1)}) custom-call(bf16[128,2,4096]{2,1,0:T(2,128)(2,1)} %rows_ref.3, bf16[1,1,64,64]{3,2,1,0:T(8,128)(2,1)} %occupied_ref.1, bf16[1,1,64,64]{3,2,1,0:T(8,128)(2,1)} %virtual_ref.1), custom_call_target="tpu_custom_call" | custom-call | flops 2000000000 | tf_op jit(solution)/shard_map/pallas_call | solution.py:370
  2.0 3.0 %collective-permute-start = (bf16[16,8704]{1,0:T(8,128)(2,1)}, bf16[16,8704]{1,0:T(8,128)(2,1)S(1)}, u32[]{:S(2)}, u32[]{:S(2)}) collective-permute-start(bf16[16,8704]{1,0:T(8,128)(2,1)} %get-tuple-element.20.low_ref), channel_id=1, source_target_pairs={{0,2},{1,3},{2,0},{3,1},{4,6},{5,7},{6,4},{7,5},{8,10},{9,11},{10,... | collective-permute-start | bytes 835592 | tf_op jit(solution)/shard_map/ppermute | solution.py:358
  5.0 1.5 %collective-permute-start.1 = (bf16[16,8704]{1,0:T(8,128)(2,1)}, bf16[16,8704]{1,0:T(8,128)(2,1)S(1)}, u32[]{:S(2)}, u32[]{:S(2)}) collective-permute-start(bf16[16,8704]{1,0:T(8,128)(2,1)} %get-tuple-element.21.high_ref), channel_id=1, source_target_pairs={{0,4},{1,5},{2,6},{3,7},{4,0},{5,1},{6,2},{7,3},{8,12},{9,13},{10,... | collective-permute-start | bytes 835592 | tf_op jit(solution)/shard_map/ppermute | solution.py:358
  6.6 1.6 %copy-done.4 = bf16[128,2,4096]{2,1,0:T(2,128)(2,1)S(1)} copy-done((bf16[128,2,4096]{2,1,0:T(2,128)(2,1)S(1)}, bf16[128,2,4096]{2,1,0:T(2,128)(2,1)}, u32[]{:S(2)}) %copy-start.4) | copy-done | bytes 2097176
  8.2 1.5 %shard_map.64.refs_0_.turned_ref = bf16[2,2,64,4096]{3,2,1,0:T(8,128)(2,1)S(1)} custom-call(bf16[128,2,4096]{2,1,0:T(2,128)(2,1)S(1)} %copy-done.4), custom_call_target="tpu_custom_call" | custom-call | flops 1200000000 | tf_op jit(solution)/shard_map/pallas_call | solution.py:384
  9.7 0.2 shard_map.67.refs_2_.factor_ref
  9.9 3.6 %collective-permute-done.2.d_ref = bf16[64,128]{1,0:T(8,128)(2,1)S(1)} collective-permute-done((bf16[64,128]{1,0:T(8,128)(2,1)}, bf16[64,128]{1,0:T(8,128)(2,1)S(1)}, u32[]{:S(2)}, u32[]{:S(2)}) %collective-permute-start.2) | collective-permute-done | bytes 16416 | tf_op jit(solution)/shard_map/ppermute | solution.py:358
  13.6 0.1 collective-permute-done.1.y_ref
  13.8 0.1 shard_map.68
  13.8 1.3 %collective-permute-start.7 = (bf16[2,2,16,4096]{3,2,1,0:T(8,128)(2,1)S(1)}, bf16[2,2,16,4096]{3,2,1,0:T(8,128)(2,1)S(1)}, u32[]{:S(2)}, u32[]{:S(2)}) collective-permute-start(bf16[2,2,16,4096]{3,2,1,0:T(8,128)(2,1)S(1)} %get-tuple-element.22.after_ref.refs_4_), channel_id=1, source_target_pairs={{0,2},{1,3},{2,0},{3,1},{4,6},{5,7},{6,4},{7,5},{8,10},{9,11},{10,... | collective-permute-start | bytes 1572872 | tf_op jit(solution)/shard_map/ppermute | solution.py:358
  15.2 0.8 %collective-permute-start.8 = (bf16[2,2,16,4096]{3,2,1,0:T(8,128)(2,1)S(1)}, bf16[2,2,16,4096]{3,2,1,0:T(8,128)(2,1)S(1)}, u32[]{:S(2)}, u32[]{:S(2)}) collective-permute-start(bf16[2,2,16,4096]{3,2,1,0:T(8,128)(2,1)S(1)} %get-tuple-element.27.refs_5_), channel_id=1, source_target_pairs={{0,4},{1,5},{2,6},{3,7},{4,0},{5,1},{6,2},{7,3},{8,12},{9,13},{10,... | collective-permute-start | bytes 1572872 | tf_op jit(solution)/shard_map/ppermute | solution.py:358
  16.0 1.3 %collective-permute-done.3.core_ref = bf16[4,64,128]{2,1,0:T(8,128)(2,1)S(1)} collective-permute-done((bf16[4,64,128]{2,1,0:T(8,128)(2,1)S(1)}, bf16[4,64,128]{2,1,0:T(8,128)(2,1)S(1)}, u32[]{:S(2)}, u32[]{:S(2)}) %collective-permute-start.3) | collective-permute-done | bytes 65568 | tf_op jit(solution)/shard_map/ppermute | solution.py:358
  17.2 0.6 %shard_map.69.density_ref = bf16[2,2,64,128]{3,2,1,0:T(8,128)(2,1)S(1)} custom-call(s32[2,16]{1,0:T(2,128)S(1)} %bitcast.7, bf16[4,64,128]{2,1,0:T(8,128)(2,1)S(1)} %shard_map.66.refs_1_.near_ref, bf16[4,64,128]{2,1,0:T(8,128)(2,1)S(1)} %collective-permute-done.3.core_ref, bf16[2,2,16,4096]{3,2,1,0:T(8,128)(2,1)S(1)} %get-tuple-element.22.after_ref.refs_4_), custom_call_target="tpu_custom_call" | custom-call | flops 1000000000 | tf_op jit(solution)/shard_map/pallas_call | solution.py:396
  17.8 1.6 %collective-permute-start.4 = (bf16[2,2,64,128]{3,2,1,0:T(8,128)(2,1)S(1)}, bf16[2,2,64,128]{3,2,1,0:T(8,128)(2,1)S(1)}, u32[]{:S(2)}, u32[]{:S(2)}) collective-permute-start(bf16[2,2,64,128]{3,2,1,0:T(8,128)(2,1)S(1)} %shard_map.69.density_ref), channel_id=1, source_target_pairs={{0,8},{8,0},{16,24},{24,16},{1,9},{9,1},{17,25},{25,17},{2,10},{10... | collective-permute-start | bytes 196616 | tf_op jit(solution)/shard_map/ppermute | solution.py:361
  19.4 2.6 %collective-permute-start.5 = (bf16[2,2,64,128]{3,2,1,0:T(8,128)(2,1)S(1)}, bf16[2,2,64,128]{3,2,1,0:T(8,128)(2,1)S(1)}, u32[]{:S(2)}, u32[]{:S(2)}) collective-permute-start(bf16[2,2,64,128]{3,2,1,0:T(8,128)(2,1)S(1)} %shard_map.69.density_ref), channel_id=1, source_target_pairs={{0,16},{8,24},{16,0},{24,8},{1,17},{9,25},{17,1},{25,9},{2,18},{10... | collective-permute-start | bytes 196616 | tf_op jit(solution)/shard_map/ppermute | solution.py:361
  22.0 0.3 collective-permute-start.6
  22.3 1.7 %shard_map.70 = (bf16[2,2,64,4096]{3,2,1,0:T(8,128)(2,1)S(1)}, f32[8,128]{1,0:T(8,128)S(1)}) custom-call(bf16[2,2,64,4096]{3,2,1,0:T(8,128)(2,1)S(1)} %shard_map.64.refs_0_.turned_ref, bf16[2,2,64,128]{3,2,1,0:T(8,128)(2,1)S(1)} %shard_map.69.density_ref), custom_call_target="tpu_custom_call" | custom-call | flops 100000000 | tf_op jit(solution)/shard_map/pallas_call | solution.py:407
  24.0 0.1 collective-permute-start.9
  24.1 1.7 %shard_map.71 = (bf16[2,2,64,4096]{3,2,1,0:T(8,128)(2,1)S(1)}, f32[8,128]{1,0:T(8,128)S(1)}) custom-call(bf16[2,2,64,4096]{3,2,1,0:T(8,128)(2,1)S(1)} %shard_map.64.refs_0_.turned_ref, bf16[2,2,64,128]{3,2,1,0:T(8,128)(2,1)S(1)} %collective-permute-done.4.density_ref), custom_call_target="tpu_custom_call" | custom-call | flops 100000000 | tf_op jit(solution)/shard_map/pallas_call | solution.py:407
  25.8 1.1 %collective-permute-done.5.density_ref = bf16[2,2,64,128]{3,2,1,0:T(8,128)(2,1)S(1)} collective-permute-done((bf16[2,2,64,128]{3,2,1,0:T(8,128)(2,1)S(1)}, bf16[2,2,64,128]{3,2,1,0:T(8,128)(2,1)S(1)}, u32[]{:S(2)}, u32[]{:S(2)}) %collective-permute-start.5) | collective-permute-done | bytes 65568 | tf_op jit(solution)/shard_map/ppermute | solution.py:361
  26.9 1.7 %shard_map.72 = (bf16[2,2,64,4096]{3,2,1,0:T(8,128)(2,1)S(1)}, f32[8,128]{1,0:T(8,128)S(1)}) custom-call(bf16[2,2,64,4096]{3,2,1,0:T(8,128)(2,1)S(1)} %shard_map.64.refs_0_.turned_ref, bf16[2,2,64,128]{3,2,1,0:T(8,128)(2,1)S(1)} %collective-permute-done.5.density_ref), custom_call_target="tpu_custom_call" | custom-call | flops 100000000 | tf_op jit(solution)/shard_map/pallas_call | solution.py:407
  28.7 0.1 shard_map.74
  28.8 0.6 %collective-permute-start.11 = (bf16[2,2,16,4096]{3,2,1,0:T(8,128)(2,1)S(1)}, bf16[2,2,16,4096]{3,2,1,0:T(8,128)(2,1)S(1)}, u32[]{:S(2)}, u32[]{:S(2)}) collective-permute-start(bf16[2,2,16,4096]{3,2,1,0:T(8,128)(2,1)S(1)} %get-tuple-element.31.refs_6_), channel_id=1, source_target_pairs={{0,1},{1,0},{2,3},{3,2},{4,5},{5,4},{6,7},{7,6},{8,9},{9,8},{10,11... | collective-permute-start | bytes 1572872 | tf_op jit(solution)/shard_map/ppermute | solution.py:358
  29.4 0.1 collective-permute-start.12
  29.5 1.7 %shard_map.73 = (bf16[2,2,64,4096]{3,2,1,0:T(8,128)(2,1)S(1)}, f32[8,128]{1,0:T(8,128)}) custom-call(bf16[2,2,64,4096]{3,2,1,0:T(8,128)(2,1)S(1)} %shard_map.64.refs_0_.turned_ref, bf16[2,2,64,128]{3,2,1,0:T(8,128)(2,1)S(1)} %collective-permute-done.6.density_ref.refs_3_), custom_call_target="tpu_custom_call" | custom-call | flops 100000000 | tf_op jit(solution)/shard_map/pallas_call | solution.py:407
  31.2 0.4 collective-permute-done.12.refs_11_
  31.7 3.1 %shard_map.75.chi_ref = bf16[4,128,256]{2,1,0:T(8,128)(2,1)S(1)} custom-call(f32[4,4]{1,0:T(4,128)S(1)} %copy-done.2, s32[2,16]{1,0:T(2,128)S(1)} %bitcast.8, bf16[2,2,64,4096]{3,2,1,0:T(8,128)(2,1)S(1)} %get-tuple-element.23.refs_0_, bf16[2,2,64,4096]{3,2,1,0:T(8,128)(2,1)S(1)} %get-tuple-element.24.refs_1_, ...), custom_call_target="tpu_custom_call" | custom-call | flops 3000000000 | tf_op jit(solution)/shard_map/pallas_call | solution.py:414
  34.8 3.3 %collective-permute-start.13 = (bf16[128,256]{1,0:T(8,128)(2,1)S(1)}, bf16[128,256]{1,0:T(8,128)(2,1)S(1)}, u32[]{:S(2)}, u32[]{:S(2)}) collective-permute-start(bf16[128,256]{1,0:T(8,128)(2,1)S(1)} %get-tuple-element.35), channel_id=1, source_target_pairs={{0,24},{8,16},{16,8},{24,0},{1,25},{9,17},{17,9},{25,1},{2,26},{10... | collective-permute-start | bytes 196616 | tf_op jit(solution)/shard_map/ppermute | solution.py:361
  38.1 1.2 %collective-permute-start.15 = (bf16[128,256]{1,0:T(8,128)(2,1)S(1)}, bf16[128,256]{1,0:T(8,128)(2,1)S(1)}, u32[]{:S(2)}, u32[]{:S(2)}) collective-permute-start(bf16[128,256]{1,0:T(8,128)(2,1)S(1)} %get-tuple-element.33), channel_id=1, source_target_pairs={{0,8},{8,0},{16,24},{24,16},{1,9},{9,1},{17,25},{25,17},{2,10},{10... | collective-permute-start | bytes 196616 | tf_op jit(solution)/shard_map/ppermute | solution.py:361
  39.3 2.3 %collective-permute-done.13.r3 = bf16[128,256]{1,0:T(8,128)(2,1)S(1)} collective-permute-done((bf16[128,256]{1,0:T(8,128)(2,1)S(1)}, bf16[128,256]{1,0:T(8,128)(2,1)S(1)}, u32[]{:S(2)}, u32[]{:S(2)}) %collective-permute-start.13) | collective-permute-done | bytes 65568 | tf_op jit(solution)/shard_map/ppermute | solution.py:361
  41.6 2.4 %collective-permute-done.14.r2 = bf16[128,256]{1,0:T(8,128)(2,1)S(1)} collective-permute-done((bf16[128,256]{1,0:T(8,128)(2,1)S(1)}, bf16[128,256]{1,0:T(8,128)(2,1)S(1)}, u32[]{:S(2)}, u32[]{:S(2)}) %collective-permute-start.14) | collective-permute-done | bytes 65568 | tf_op jit(solution)/shard_map/ppermute | solution.py:361
  44.0 1.2 %shard_map.76 = f32[1,128,1024]{2,1,0:T(8,128)} custom-call(bf16[4,128,256]{2,1,0:T(8,128)(2,1)S(1)} %shard_map.75.chi_ref, bf16[128,256]{1,0:T(8,128)(2,1)S(1)} %collective-permute-done.13.r3, bf16[128,256]{1,0:T(8,128)(2,1)S(1)} %collective-permute-done.14.r2, bf16[128,256]{1,0:T(8,128)(2,1)S(1)} %collective-permute-done.15.r1, ...), custom_call_target="tpu_custom_call" | custom-call | flops 1000000000 | tf_op jit(solution)/shard_map/pallas_call | solution.py:422
  (28 shorter events, 0.1 us)
Async XLA Ops:
  2.0 11.5 %collective-permute-start = (bf16[16,8704]{1,0:T(8,128)(2,1)}, bf16[16,8704]{1,0:T(8,128)(2,1)S(1)}, u32[]{:S(2)}, u32[]{:S(2)}) collective-permute-start(bf16[16,8704]{1,0:T(8,128)(2,1)} %get-tuple-element.20.low_ref), channel_id=1, source_target_pairs={{0,2},{1,3},{2,0},{3,1},{4,6},{5,7},{6,4},{7,5},{8,10},{9,11},{10,... | collective-permute-start | bytes 835592 | tf_op jit(solution)/shard_map/ppermute | solution.py:358
  5.0 8.7 %collective-permute-start.1 = (bf16[16,8704]{1,0:T(8,128)(2,1)}, bf16[16,8704]{1,0:T(8,128)(2,1)S(1)}, u32[]{:S(2)}, u32[]{:S(2)}) collective-permute-start(bf16[16,8704]{1,0:T(8,128)(2,1)} %get-tuple-element.21.high_ref), channel_id=1, source_target_pairs={{0,4},{1,5},{2,6},{3,7},{4,0},{5,1},{6,2},{7,3},{8,12},{9,13},{10,... | collective-permute-start | bytes 835592 | tf_op jit(solution)/shard_map/ppermute | solution.py:358
  6.6 7.0 %collective-permute-start.2 = (bf16[64,128]{1,0:T(8,128)(2,1)}, bf16[64,128]{1,0:T(8,128)(2,1)S(1)}, u32[]{:S(2)}, u32[]{:S(2)}) collective-permute-start(bf16[64,128]{1,0:T(8,128)(2,1)} %get-tuple-element.19.density_ref), channel_id=1, source_target_pairs={{0,6},{1,7},{2,4},{3,5},{4,2},{5,3},{6,0},{7,1},{8,14},{9,15},{10,... | collective-permute-start | bytes 49160 | tf_op jit(solution)/shard_map/ppermute | solution.py:358
  6.6 1.6 %copy-start.4 = (bf16[128,2,4096]{2,1,0:T(2,128)(2,1)S(1)}, bf16[128,2,4096]{2,1,0:T(2,128)(2,1)}, u32[]{:S(2)}) copy-start(bf16[128,2,4096]{2,1,0:T(2,128)(2,1)} %rows_ref.3) | copy-start | bytes 6291460
  8.2 1.5 %copy-start.5 = (f32[16,64,64]{2,1,0:T(8,128)S(1)}, f32[16,64,64]{2,1,0:T(8,128)}, u32[]{:S(2)}) copy-start(f32[16,64,64]{2,1,0:T(8,128)} %factor_ref.1) | copy-start | bytes 786436
  9.7 4.1 %copy-start.6 = (bf16[64,128]{1,0:T(8,128)(2,1)S(1)}, bf16[64,128]{1,0:T(8,128)(2,1)}, u32[]{:S(2)}) copy-start(bf16[64,128]{1,0:T(8,128)(2,1)} %get-tuple-element.19.density_ref) | copy-start | bytes 49156
  9.7 4.1 %copy-start = (bf16[16,8704]{1,0:T(8,128)(2,1)S(1)}, bf16[16,8704]{1,0:T(8,128)(2,1)}, u32[]{:S(2)}) copy-start(bf16[16,8704]{1,0:T(8,128)(2,1)} %get-tuple-element.20.low_ref) | copy-start | bytes 835588
  9.7 4.1 %copy-start.1 = (bf16[16,8704]{1,0:T(8,128)(2,1)S(1)}, bf16[16,8704]{1,0:T(8,128)(2,1)}, u32[]{:S(2)}) copy-start(bf16[16,8704]{1,0:T(8,128)(2,1)} %get-tuple-element.21.high_ref) | copy-start | bytes 835588
  13.8 3.5 %copy-start.3 = (s32[16,2]{0,1:T(2,128)S(1)}, s32[16,2]{0,1:T(2,128)}, u32[]{:S(2)}) copy-start(s32[16,2]{0,1:T(2,128)} %param.7) | copy-start | bytes 388
  13.8 14.9 %collective-permute-start.7 = (bf16[2,2,16,4096]{3,2,1,0:T(8,128)(2,1)S(1)}, bf16[2,2,16,4096]{3,2,1,0:T(8,128)(2,1)S(1)}, u32[]{:S(2)}, u32[]{:S(2)}) collective-permute-start(bf16[2,2,16,4096]{3,2,1,0:T(8,128)(2,1)S(1)} %get-tuple-element.22.after_ref.refs_4_), channel_id=1, source_target_pairs={{0,2},{1,3},{2,0},{3,1},{4,6},{5,7},{6,4},{7,5},{8,10},{9,11},{10,... | collective-permute-start | bytes 1572872 | tf_op jit(solution)/shard_map/ppermute | solution.py:358
  15.2 13.6 %collective-permute-start.8 = (bf16[2,2,16,4096]{3,2,1,0:T(8,128)(2,1)S(1)}, bf16[2,2,16,4096]{3,2,1,0:T(8,128)(2,1)S(1)}, u32[]{:S(2)}, u32[]{:S(2)}) collective-permute-start(bf16[2,2,16,4096]{3,2,1,0:T(8,128)(2,1)S(1)} %get-tuple-element.27.refs_5_), channel_id=1, source_target_pairs={{0,4},{1,5},{2,6},{3,7},{4,0},{5,1},{6,2},{7,3},{8,12},{9,13},{10,... | collective-permute-start | bytes 1572872 | tf_op jit(solution)/shard_map/ppermute | solution.py:358
  16.0 1.3 %collective-permute-start.3 = (bf16[4,64,128]{2,1,0:T(8,128)(2,1)S(1)}, bf16[4,64,128]{2,1,0:T(8,128)(2,1)S(1)}, u32[]{:S(2)}, u32[]{:S(2)}) collective-permute-start(bf16[4,64,128]{2,1,0:T(8,128)(2,1)S(1)} %shard_map.66.refs_1_.near_ref), channel_id=1, source_target_pairs={{0,1},{1,0},{2,3},{3,2},{4,5},{5,4},{6,7},{7,6},{8,9},{9,8},{10,11... | collective-permute-start | bytes 196616 | tf_op jit(solution)/shard_map/ppermute | solution.py:358
  17.8 6.2 %collective-permute-start.4 = (bf16[2,2,64,128]{3,2,1,0:T(8,128)(2,1)S(1)}, bf16[2,2,64,128]{3,2,1,0:T(8,128)(2,1)S(1)}, u32[]{:S(2)}, u32[]{:S(2)}) collective-permute-start(bf16[2,2,64,128]{3,2,1,0:T(8,128)(2,1)S(1)} %shard_map.69.density_ref), channel_id=1, source_target_pairs={{0,8},{8,0},{16,24},{24,16},{1,9},{9,1},{17,25},{25,17},{2,10},{10... | collective-permute-start | bytes 196616 | tf_op jit(solution)/shard_map/ppermute | solution.py:361
  19.4 7.5 %collective-permute-start.5 = (bf16[2,2,64,128]{3,2,1,0:T(8,128)(2,1)S(1)}, bf16[2,2,64,128]{3,2,1,0:T(8,128)(2,1)S(1)}, u32[]{:S(2)}, u32[]{:S(2)}) collective-permute-start(bf16[2,2,64,128]{3,2,1,0:T(8,128)(2,1)S(1)} %shard_map.69.density_ref), channel_id=1, source_target_pairs={{0,16},{8,24},{16,0},{24,8},{1,17},{9,25},{17,1},{25,9},{2,18},{10... | collective-permute-start | bytes 196616 | tf_op jit(solution)/shard_map/ppermute | solution.py:361
  22.0 6.7 %collective-permute-start.6 = (bf16[2,2,64,128]{3,2,1,0:T(8,128)(2,1)S(1)}, bf16[2,2,64,128]{3,2,1,0:T(8,128)(2,1)S(1)}, u32[]{:S(2)}, u32[]{:S(2)}) collective-permute-start(bf16[2,2,64,128]{3,2,1,0:T(8,128)(2,1)S(1)} %shard_map.69.density_ref), channel_id=1, source_target_pairs={{0,24},{8,16},{16,8},{24,0},{1,25},{9,17},{17,9},{25,1},{2,26},{10... | collective-permute-start | bytes 196616 | tf_op jit(solution)/shard_map/ppermute | solution.py:361
  24.0 7.2 %collective-permute-start.9 = (bf16[2,2,16,4096]{3,2,1,0:T(8,128)(2,1)S(1)}, bf16[2,2,16,4096]{3,2,1,0:T(8,128)(2,1)S(1)}, u32[]{:S(2)}, u32[]{:S(2)}) collective-permute-start(bf16[2,2,16,4096]{3,2,1,0:T(8,128)(2,1)S(1)} %get-tuple-element.22.after_ref.refs_4_), channel_id=1, source_target_pairs={{0,1},{1,0},{2,3},{3,2},{4,5},{5,4},{6,7},{7,6},{8,9},{9,8},{10,11... | collective-permute-start | bytes 1572872 | tf_op jit(solution)/shard_map/ppermute | solution.py:358
  26.9 4.3 %collective-permute-start.10 = (bf16[2,2,16,4096]{3,2,1,0:T(8,128)(2,1)S(1)}, bf16[2,2,16,4096]{3,2,1,0:T(8,128)(2,1)S(1)}, u32[]{:S(2)}, u32[]{:S(2)}) collective-permute-start(bf16[2,2,16,4096]{3,2,1,0:T(8,128)(2,1)S(1)} %get-tuple-element.27.refs_5_), channel_id=1, source_target_pairs={{0,1},{1,0},{2,3},{3,2},{4,5},{5,4},{6,7},{7,6},{8,9},{9,8},{10,11... | collective-permute-start | bytes 1572872 | tf_op jit(solution)/shard_map/ppermute | solution.py:358
  28.7 3.0 %copy-start.2 = (f32[4,4]{1,0:T(4,128)S(1)}, f32[4,4]{1,0:T(4,128)}, u32[]{:S(2)}) copy-start(f32[4,4]{1,0:T(4,128)} %weights_ref.1) | copy-start | bytes 196
  28.8 2.4 %collective-permute-start.11 = (bf16[2,2,16,4096]{3,2,1,0:T(8,128)(2,1)S(1)}, bf16[2,2,16,4096]{3,2,1,0:T(8,128)(2,1)S(1)}, u32[]{:S(2)}, u32[]{:S(2)}) collective-permute-start(bf16[2,2,16,4096]{3,2,1,0:T(8,128)(2,1)S(1)} %get-tuple-element.31.refs_6_), channel_id=1, source_target_pairs={{0,1},{1,0},{2,3},{3,2},{4,5},{5,4},{6,7},{7,6},{8,9},{9,8},{10,11... | collective-permute-start | bytes 1572872 | tf_op jit(solution)/shard_map/ppermute | solution.py:358
  29.4 2.3 %collective-permute-start.12 = (bf16[2,2,16,4096]{3,2,1,0:T(8,128)(2,1)S(1)}, bf16[2,2,16,4096]{3,2,1,0:T(8,128)(2,1)S(1)}, u32[]{:S(2)}, u32[]{:S(2)}) collective-permute-start(bf16[2,2,16,4096]{3,2,1,0:T(8,128)(2,1)S(1)} %get-tuple-element.32.refs_7_), channel_id=1, source_target_pairs={{0,1},{1,0},{2,3},{3,2},{4,5},{5,4},{6,7},{7,6},{8,9},{9,8},{10,11... | collective-permute-start | bytes 1572872 | tf_op jit(solution)/shard_map/ppermute | solution.py:358
  34.8 6.8 %collective-permute-start.13 = (bf16[128,256]{1,0:T(8,128)(2,1)S(1)}, bf16[128,256]{1,0:T(8,128)(2,1)S(1)}, u32[]{:S(2)}, u32[]{:S(2)}) collective-permute-start(bf16[128,256]{1,0:T(8,128)(2,1)S(1)} %get-tuple-element.35), channel_id=1, source_target_pairs={{0,24},{8,16},{16,8},{24,0},{1,25},{9,17},{17,9},{25,1},{2,26},{10... | collective-permute-start | bytes 196616 | tf_op jit(solution)/shard_map/ppermute | solution.py:361
  38.1 5.9 %collective-permute-start.14 = (bf16[128,256]{1,0:T(8,128)(2,1)S(1)}, bf16[128,256]{1,0:T(8,128)(2,1)S(1)}, u32[]{:S(2)}, u32[]{:S(2)}) collective-permute-start(bf16[128,256]{1,0:T(8,128)(2,1)S(1)} %get-tuple-element.34), channel_id=1, source_target_pairs={{0,16},{8,24},{16,0},{24,8},{1,17},{9,25},{17,1},{25,9},{2,18},{10... | collective-permute-start | bytes 196616 | tf_op jit(solution)/shard_map/ppermute | solution.py:361
  38.1 5.9 %collective-permute-start.15 = (bf16[128,256]{1,0:T(8,128)(2,1)S(1)}, bf16[128,256]{1,0:T(8,128)(2,1)S(1)}, u32[]{:S(2)}, u32[]{:S(2)}) collective-permute-start(bf16[128,256]{1,0:T(8,128)(2,1)S(1)} %get-tuple-element.33), channel_id=1, source_target_pairs={{0,8},{8,0},{16,24},{24,16},{1,9},{9,1},{17,25},{25,17},{2,10},{10... | collective-permute-start | bytes 196616 | tf_op jit(solution)/shard_map/ppermute | solution.py:361

commit v6 on v5

--- a/solution.py
+++ b/solution.py
@@ -407,8 +407,8 @@
         *[kernel(mix_kernel, [tiles, mark], [vmem] * 2, 0.1)(turned, each) for each in per_time]
     )
 
-    from_x, from_y = kernel(order_kernel, [both] * 2, [vmem] * 6, 0.3)(
-        across(to_x, 2), across(to_y, 4), *marks[:3], per_time[3]
+    from_x, from_y = kernel(order_kernel, [both] * 2, [vmem] * 7, 0.3)(
+        across(to_x, 2), across(to_y, 4), per_time[3], per_time[2], *marks[:3]
     )
     pieces = [to_x, to_y, from_x, from_y]
     chi = kernel(

time: 45.4 us -> 45.5 us (level)
  no operation moved by 1% of the time
where the time goes in v6:
time: 45.5 us; the launch traced here: 45.2 us
  starting transfers between devices  16.3 us (36%)
  Pallas kernels  15.7 us (35%)
  waiting for transfers between devices  11.3 us (25%)
  local copies, waits for them, and re-layouts  1.64 us (4%)
    ppermute x6, starting transfers between devices, planes(): return lax.ppermute(array, 'tm', [(i, i ^ move) for i in range(4)])  8.92 us
    ppermute x10, starting transfers between devices, across(): return lax.ppermute(array, 'tensor', [(i, i ^ move) for i in range(8)])  7.38 us
    pallas_call x4, Pallas kernels, small_slice(): kernel(mix_kernel, [tiles, mark], [vmem] * 2, 0.1)(turned, each)  6.95 us
    ppermute x6, waiting for transfers between devices, planes(): return lax.ppermute(array, 'tm', [(i, i ^ move) for i in range(4)])  5.84 us
    ppermute x10, waiting for transfers between devices, across(): return lax.ppermute(array, 'tensor', [(i, i ^ move) for i in range(8)])  5.47 us
    pallas_call x1, Pallas kernels, small_slice(): kernel(gram_kernel, jax.ShapeDtypeStruct((4, local_count, columns), jnp.b...  3.08 us
    pallas_call x1, Pallas kernels, small_slice(): kernel(own_kernel, [message, message, block], [pl.BlockSpec(memory_space=...  2.02 us
    unnamed x14, local copies, waits for them, and re-layouts  1.62 us
  transfers between devices with their start and end apart: 16, of which 7 were waited for; matrix products, arithmetic and copies ran while one was open for 0% of the time, Pallas kernels for 21%

profile of v6, /device:TPU:0, one launch (start us, length us, event | category | flops | bytes accessed | tf_op | source)
XLA Modules:
  0.0 45.2 jit_solution(2148897209809446966)
XLA Ops:
  0.0 2.0 %shard_map.65 = (bf16[16,8704]{1,0:T(8,128)(2,1)}, bf16[16,8704]{1,0:T(8,128)(2,1)}, bf16[64,128]{1,0:T(8,128)(2,1)}) custom-call(bf16[128,2,4096]{2,1,0:T(2,128)(2,1)} %rows_ref.3, bf16[1,1,64,64]{3,2,1,0:T(8,128)(2,1)} %occupied_ref.1, bf16[1,1,64,64]{3,2,1,0:T(8,128)(2,1)} %virtual_ref.1), custom_call_target="tpu_custom_call" | custom-call | flops 2000000000 | tf_op jit(solution)/shard_map/pallas_call | solution.py:370
  2.0 3.0 %collective-permute-start = (bf16[16,8704]{1,0:T(8,128)(2,1)}, bf16[16,8704]{1,0:T(8,128)(2,1)S(1)}, u32[]{:S(2)}, u32[]{:S(2)}) collective-permute-start(bf16[16,8704]{1,0:T(8,128)(2,1)} %get-tuple-element.20.low_ref), channel_id=1, source_target_pairs={{0,2},{1,3},{2,0},{3,1},{4,6},{5,7},{6,4},{7,5},{8,10},{9,11},{10,... | collective-permute-start | bytes 835592 | tf_op jit(solution)/shard_map/ppermute | solution.py:358
  5.0 1.5 %collective-permute-start.1 = (bf16[16,8704]{1,0:T(8,128)(2,1)}, bf16[16,8704]{1,0:T(8,128)(2,1)S(1)}, u32[]{:S(2)}, u32[]{:S(2)}) collective-permute-start(bf16[16,8704]{1,0:T(8,128)(2,1)} %get-tuple-element.21.high_ref), channel_id=1, source_target_pairs={{0,4},{1,5},{2,6},{3,7},{4,0},{5,1},{6,2},{7,3},{8,12},{9,13},{10,... | collective-permute-start | bytes 835592 | tf_op jit(solution)/shard_map/ppermute | solution.py:358
  6.6 1.6 %copy-done.4 = bf16[128,2,4096]{2,1,0:T(2,128)(2,1)S(1)} copy-done((bf16[128,2,4096]{2,1,0:T(2,128)(2,1)S(1)}, bf16[128,2,4096]{2,1,0:T(2,128)(2,1)}, u32[]{:S(2)}) %copy-start.4) | copy-done | bytes 2097176
  8.2 1.5 %shard_map.64.refs_0_.turned_ref = bf16[2,2,64,4096]{3,2,1,0:T(8,128)(2,1)S(1)} custom-call(bf16[128,2,4096]{2,1,0:T(2,128)(2,1)S(1)} %copy-done.4), custom_call_target="tpu_custom_call" | custom-call | flops 1200000000 | tf_op jit(solution)/shard_map/pallas_call | solution.py:384
  9.7 0.2 shard_map.67.refs_2_.factor_ref
  9.9 3.6 %collective-permute-done.2.d_ref = bf16[64,128]{1,0:T(8,128)(2,1)S(1)} collective-permute-done((bf16[64,128]{1,0:T(8,128)(2,1)}, bf16[64,128]{1,0:T(8,128)(2,1)S(1)}, u32[]{:S(2)}, u32[]{:S(2)}) %collective-permute-start.2) | collective-permute-done | bytes 16416 | tf_op jit(solution)/shard_map/ppermute | solution.py:358
  13.6 0.1 collective-permute-done.1.y_ref
  13.8 0.1 shard_map.68
  13.8 1.3 %collective-permute-start.7 = (bf16[2,2,16,4096]{3,2,1,0:T(8,128)(2,1)S(1)}, bf16[2,2,16,4096]{3,2,1,0:T(8,128)(2,1)S(1)}, u32[]{:S(2)}, u32[]{:S(2)}) collective-permute-start(bf16[2,2,16,4096]{3,2,1,0:T(8,128)(2,1)S(1)} %get-tuple-element.22.after_ref.refs_4_), channel_id=1, source_target_pairs={{0,2},{1,3},{2,0},{3,1},{4,6},{5,7},{6,4},{7,5},{8,10},{9,11},{10,... | collective-permute-start | bytes 1572872 | tf_op jit(solution)/shard_map/ppermute | solution.py:358
  15.2 0.8 %collective-permute-start.8 = (bf16[2,2,16,4096]{3,2,1,0:T(8,128)(2,1)S(1)}, bf16[2,2,16,4096]{3,2,1,0:T(8,128)(2,1)S(1)}, u32[]{:S(2)}, u32[]{:S(2)}) collective-permute-start(bf16[2,2,16,4096]{3,2,1,0:T(8,128)(2,1)S(1)} %get-tuple-element.27.refs_5_), channel_id=1, source_target_pairs={{0,4},{1,5},{2,6},{3,7},{4,0},{5,1},{6,2},{7,3},{8,12},{9,13},{10,... | collective-permute-start | bytes 1572872 | tf_op jit(solution)/shard_map/ppermute | solution.py:358
  16.0 1.3 %collective-permute-done.3.core_ref = bf16[4,64,128]{2,1,0:T(8,128)(2,1)S(1)} collective-permute-done((bf16[4,64,128]{2,1,0:T(8,128)(2,1)S(1)}, bf16[4,64,128]{2,1,0:T(8,128)(2,1)S(1)}, u32[]{:S(2)}, u32[]{:S(2)}) %collective-permute-start.3) | collective-permute-done | bytes 65568 | tf_op jit(solution)/shard_map/ppermute | solution.py:358
  17.2 0.6 %shard_map.69.density_ref = bf16[2,2,64,128]{3,2,1,0:T(8,128)(2,1)S(1)} custom-call(s32[2,16]{1,0:T(2,128)S(1)} %bitcast.7, bf16[4,64,128]{2,1,0:T(8,128)(2,1)S(1)} %shard_map.66.refs_1_.near_ref, bf16[4,64,128]{2,1,0:T(8,128)(2,1)S(1)} %collective-permute-done.3.core_ref, bf16[2,2,16,4096]{3,2,1,0:T(8,128)(2,1)S(1)} %get-tuple-element.22.after_ref.refs_4_), custom_call_target="tpu_custom_call" | custom-call | flops 1000000000 | tf_op jit(solution)/shard_map/pallas_call | solution.py:396
  17.8 1.6 %collective-permute-start.4 = (bf16[2,2,64,128]{3,2,1,0:T(8,128)(2,1)S(1)}, bf16[2,2,64,128]{3,2,1,0:T(8,128)(2,1)S(1)}, u32[]{:S(2)}, u32[]{:S(2)}) collective-permute-start(bf16[2,2,64,128]{3,2,1,0:T(8,128)(2,1)S(1)} %shard_map.69.density_ref), channel_id=1, source_target_pairs={{0,8},{8,0},{16,24},{24,16},{1,9},{9,1},{17,25},{25,17},{2,10},{10... | collective-permute-start | bytes 196616 | tf_op jit(solution)/shard_map/ppermute | solution.py:361
  19.4 2.6 %collective-permute-start.5 = (bf16[2,2,64,128]{3,2,1,0:T(8,128)(2,1)S(1)}, bf16[2,2,64,128]{3,2,1,0:T(8,128)(2,1)S(1)}, u32[]{:S(2)}, u32[]{:S(2)}) collective-permute-start(bf16[2,2,64,128]{3,2,1,0:T(8,128)(2,1)S(1)} %shard_map.69.density_ref), channel_id=1, source_target_pairs={{0,16},{8,24},{16,0},{24,8},{1,17},{9,25},{17,1},{25,9},{2,18},{10... | collective-permute-start | bytes 196616 | tf_op jit(solution)/shard_map/ppermute | solution.py:361
  22.0 0.3 collective-permute-start.6
  22.3 1.7 %shard_map.70 = (bf16[2,2,64,4096]{3,2,1,0:T(8,128)(2,1)S(1)}, f32[8,128]{1,0:T(8,128)S(1)}) custom-call(bf16[2,2,64,4096]{3,2,1,0:T(8,128)(2,1)S(1)} %shard_map.64.refs_0_.turned_ref, bf16[2,2,64,128]{3,2,1,0:T(8,128)(2,1)S(1)} %shard_map.69.density_ref), custom_call_target="tpu_custom_call" | custom-call | flops 100000000 | tf_op jit(solution)/shard_map/pallas_call | solution.py:407
  24.0 0.1 collective-permute-start.9
  24.1 1.7 %shard_map.71 = (bf16[2,2,64,4096]{3,2,1,0:T(8,128)(2,1)S(1)}, f32[8,128]{1,0:T(8,128)S(1)}) custom-call(bf16[2,2,64,4096]{3,2,1,0:T(8,128)(2,1)S(1)} %shard_map.64.refs_0_.turned_ref, bf16[2,2,64,128]{3,2,1,0:T(8,128)(2,1)S(1)} %collective-permute-done.4.density_ref), custom_call_target="tpu_custom_call" | custom-call | flops 100000000 | tf_op jit(solution)/shard_map/pallas_call | solution.py:407
  25.8 1.1 %collective-permute-done.5.density_ref.refs_1_ = bf16[2,2,64,128]{3,2,1,0:T(8,128)(2,1)S(1)} collective-permute-done((bf16[2,2,64,128]{3,2,1,0:T(8,128)(2,1)S(1)}, bf16[2,2,64,128]{3,2,1,0:T(8,128)(2,1)S(1)}, u32[]{:S(2)}, u32[]{:S(2)}) %collective-permute-start.5) | collective-permute-done | bytes 65568 | tf_op jit(solution)/shard_map/ppermute | solution.py:361
  26.9 1.7 %shard_map.72 = (bf16[2,2,64,4096]{3,2,1,0:T(8,128)(2,1)S(1)}, f32[8,128]{1,0:T(8,128)S(1)}) custom-call(bf16[2,2,64,4096]{3,2,1,0:T(8,128)(2,1)S(1)} %shard_map.64.refs_0_.turned_ref, bf16[2,2,64,128]{3,2,1,0:T(8,128)(2,1)S(1)} %collective-permute-done.5.density_ref.refs_1_), custom_call_target="tpu_custom_call" | custom-call | flops 100000000 | tf_op jit(solution)/shard_map/pallas_call | solution.py:407
  28.7 0.1 shard_map.74
  28.8 0.6 %collective-permute-start.11 = (bf16[2,2,16,4096]{3,2,1,0:T(8,128)(2,1)S(1)}, bf16[2,2,16,4096]{3,2,1,0:T(8,128)(2,1)S(1)}, u32[]{:S(2)}, u32[]{:S(2)}) collective-permute-start(bf16[2,2,16,4096]{3,2,1,0:T(8,128)(2,1)S(1)} %get-tuple-element.31.refs_6_), channel_id=1, source_target_pairs={{0,1},{1,0},{2,3},{3,2},{4,5},{5,4},{6,7},{7,6},{8,9},{9,8},{10,11... | collective-permute-start | bytes 1572872 | tf_op jit(solution)/shard_map/ppermute | solution.py:358
  29.4 0.1 collective-permute-start.12
  29.5 1.7 %shard_map.73 = (bf16[2,2,64,4096]{3,2,1,0:T(8,128)(2,1)S(1)}, f32[8,128]{1,0:T(8,128)}) custom-call(bf16[2,2,64,4096]{3,2,1,0:T(8,128)(2,1)S(1)} %shard_map.64.refs_0_.turned_ref, bf16[2,2,64,128]{3,2,1,0:T(8,128)(2,1)S(1)} %collective-permute-done.6.density_ref.refs_0_), custom_call_target="tpu_custom_call" | custom-call | flops 100000000 | tf_op jit(solution)/shard_map/pallas_call | solution.py:407
  31.2 0.4 collective-permute-done.12.refs_11_
  31.7 3.1 %shard_map.75.chi_ref = bf16[4,128,256]{2,1,0:T(8,128)(2,1)S(1)} custom-call(f32[4,4]{1,0:T(4,128)S(1)} %copy-done.2, s32[2,16]{1,0:T(2,128)S(1)} %bitcast.8, bf16[2,2,64,4096]{3,2,1,0:T(8,128)(2,1)S(1)} %get-tuple-element.23.refs_0_, bf16[2,2,64,4096]{3,2,1,0:T(8,128)(2,1)S(1)} %get-tuple-element.24.refs_1_, ...), custom_call_target="tpu_custom_call" | custom-call | flops 3000000000 | tf_op jit(solution)/shard_map/pallas_call | solution.py:414
  34.8 3.3 %collective-permute-start.13 = (bf16[128,256]{1,0:T(8,128)(2,1)S(1)}, bf16[128,256]{1,0:T(8,128)(2,1)S(1)}, u32[]{:S(2)}, u32[]{:S(2)}) collective-permute-start(bf16[128,256]{1,0:T(8,128)(2,1)S(1)} %get-tuple-element.35), channel_id=1, source_target_pairs={{0,24},{8,16},{16,8},{24,0},{1,25},{9,17},{17,9},{25,1},{2,26},{10... | collective-permute-start | bytes 196616 | tf_op jit(solution)/shard_map/ppermute | solution.py:361
  38.1 1.2 %collective-permute-start.15 = (bf16[128,256]{1,0:T(8,128)(2,1)S(1)}, bf16[128,256]{1,0:T(8,128)(2,1)S(1)}, u32[]{:S(2)}, u32[]{:S(2)}) collective-permute-start(bf16[128,256]{1,0:T(8,128)(2,1)S(1)} %get-tuple-element.33), channel_id=1, source_target_pairs={{0,8},{8,0},{16,24},{24,16},{1,9},{9,1},{17,25},{25,17},{2,10},{10... | collective-permute-start | bytes 196616 | tf_op jit(solution)/shard_map/ppermute | solution.py:361
  39.3 2.3 %collective-permute-done.13.r3 = bf16[128,256]{1,0:T(8,128)(2,1)S(1)} collective-permute-done((bf16[128,256]{1,0:T(8,128)(2,1)S(1)}, bf16[128,256]{1,0:T(8,128)(2,1)S(1)}, u32[]{:S(2)}, u32[]{:S(2)}) %collective-permute-start.13) | collective-permute-done | bytes 65568 | tf_op jit(solution)/shard_map/ppermute | solution.py:361
  41.6 2.4 %collective-permute-done.14.r2 = bf16[128,256]{1,0:T(8,128)(2,1)S(1)} collective-permute-done((bf16[128,256]{1,0:T(8,128)(2,1)S(1)}, bf16[128,256]{1,0:T(8,128)(2,1)S(1)}, u32[]{:S(2)}, u32[]{:S(2)}) %collective-permute-start.14) | collective-permute-done | bytes 65568 | tf_op jit(solution)/shard_map/ppermute | solution.py:361
  44.0 1.2 %shard_map.76 = f32[1,128,1024]{2,1,0:T(8,128)} custom-call(bf16[4,128,256]{2,1,0:T(8,128)(2,1)S(1)} %shard_map.75.chi_ref, bf16[128,256]{1,0:T(8,128)(2,1)S(1)} %collective-permute-done.13.r3, bf16[128,256]{1,0:T(8,128)(2,1)S(1)} %collective-permute-done.14.r2, bf16[128,256]{1,0:T(8,128)(2,1)S(1)} %collective-permute-done.15.r1, ...), custom_call_target="tpu_custom_call" | custom-call | flops 1000000000 | tf_op jit(solution)/shard_map/pallas_call | solution.py:422
  (28 shorter events, 0.1 us)
Async XLA Ops:
  2.0 11.5 %collective-permute-start = (bf16[16,8704]{1,0:T(8,128)(2,1)}, bf16[16,8704]{1,0:T(8,128)(2,1)S(1)}, u32[]{:S(2)}, u32[]{:S(2)}) collective-permute-start(bf16[16,8704]{1,0:T(8,128)(2,1)} %get-tuple-element.20.low_ref), channel_id=1, source_target_pairs={{0,2},{1,3},{2,0},{3,1},{4,6},{5,7},{6,4},{7,5},{8,10},{9,11},{10,... | collective-permute-start | bytes 835592 | tf_op jit(solution)/shard_map/ppermute | solution.py:358
  5.0 8.7 %collective-permute-start.1 = (bf16[16,8704]{1,0:T(8,128)(2,1)}, bf16[16,8704]{1,0:T(8,128)(2,1)S(1)}, u32[]{:S(2)}, u32[]{:S(2)}) collective-permute-start(bf16[16,8704]{1,0:T(8,128)(2,1)} %get-tuple-element.21.high_ref), channel_id=1, source_target_pairs={{0,4},{1,5},{2,6},{3,7},{4,0},{5,1},{6,2},{7,3},{8,12},{9,13},{10,... | collective-permute-start | bytes 835592 | tf_op jit(solution)/shard_map/ppermute | solution.py:358
  6.6 7.0 %collective-permute-start.2 = (bf16[64,128]{1,0:T(8,128)(2,1)}, bf16[64,128]{1,0:T(8,128)(2,1)S(1)}, u32[]{:S(2)}, u32[]{:S(2)}) collective-permute-start(bf16[64,128]{1,0:T(8,128)(2,1)} %get-tuple-element.19.density_ref), channel_id=1, source_target_pairs={{0,6},{1,7},{2,4},{3,5},{4,2},{5,3},{6,0},{7,1},{8,14},{9,15},{10,... | collective-permute-start | bytes 49160 | tf_op jit(solution)/shard_map/ppermute | solution.py:358
  6.6 1.6 %copy-start.4 = (bf16[128,2,4096]{2,1,0:T(2,128)(2,1)S(1)}, bf16[128,2,4096]{2,1,0:T(2,128)(2,1)}, u32[]{:S(2)}) copy-start(bf16[128,2,4096]{2,1,0:T(2,128)(2,1)} %rows_ref.3) | copy-start | bytes 6291460
  8.2 1.5 %copy-start.5 = (f32[16,64,64]{2,1,0:T(8,128)S(1)}, f32[16,64,64]{2,1,0:T(8,128)}, u32[]{:S(2)}) copy-start(f32[16,64,64]{2,1,0:T(8,128)} %factor_ref.1) | copy-start | bytes 786436
  9.7 4.1 %copy-start.6 = (bf16[64,128]{1,0:T(8,128)(2,1)S(1)}, bf16[64,128]{1,0:T(8,128)(2,1)}, u32[]{:S(2)}) copy-start(bf16[64,128]{1,0:T(8,128)(2,1)} %get-tuple-element.19.density_ref) | copy-start | bytes 49156
  9.7 4.1 %copy-start = (bf16[16,8704]{1,0:T(8,128)(2,1)S(1)}, bf16[16,8704]{1,0:T(8,128)(2,1)}, u32[]{:S(2)}) copy-start(bf16[16,8704]{1,0:T(8,128)(2,1)} %get-tuple-element.20.low_ref) | copy-start | bytes 835588
  9.7 4.1 %copy-start.1 = (bf16[16,8704]{1,0:T(8,128)(2,1)S(1)}, bf16[16,8704]{1,0:T(8,128)(2,1)}, u32[]{:S(2)}) copy-start(bf16[16,8704]{1,0:T(8,128)(2,1)} %get-tuple-element.21.high_ref) | copy-start | bytes 835588
  13.8 3.5 %copy-start.3 = (s32[16,2]{0,1:T(2,128)S(1)}, s32[16,2]{0,1:T(2,128)}, u32[]{:S(2)}) copy-start(s32[16,2]{0,1:T(2,128)} %param.7) | copy-start | bytes 388
  13.8 14.9 %collective-permute-start.7 = (bf16[2,2,16,4096]{3,2,1,0:T(8,128)(2,1)S(1)}, bf16[2,2,16,4096]{3,2,1,0:T(8,128)(2,1)S(1)}, u32[]{:S(2)}, u32[]{:S(2)}) collective-permute-start(bf16[2,2,16,4096]{3,2,1,0:T(8,128)(2,1)S(1)} %get-tuple-element.22.after_ref.refs_4_), channel_id=1, source_target_pairs={{0,2},{1,3},{2,0},{3,1},{4,6},{5,7},{6,4},{7,5},{8,10},{9,11},{10,... | collective-permute-start | bytes 1572872 | tf_op jit(solution)/shard_map/ppermute | solution.py:358
  15.2 13.6 %collective-permute-start.8 = (bf16[2,2,16,4096]{3,2,1,0:T(8,128)(2,1)S(1)}, bf16[2,2,16,4096]{3,2,1,0:T(8,128)(2,1)S(1)}, u32[]{:S(2)}, u32[]{:S(2)}) collective-permute-start(bf16[2,2,16,4096]{3,2,1,0:T(8,128)(2,1)S(1)} %get-tuple-element.27.refs_5_), channel_id=1, source_target_pairs={{0,4},{1,5},{2,6},{3,7},{4,0},{5,1},{6,2},{7,3},{8,12},{9,13},{10,... | collective-permute-start | bytes 1572872 | tf_op jit(solution)/shard_map/ppermute | solution.py:358
  16.0 1.3 %collective-permute-start.3 = (bf16[4,64,128]{2,1,0:T(8,128)(2,1)S(1)}, bf16[4,64,128]{2,1,0:T(8,128)(2,1)S(1)}, u32[]{:S(2)}, u32[]{:S(2)}) collective-permute-start(bf16[4,64,128]{2,1,0:T(8,128)(2,1)S(1)} %shard_map.66.refs_1_.near_ref), channel_id=1, source_target_pairs={{0,1},{1,0},{2,3},{3,2},{4,5},{5,4},{6,7},{7,6},{8,9},{9,8},{10,11... | collective-permute-start | bytes 196616 | tf_op jit(solution)/shard_map/ppermute | solution.py:358
  17.8 6.2 %collective-permute-start.4 = (bf16[2,2,64,128]{3,2,1,0:T(8,128)(2,1)S(1)}, bf16[2,2,64,128]{3,2,1,0:T(8,128)(2,1)S(1)}, u32[]{:S(2)}, u32[]{:S(2)}) collective-permute-start(bf16[2,2,64,128]{3,2,1,0:T(8,128)(2,1)S(1)} %shard_map.69.density_ref), channel_id=1, source_target_pairs={{0,8},{8,0},{16,24},{24,16},{1,9},{9,1},{17,25},{25,17},{2,10},{10... | collective-permute-start | bytes 196616 | tf_op jit(solution)/shard_map/ppermute | solution.py:361
  19.4 7.5 %collective-permute-start.5 = (bf16[2,2,64,128]{3,2,1,0:T(8,128)(2,1)S(1)}, bf16[2,2,64,128]{3,2,1,0:T(8,128)(2,1)S(1)}, u32[]{:S(2)}, u32[]{:S(2)}) collective-permute-start(bf16[2,2,64,128]{3,2,1,0:T(8,128)(2,1)S(1)} %shard_map.69.density_ref), channel_id=1, source_target_pairs={{0,16},{8,24},{16,0},{24,8},{1,17},{9,25},{17,1},{25,9},{2,18},{10... | collective-permute-start | bytes 196616 | tf_op jit(solution)/shard_map/ppermute | solution.py:361
  22.0 6.7 %collective-permute-start.6 = (bf16[2,2,64,128]{3,2,1,0:T(8,128)(2,1)S(1)}, bf16[2,2,64,128]{3,2,1,0:T(8,128)(2,1)S(1)}, u32[]{:S(2)}, u32[]{:S(2)}) collective-permute-start(bf16[2,2,64,128]{3,2,1,0:T(8,128)(2,1)S(1)} %shard_map.69.density_ref), channel_id=1, source_target_pairs={{0,24},{8,16},{16,8},{24,0},{1,25},{9,17},{17,9},{25,1},{2,26},{10... | collective-permute-start | bytes 196616 | tf_op jit(solution)/shard_map/ppermute | solution.py:361
  24.0 7.2 %collective-permute-start.9 = (bf16[2,2,16,4096]{3,2,1,0:T(8,128)(2,1)S(1)}, bf16[2,2,16,4096]{3,2,1,0:T(8,128)(2,1)S(1)}, u32[]{:S(2)}, u32[]{:S(2)}) collective-permute-start(bf16[2,2,16,4096]{3,2,1,0:T(8,128)(2,1)S(1)} %get-tuple-element.22.after_ref.refs_4_), channel_id=1, source_target_pairs={{0,1},{1,0},{2,3},{3,2},{4,5},{5,4},{6,7},{7,6},{8,9},{9,8},{10,11... | collective-permute-start | bytes 1572872 | tf_op jit(solution)/shard_map/ppermute | solution.py:358
  26.9 4.3 %collective-permute-start.10 = (bf16[2,2,16,4096]{3,2,1,0:T(8,128)(2,1)S(1)}, bf16[2,2,16,4096]{3,2,1,0:T(8,128)(2,1)S(1)}, u32[]{:S(2)}, u32[]{:S(2)}) collective-permute-start(bf16[2,2,16,4096]{3,2,1,0:T(8,128)(2,1)S(1)} %get-tuple-element.27.refs_5_), channel_id=1, source_target_pairs={{0,1},{1,0},{2,3},{3,2},{4,5},{5,4},{6,7},{7,6},{8,9},{9,8},{10,11... | collective-permute-start | bytes 1572872 | tf_op jit(solution)/shard_map/ppermute | solution.py:358
  28.7 3.0 %copy-start.2 = (f32[4,4]{1,0:T(4,128)S(1)}, f32[4,4]{1,0:T(4,128)}, u32[]{:S(2)}) copy-start(f32[4,4]{1,0:T(4,128)} %weights_ref.1) | copy-start | bytes 196
  28.8 2.4 %collective-permute-start.11 = (bf16[2,2,16,4096]{3,2,1,0:T(8,128)(2,1)S(1)}, bf16[2,2,16,4096]{3,2,1,0:T(8,128)(2,1)S(1)}, u32[]{:S(2)}, u32[]{:S(2)}) collective-permute-start(bf16[2,2,16,4096]{3,2,1,0:T(8,128)(2,1)S(1)} %get-tuple-element.31.refs_6_), channel_id=1, source_target_pairs={{0,1},{1,0},{2,3},{3,2},{4,5},{5,4},{6,7},{7,6},{8,9},{9,8},{10,11... | collective-permute-start | bytes 1572872 | tf_op jit(solution)/shard_map/ppermute | solution.py:358
  29.4 2.3 %collective-permute-start.12 = (bf16[2,2,16,4096]{3,2,1,0:T(8,128)(2,1)S(1)}, bf16[2,2,16,4096]{3,2,1,0:T(8,128)(2,1)S(1)}, u32[]{:S(2)}, u32[]{:S(2)}) collective-permute-start(bf16[2,2,16,4096]{3,2,1,0:T(8,128)(2,1)S(1)} %get-tuple-element.32.refs_7_), channel_id=1, source_target_pairs={{0,1},{1,0},{2,3},{3,2},{4,5},{5,4},{6,7},{7,6},{8,9},{9,8},{10,11... | collective-permute-start | bytes 1572872 | tf_op jit(solution)/shard_map/ppermute | solution.py:358
  34.8 6.8 %collective-permute-start.13 = (bf16[128,256]{1,0:T(8,128)(2,1)S(1)}, bf16[128,256]{1,0:T(8,128)(2,1)S(1)}, u32[]{:S(2)}, u32[]{:S(2)}) collective-permute-start(bf16[128,256]{1,0:T(8,128)(2,1)S(1)} %get-tuple-element.35), channel_id=1, source_target_pairs={{0,24},{8,16},{16,8},{24,0},{1,25},{9,17},{17,9},{25,1},{2,26},{10... | collective-permute-start | bytes 196616 | tf_op jit(solution)/shard_map/ppermute | solution.py:361
  38.1 5.9 %collective-permute-start.14 = (bf16[128,256]{1,0:T(8,128)(2,1)S(1)}, bf16[128,256]{1,0:T(8,128)(2,1)S(1)}, u32[]{:S(2)}, u32[]{:S(2)}) collective-permute-start(bf16[128,256]{1,0:T(8,128)(2,1)S(1)} %get-tuple-element.34), channel_id=1, source_target_pairs={{0,16},{8,24},{16,0},{24,8},{1,17},{9,25},{17,1},{25,9},{2,18},{10... | collective-permute-start | bytes 196616 | tf_op jit(solution)/shard_map/ppermute | solution.py:361
  38.1 5.9 %collective-permute-start.15 = (bf16[128,256]{1,0:T(8,128)(2,1)S(1)}, bf16[128,256]{1,0:T(8,128)(2,1)S(1)}, u32[]{:S(2)}, u32[]{:S(2)}) collective-permute-start(bf16[128,256]{1,0:T(8,128)(2,1)S(1)} %get-tuple-element.33), channel_id=1, source_target_pairs={{0,8},{8,0},{16,24},{24,16},{1,9},{9,1},{17,25},{25,17},{2,10},{10... | collective-permute-start | bytes 196616 | tf_op jit(solution)/shard_map/ppermute | solution.py:361
